TPU v7x, 32 devices: a whole 2x2x4 slice. The times are simulated.
32 devices in a mesh: rep: 4 (over z), fsdp: 8 (over y, x, core).
Axes of the slice: x: 2, y: 2, z: 4, core: 2. Of those that a mesh axis runs over, the one named last changes fastest.
Arguments:
- block_input: bfloat16 [65536, 768], P(('rep', 'fsdp')), may hold values from -6 to 6
- lengths: int32 [512, 4], P(('rep', 'fsdp')), may hold values from 8 to 40, as said below
- segments: int32 [65536], P(('rep', 'fsdp')), may hold values from 0 to 4, as said below
- gain_attn: bfloat16 [768], P('fsdp'), may hold values from 0.099609375 to 1.8984375
- w_qkv: bfloat16 [768, 2304], P('fsdp'), may hold values from -0.21875 to 0.21875
- w_attn_out: bfloat16 [768, 768], P('fsdp'), may hold values from -0.875 to 0.875
- gain_mlp: bfloat16 [768], P('fsdp'), may hold values from 0.099609375 to 1.8984375
- w_mlp_in: bfloat16 [768, 3072], P('fsdp'), may hold values from -0.21875 to 0.21875
- w_mlp_out: bfloat16 [3072, 768], P('fsdp'), may hold values from -0.15625 to 0.15625
- cotangent: bfloat16 [65536, 768], P(('rep', 'fsdp')), may hold values from -6 to 6
Outputs:
- block_output: bfloat16 [65536, 768], P(('rep', 'fsdp'))
- grad_input: bfloat16 [65536, 768], P(('rep', 'fsdp'))
- grad_gain_attn: float32 [768], P('fsdp')
- grad_qkv: float32 [768, 2304], P('fsdp')
- grad_attn_out: float32 [768, 768], P('fsdp')
- grad_gain_mlp: float32 [768], P('fsdp')
- grad_mlp_in: float32 [768, 3072], P('fsdp')
- grad_mlp_out: float32 [3072, 768], P('fsdp')
Inputs may be any that keep to these rules, and one draw needn't show every extreme that they name: `lengths`: each packed row holds 4 sentences in order; one has exactly 40 tokens and the next one (cyclically) exactly 8; the rest of the row after them is padding. `segments`: within a packed row, token p has the number of sentences that end at or before p, so padding has 4; consistent with lengths.
All inputs are finite; a program needn't handle non-finite values.
Results may differ from a plain program's by a relative error of at most 0.01.
Values may be sent and summed in bfloat16 or wider, within the bound.
A program may use at most 192 MiB of HBM per device.

v0:
```python
import math

import jax
import jax.numpy as jnp
from jax import lax
from jax.sharding import PartitionSpec as P

HEADS = 12
HEAD = 64


EPS = 1e-05
NEGATIVE = -1e30


def permitted(lengths, segments):
    row_count = lengths.shape[0]
    row_span = segments.shape[0] // row_count
    labels = segments.reshape(row_count, row_span)
    filled = jnp.sum(lengths, axis=1)
    place = jnp.arange(row_span, dtype=jnp.int32)
    real_key = place[None, :] < filled[:, None]
    same = labels[:, :, None] == labels[:, None, :]
    itself = place[:, None] == place[None, :]
    return same & (real_key[:, None, :] | itself[None])


def moments(values):
    middle = jnp.mean(values, axis=-1, keepdims=True)
    centred = values - middle
    spread = jnp.mean(centred * centred, axis=-1, keepdims=True)
    inverse = lax.rsqrt(spread + EPS)
    return (centred * inverse, inverse)


def norm_back(incoming, normed, inverse, gain):
    scaled = incoming * gain
    inner = (
        scaled
        - jnp.mean(scaled, axis=-1, keepdims=True)
        - normed * jnp.mean(scaled * normed, axis=-1, keepdims=True)
    )
    return (inner * inverse, jnp.sum(incoming * normed, axis=0))


def across(left, right):
    return lax.dot_general(
        left, right, (((0,), (0,)), ((), ())), preferred_element_type=jnp.float32
    )


def against(left, right):
    return lax.dot_general(
        left, right, (((1,), (1,)), ((), ())), preferred_element_type=jnp.float32
    )


def smooth(values):
    return jax.nn.gelu(values, approximate=True)


def scores_of(queries, key_rows, allowed):
    raw_scores = jnp.einsum(
        "gqhd,gkhd->ghqk", queries, key_rows, preferred_element_type=jnp.float32
    )
    return jnp.where(allowed[:, None], raw_scores * queries.shape[-1] ** (-0.5), NEGATIVE)


def attend_forward(block):
    stacked, allowed = block
    queries = stacked[:, :, 0]
    key_rows = stacked[:, :, 1]
    value_rows = stacked[:, :, 2]
    scores = scores_of(queries, key_rows, allowed)
    highest = jnp.max(scores, axis=-1, keepdims=True)
    raised = jnp.exp(scores - highest)
    total = jnp.sum(raised, axis=-1, keepdims=True)
    weights = (raised / total).astype(jnp.bfloat16)
    mixed = jnp.einsum("ghqk,gkhd->gqhd", weights, value_rows, preferred_element_type=jnp.float32)
    return (mixed, highest + jnp.log(total))


def attend_backward(block):
    stacked, allowed, log_total, grad_mixed = block
    queries = stacked[:, :, 0]
    key_rows = stacked[:, :, 1]
    value_rows = stacked[:, :, 2]
    scores = scores_of(queries, key_rows, allowed)
    probs = jnp.exp(scores - log_total)
    weights = probs.astype(jnp.bfloat16)
    grad_value = jnp.einsum(
        "ghqk,gqhd->gkhd", weights, grad_mixed, preferred_element_type=jnp.float32
    )
    grad_probs = jnp.einsum(
        "gqhd,gkhd->ghqk", grad_mixed, value_rows, preferred_element_type=jnp.float32
    )
    inner = jnp.sum(probs * grad_probs, axis=-1, keepdims=True)
    grad_raw = (probs * (grad_probs - inner) * queries.shape[-1] ** (-0.5)).astype(jnp.bfloat16)
    grad_query = jnp.einsum(
        "ghqk,gkhd->gqhd", grad_raw, key_rows, preferred_element_type=jnp.float32
    )
    grad_key = jnp.einsum("ghqk,gqhd->gkhd", grad_raw, queries, preferred_element_type=jnp.float32)
    return jnp.stack([grad_query, grad_key, grad_value], axis=2)


def shards(
    block_input,
    lengths,
    segments,
    gain_attn,
    w_qkv,
    w_attn_out,
    gain_mlp,
    w_mlp_in,
    w_mlp_out,
    cotangent,
):
    gathered = (
        lax.all_gather(gain_attn, "fsdp", axis=0, tiled=True),
        lax.all_gather(w_qkv, "fsdp", axis=0, tiled=True),
        lax.all_gather(w_attn_out, "fsdp", axis=0, tiled=True),
        lax.all_gather(gain_mlp, "fsdp", axis=0, tiled=True),
        lax.all_gather(w_mlp_in, "fsdp", axis=0, tiled=True),
        lax.all_gather(w_mlp_out, "fsdp", axis=0, tiled=True),
    )
    full_gain_attn, full_qkv, full_attn_out, full_gain_mlp, full_mlp_in, full_mlp_out = gathered
    allowed = permitted(lengths, segments)
    row_count, row_span = (allowed.shape[0], allowed.shape[1])
    per_block = math.gcd(row_count, max(1, 512 // row_span))
    block_count = row_count // per_block
    token_count, width = block_input.shape
    inputs = block_input.astype(jnp.float32)
    normed_one, inverse_one = moments(inputs)
    gain_one = full_gain_attn.astype(jnp.float32)
    normed_attn = (normed_one * gain_one).astype(jnp.bfloat16)
    projected = jnp.dot(normed_attn, full_qkv, preferred_element_type=jnp.float32).astype(
        jnp.bfloat16
    )
    stacked = projected.reshape(block_count, per_block, row_span, 3, HEADS, HEAD)
    allowed_blocks = allowed.reshape(block_count, per_block, row_span, row_span)
    mixed, log_total = lax.map(attend_forward, (stacked, allowed_blocks))
    mixed_low = mixed.reshape(token_count, width).astype(jnp.bfloat16)
    middle = inputs + jnp.dot(mixed_low, full_attn_out, preferred_element_type=jnp.float32)
    normed_two, inverse_two = moments(middle)
    gain_two = full_gain_mlp.astype(jnp.float32)
    normed_mlp = (normed_two * gain_two).astype(jnp.bfloat16)
    hidden = jnp.dot(normed_mlp, full_mlp_in, preferred_element_type=jnp.float32)
    active = smooth(hidden).astype(jnp.bfloat16)
    result = middle + jnp.dot(active, full_mlp_out, preferred_element_type=jnp.float32)
    block_output = result.astype(jnp.bfloat16)
    again = (
        lax.all_gather(gain_attn, "fsdp", axis=0, tiled=True),
        lax.all_gather(w_qkv, "fsdp", axis=0, tiled=True),
        lax.all_gather(w_attn_out, "fsdp", axis=0, tiled=True),
        lax.all_gather(gain_mlp, "fsdp", axis=0, tiled=True),
        lax.all_gather(w_mlp_in, "fsdp", axis=0, tiled=True),
        lax.all_gather(w_mlp_out, "fsdp", axis=0, tiled=True),
    )
    full_gain_attn, full_qkv, full_attn_out, full_gain_mlp, full_mlp_in, full_mlp_out = again
    gain_one = full_gain_attn.astype(jnp.float32)
    gain_two = full_gain_mlp.astype(jnp.float32)
    grad_out = cotangent.astype(jnp.float32)
    grad_branch = grad_out.astype(jnp.bfloat16)
    grad_mlp_out = across(active, grad_branch)
    grad_active = against(grad_branch, full_mlp_out)
    unused, smooth_back = jax.vjp(smooth, hidden)
    grad_hidden = smooth_back(grad_active)[0].astype(jnp.bfloat16)
    grad_mlp_in = across(normed_mlp, grad_hidden)
    grad_normed_mlp = against(grad_hidden, full_mlp_in)
    grad_middle_norm, grad_gain_mlp = norm_back(grad_normed_mlp, normed_two, inverse_two, gain_two)
    grad_middle = grad_out + grad_middle_norm
    grad_attn_branch = grad_middle.astype(jnp.bfloat16)
    grad_attn_out = across(mixed_low, grad_attn_branch)
    grad_mixed = against(grad_attn_branch, full_attn_out).astype(jnp.bfloat16)
    grad_mixed_blocks = grad_mixed.reshape(block_count, per_block, row_span, HEADS, HEAD)
    grad_stacked = lax.map(attend_backward, (stacked, allowed_blocks, log_total, grad_mixed_blocks))
    grad_projected = grad_stacked.reshape(token_count, 3 * width).astype(jnp.bfloat16)
    grad_qkv = across(normed_attn, grad_projected)
    grad_normed_attn = against(grad_projected, full_qkv)
    grad_input_norm, grad_gain_attn = norm_back(grad_normed_attn, normed_one, inverse_one, gain_one)
    grad_input = (grad_middle + grad_input_norm).astype(jnp.bfloat16)
    owned = (
        lax.psum_scatter(grad_gain_attn, "fsdp", scatter_dimension=0, tiled=True),
        lax.psum_scatter(grad_qkv, "fsdp", scatter_dimension=0, tiled=True),
        lax.psum_scatter(grad_attn_out, "fsdp", scatter_dimension=0, tiled=True),
        lax.psum_scatter(grad_gain_mlp, "fsdp", scatter_dimension=0, tiled=True),
        lax.psum_scatter(grad_mlp_in, "fsdp", scatter_dimension=0, tiled=True),
        lax.psum_scatter(grad_mlp_out, "fsdp", scatter_dimension=0, tiled=True),
    )
    summed = lax.psum((owned[0], owned[1], owned[2], owned[3], owned[4], owned[5]), "rep")
    return (
        block_output,
        grad_input,
        summed[0],
        summed[1],
        summed[2],
        summed[3],
        summed[4],
        summed[5],
    )


def solution(mesh):
    return jax.shard_map(
        shards,
        mesh=mesh,
        in_specs=(
            P(("rep", "fsdp"), None),
            P(("rep", "fsdp"), None),
            P(("rep", "fsdp")),
            P("fsdp"),
            P("fsdp", None),
            P("fsdp", None),
            P("fsdp"),
            P("fsdp", None),
            P("fsdp", None),
            P(("rep", "fsdp"), None),
        ),
        out_specs=(
            P(("rep", "fsdp"), None),
            P(("rep", "fsdp"), None),
            P("fsdp"),
            P("fsdp", None),
            P("fsdp", None),
            P("fsdp"),
            P("fsdp", None),
            P("fsdp", None),
        ),
        check_vma=False,
    )
```

profile of v0, /device:TPU:0, one launch (start us, length us, event | category | flops | bytes accessed | tf_op | source)
XLA Modules:
  0.0 764.0 jit_solution(10944796776455292124)
XLA Ops:
  17.1 15.6 %all-reduce.7 = (bf16[768]{0:T(1024)(128)(2,1)S(1)}, bf16[768]{0:T(1024)(128)(2,1)S(1)}) all-reduce(bf16[768]{0:T(1024)(128)(2,1)S(1)} %dynamic-update-slice, bf16[768]{0:T(1024)(128)(2,1)S(1)} %dynamic-update-slice.1), channel_id=1, replica_groups=mesh['rep'=4,'fsdp'=8] {'fsdp'}, use_global_device_ids=true, to_apply=%add | all-reduce | flops 1536 | bytes 6144
  46.7 12.2 %convolution_convert_fusion = bf16[2048,2304]{1,0:T(8,128)(2,1)} fusion(bf16[768,2304]{1,0:T(8,128)(2,1)} %all-gather.5.cloned.1.call-done, bf16[2048,768]{0,1:T(8,128)(2,1)S(1)} %copy.50, f32[768]{0:T(1024)} %convert_element_type.64, f32[2048]{0:T(1024)S(1)} %add_rsqrt_fusion.1, f32[2048]{0:T(1024)S(1)} %broadcast_multiply_fusion.5), kind=kOutput, calls=%fused_computation.56 | convolution fusion | flops 7260340224 | bytes 16141312 | tf_op jit(solution)/shard_map/dot_general | solution.py:136
  58.9 12.7 %copy.51 = bf16[2048,2304]{0,1:T(8,128)(2,1)} copy(bf16[2048,2304]{1,0:T(8,128)(2,1)} %convolution_convert_fusion) | data formatting | bytes 18874368 | tf_op jit(solution)/shard_map/convert_element_type | solution.py:136
  71.7 16.0 %reshape.134 = bf16[4,4,128,3,12,64]{2,1,0,5,4,3:T(4,128)(2,1)} reshape(bf16[2048,2304]{0,1:T(8,128)(2,1)} %copy.51) | data formatting | bytes 18874368 | tf_op jit(solution)/shard_map/reshape | solution.py:139
  87.7 10.1 %copy.52 = bf16[4,4,128,3,12,64]{2,5,4,1,3,0:T(8,128)(2,1)} copy(bf16[4,4,128,3,12,64]{2,1,0,5,4,3:T(4,128)(2,1)} %reshape.134) | data formatting | bytes 18874368 | tf_op jit(solution)/shard_map/while | solution.py:141
  97.8 23.7 %while.22 = (s32[]{:T(128)}, bf16[4,4,128,12,64]{2,4,3,1,0:T(8,128)(2,1)}, f32[4,4,12,128,1]{3,2,1,4,0:T(8,128)S(1)}, bf16[4,4,128,3,12,64]{2,5,4,1,3,0:T(8,128)...) while((s32[]{:T(128)}, bf16[4,4,128,12,64]{2,4,3,1,0:T(8,128)(2,1)}, ...), condition=%wide.region_6.7_spmd, body=%wide.region_3.6_spmd.sunk | while | flops 210757632 | bytes 18653776 | solution.py:141
  142.2 18.5 %fusion.64 = f32[2048,3072]{1,0:T(8,128)} fusion(bf16[768,3072]{1,0:T(8,128)(2,1)} %all-gather.9.cloned.1.call-done, f32[2048,768]{0,1:T(8,128)} %copy-done.2, f32[768]{0:T(1024)} %convert_element_type.69, f32[2048]{0:T(1024)S(1)} %add_rsqrt_fusion, f32[2048]{0:T(1024)S(1)} %broadcast_multiply_fusion.4), kind=kOutput, calls=%fused_computation.100 | convolution fusion | flops 9669967872 | bytes 36195328 | tf_op jit(solution)/shard_map/dot_general | solution.py:147
  160.7 27.5 %fusion.42 = bf16[2048,3072]{1,0:T(8,128)(2,1)} fusion(f32[2048,3072]{1,0:T(8,128)} %fusion.64, bf16[2048,768]{1,0:T(8,128)(2,1)S(1)} %copy-done.6, bf16[3072,768]{1,0:T(8,128)(2,1)} %all-gather.11.cloned.1.call-done), kind=kOutput, calls=%fused_computation.54 | convolution fusion | flops 9789505536 | bytes 45613056 | tf_op jit(solution)/shard_map/dot_general | solution.py:53
  188.2 16.2 %multiply_reduce_fusion.1 = (f32[768]{0:T(1024)}, f32[2048]{0:T(1024)S(1)}, f32[2048]{0:T(1024)S(1)}, f32[2048,768]{0,1:T(8,128)S(1)}) fusion(f32[2048,768]{0,1:T(8,128)S(1)} %copy-done.3, f32[2048]{0:T(1024)S(1)} %add_rsqrt_fusion, f32[2048]{0:T(1024)S(1)} %broadcast_multiply_fusion.4, f32[768]{0:T(1024)S(1)} %copy-done.12, ...), kind=kOutput, calls=%fused_computation.74 | convolution fusion | flops 9676254208 | bytes 29923328 | tf_op jit(solution)/shard_map/dot_general | solution.py:53
  213.6 7.2 convolution_convert_fusion.1
  227.9 115.0 %while.23 = (s32[]{:T(128)}, bf16[4,4,128,3,12,64]{2,5,4,1,3,0:T(8,128)(2,1)}, bf16[4,4,128,3,12,64]{2,5,4,1,3,0:T(8,128)(2,1)}, pred[4,4,128,128]{2,3,1,0:T(8,1...) while((s32[]{:T(128)}, ...), condition=%wide.region_13.14_spmd, body=%wide.region_11.13_spmd.sunk | while | flops 521416960 | bytes 53756508 | solution.py:176
  342.9 12.2 %copy.59 = bf16[4,4,128,3,12,64]{2,1,0,5,4,3:T(4,128)(2,1)} copy(bf16[4,4,128,3,12,64]{2,5,4,1,3,0:T(8,128)(2,1)} %get-tuple-element.70) | data formatting | bytes 18874368 | tf_op jit(solution)/shard_map/convert_element_type | solution.py:177
  355.2 16.3 %convert_element_type.78 = bf16[2048,2304]{0,1:T(8,128)(2,1)} reshape(bf16[4,4,128,3,12,64]{2,1,0,5,4,3:T(4,128)(2,1)} %copy.59) | data formatting | bytes 18874368 | tf_op jit(solution)/shard_map/convert_element_type | solution.py:177
  371.4 13.0 %fusion.60 = f32[768,2304]{1,0:T(8,128)} fusion(bf16[2048,2304]{0,1:T(8,128)(2,1)} %convert_element_type.78, bf16[2048,768]{0,1:T(8,128)(2,1)S(1)} %copy-done.1, f32[768]{0:T(1024)S(1)} %copy-done.14, f32[2048]{0:T(1024)S(1)} %copy-done.11, f32[2048]{0:T(1024)S(1)} %copy-done.9), kind=kOutput, calls=%fused_computation.88 | convolution fusion | flops 7255621632 | bytes 19680256 | tf_op jit(solution)/shard_map/dot_general | solution.py:47
  385.1 17.3 %fusion.63 = f32[768,3072]{1,0:T(8,128)} fusion(bf16[2048,3072]{1,0:T(8,128)(2,1)} %fusion.42, f32[2048,768]{0,1:T(8,128)} %copy-done.2, f32[768]{0:T(1024)S(1)} %copy-done.13, f32[2048]{0:T(1024)S(1)} %add_rsqrt_fusion, f32[2048]{0:T(1024)S(1)} %broadcast_multiply_fusion.4), kind=kOutput, calls=%fused_computation.99 | convolution fusion | flops 9669967872 | bytes 28331008 | tf_op jit(solution)/shard_map/dot_general | solution.py:47
  402.5 21.5 %fusion.65 = f32[3072,768]{1,0:T(8,128)} fusion(bf16[2048,768]{1,0:T(8,128)(2,1)} %param.23, f32[2048,3072]{1,0:T(8,128)} %fusion.64), kind=kOutput, calls=%fused_computation.101 | convolution fusion | flops 9720299520 | bytes 37748736 | tf_op jit(solution)/shard_map/dot_general | solution.py:47
  424.7 14.0 %fusion.55 = (f32[768]{0:T(1024)S(1)}, f32[2048]{0:T(1024)S(1)}, f32[2048]{0:T(1024)S(1)}, f32[2048,768]{0,1:T(8,128)}) fusion(bf16[2048,768]{0,1:T(8,128)(2,1)S(1)} %copy-done.1, f32[2048]{0:T(1024)S(1)} %copy-done.11, f32[2048]{0:T(1024)S(1)} %copy-done.9, f32[768]{0:T(1024)S(1)} %copy-done.14, bf16[768,2304]{1,0:T(8,128)(2,1)} %all-gather.5.cloned.1.call-done, ...), kind=kOutput, calls=%fused_computation.72 | convolution fusion | flops 7261907968 | bytes 22452224 | tf_op jit(solution)/shard_map/dot_general | solution.py:53
  438.7 14.2 %all-reduce.4 = (f32[768]{0:T(1024)S(1)}, f32[768]{0:T(1024)S(1)}) all-reduce(f32[768]{0:T(1024)S(1)} %get-tuple-element.130, f32[768]{0:T(1024)S(1)} %copy-done.15), channel_id=2, replica_groups=mesh['rep'=4,'fsdp'=8] {'fsdp'}, use_global_device_ids=true, to_apply=%region_17.18.clone | all-reduce | flops 1536 | bytes 12288
  453.0 7.0 fusion.54
  465.1 65.9 %reduce-scatter.9.cloned.1.call-done = f32[96,3072]{1,0:T(8,128)} async-done(((f32[768,3072]{1,0:T(8,128)}), f32[96,3072]{1,0:T(8,128)}) %reduce-scatter.9.cloned.1.call-update) | async-done | bytes 1179664 | tf_op jit(solution)/shard_map/reduce_scatter | solution.py:187
  531.0 80.0 %reduce-scatter.11.cloned.1.call-done = f32[384,768]{1,0:T(8,128)} async-done(((f32[3072,768]{1,0:T(8,128)}), f32[384,768]{1,0:T(8,128)}) %reduce-scatter.11.cloned.1.call-update) | async-done | bytes 1179664 | tf_op jit(solution)/shard_map/reduce_scatter | solution.py:188
  611.1 17.5 %add_convert_fusion = bf16[2048,768]{0,1:T(8,128)(2,1)S(1)} fusion(f32[2048,768]{0,1:T(8,128)} %copy-done.2, bf16[3072,768]{1,0:T(8,128)(2,1)} %all-gather.11.cloned.1.call-done, f32[2048,3072]{1,0:T(8,128)} %fusion.64), kind=kOutput, calls=%fused_computation.77 | convolution fusion | flops 9723445248 | bytes 39321600 | tf_op jit(solution)/shard_map/dot_general | solution.py:149
  631.3 12.9 %all-reduce.5 = (f32[96]{0:T(128)}, f32[96]{0:T(128)}) all-reduce(f32[96]{0:T(128)S(1)} %dynamic-slice.3, f32[96]{0:T(128)S(1)} %dynamic-slice.5), channel_id=1, replica_groups=mesh['rep'=4,'fsdp'=8] {'rep'}, use_global_device_ids=true, to_apply=%region_18.19 | all-reduce | flops 192 | bytes 1536 | tf_op jit(solution)/shard_map/psum | solution.py:190
  644.3 104.5 %all-reduce.10.cloned.1.call-done = (f32[96,2304]{1,0:T(8,128)}, f32[96,768]{1,0:T(8,128)}, f32[96,3072]{1,0:T(8,128)}, f32[384,768]{1,0:T(8,128)}) async-done(((f32[96,2304]{1,0:T(8,128)}, f32[96,768]{1,0:T(8,128)}, f32[96,3072]{1,0:T(8,128)}, f32[384,768]{1,0:T(8,128)}), (f32[96,2304]{1,0:T(8,128)}, f32[96,768]{1,0:T(8,128)}, f32[96,3072]{1,0:T(8,128)}, ...) | async-done | bytes 3538960 | tf_op jit(solution)/shard_map/psum | solution.py:190
  (172 shorter events, 215.1 us)
Async XLA Ops:
  7.2 39.5 %all-gather.5.cloned.1.call-start = ((), (), s32[]{:S(2)}) async-start(), calls=%async_computation.4 | async-start | bytes 3981312 | tf_op jit(solution)/shard_map/all_gather | solution.py:120
  7.9 126.0 %all-gather.7.cloned.1.call-start = ((), (), s32[]{:S(2)}) async-start(), calls=%async_computation.5 | async-start | bytes 1327104 | tf_op jit(solution)/shard_map/all_gather | solution.py:121
  8.6 133.6 %all-gather.9.cloned.1.call-start = ((), (), s32[]{:S(2)}) async-start(), calls=%async_computation.6 | async-start | bytes 5308416 | tf_op jit(solution)/shard_map/all_gather | solution.py:123
  9.4 151.3 %all-gather.11.cloned.1.call-start = ((), (), s32[]{:S(2)}) async-start(), calls=%async_computation.7 | async-start | bytes 5308416 | tf_op jit(solution)/shard_map/all_gather | solution.py:124
  10.0 455.1 %reduce-scatter.7.cloned.1.call-start = ((), (), s32[]{:S(2)}) async-start(), calls=%async_computation.9 | async-start | bytes 2654208 | tf_op jit(solution)/shard_map/reduce_scatter | solution.py:185
  10.6 6.0 copy-start.19
  10.6 6.2 copy-start.20
  10.7 22.6 %copy-start.17 = (s32[16,4]{0,1:T(4,128)S(1)}, s32[16,4]{0,1:T(4,128)}, u32[]{:S(2)}) copy-start(s32[16,4]{0,1:T(4,128)} %param.15) | copy-start | bytes 772
  13.9 120.0 %copy-start = (bf16[2048,768]{0,1:T(8,128)(2,1)}, bf16[2048,768]{0,1:T(8,128)(2,1)S(1)}, u32[]{:S(2)}) copy-start(bf16[2048,768]{0,1:T(8,128)(2,1)S(1)} %copy.50) | copy-start | bytes 9437188
  14.4 44.5 %copy-start.8 = (f32[2048]{0:T(1024)}, f32[2048]{0:T(1024)S(1)}, u32[]{:S(2)}) copy-start(f32[2048]{0:T(1024)S(1)} %broadcast_multiply_fusion.5) | copy-start | bytes 24580
  15.3 43.7 %copy-start.10 = (f32[2048]{0:T(1024)}, f32[2048]{0:T(1024)S(1)}, u32[]{:S(2)}) copy-start(f32[2048]{0:T(1024)S(1)} %add_rsqrt_fusion.1) | copy-start | bytes 24580
  142.2 18.5 %copy-start.6 = (bf16[2048,768]{1,0:T(8,128)(2,1)S(1)}, bf16[2048,768]{1,0:T(8,128)(2,1)}, u32[]{:S(2)}) copy-start(bf16[2048,768]{1,0:T(8,128)(2,1)} %param.23) | copy-start | bytes 9437188
  160.7 27.5 %copy-start.3 = (f32[2048,768]{0,1:T(8,128)S(1)}, f32[2048,768]{0,1:T(8,128)}, u32[]{:S(2)}) copy-start(f32[2048,768]{0,1:T(8,128)} %copy-done.2) | copy-start | bytes 18874372
  160.7 27.5 %copy-start.12 = (f32[768]{0:T(1024)S(1)}, f32[768]{0:T(1024)}, u32[]{:S(2)}) copy-start(f32[768]{0:T(1024)} %convert_element_type.69) | copy-start | bytes 9220
  188.2 16.2 %copy-start.5 = (bf16[2048,768]{0,1:T(8,128)(2,1)S(1)}, bf16[2048,768]{0,1:T(8,128)(2,1)}, u32[]{:S(2)}) copy-start(bf16[2048,768]{0,1:T(8,128)(2,1)} %copy.55) | copy-start | bytes 9437188
  227.9 237.2 %reduce-scatter.5.cloned.1.call-start = ((), (), s32[]{:S(2)}) async-start(), calls=%async_computation.8 | async-start | bytes 7962624 | tf_op jit(solution)/shard_map/reduce_scatter | solution.py:184
  355.1 16.3 %copy-start.1 = (bf16[2048,768]{0,1:T(8,128)(2,1)S(1)}, bf16[2048,768]{0,1:T(8,128)(2,1)}, u32[]{:S(2)}) copy-start(bf16[2048,768]{0,1:T(8,128)(2,1)} %copy-done) | copy-start | bytes 9437188
  355.1 16.3 %copy-start.9 = (f32[2048]{0:T(1024)S(1)}, f32[2048]{0:T(1024)}, u32[]{:S(2)}) copy-start(f32[2048]{0:T(1024)} %copy-done.8) | copy-start | bytes 24580
  355.1 16.3 %copy-start.11 = (f32[2048]{0:T(1024)S(1)}, f32[2048]{0:T(1024)}, u32[]{:S(2)}) copy-start(f32[2048]{0:T(1024)} %copy-done.10) | copy-start | bytes 24580
  355.1 16.3 %copy-start.14 = (f32[768]{0:T(1024)S(1)}, f32[768]{0:T(1024)}, u32[]{:S(2)}) copy-start(f32[768]{0:T(1024)} %convert_element_type.64) | copy-start | bytes 9220
  384.4 146.6 %reduce-scatter.9.cloned.1.call-start = ((), (), s32[]{:S(2)}) async-start(), calls=%async_computation.10 | async-start | bytes 10616832 | tf_op jit(solution)/shard_map/reduce_scatter | solution.py:187
  402.5 208.6 %reduce-scatter.11.cloned.1.call-start = ((), (), s32[]{:S(2)}) async-start(), calls=%async_computation.11 | async-start | bytes 10616832 | tf_op jit(solution)/shard_map/reduce_scatter | solution.py:188
  424.0 324.7 %all-reduce.10.cloned.1.call-start = ((), (), s32[]{:S(2)}) async-start(), calls=%async_computation.12 | async-start | bytes 7077888 | tf_op jit(solution)/shard_map/psum | solution.py:190
  424.7 14.0 %copy-start.15 = (f32[768]{0:T(1024)S(1)}, f32[768]{0:T(1024)}, u32[]{:S(2)}) copy-start(f32[768]{0:T(1024)} %get-tuple-element.128) | copy-start | bytes 9220
  (6 other events, 19.9 us)
Sparse Core Ops, SparseCore 0:
  9.9 36.7 all-gather.4
  48.6 24.0 all-gather.6
  74.6 38.9 all-gather.8
  115.3 38.9 all-gather.10
  228.0 42.8 reduce-scatter.6
  384.6 66.2 reduce-scatter.4
  454.4 76.5 reduce-scatter.8
  534.5 76.4 reduce-scatter.10
  613.7 135.0 all-reduce.9
where the time goes:
time: 769 us; the launch traced here: 764 us
  matrix products  270 us (35%)
  waiting for transfers between devices  259 us (34%)
  local copies, waits for them, and re-layouts  143 us (19%)
  blocking collectives  42.7 us (6%)
  other arithmetic  32.2 us (4%)
  between operations  15.6 us (2%)
    psum x1, waiting for transfers between devices, shards(): lax.psum((owned[0], owned[1], owned[2], owned[3], owned[4], owned[5]), 'r...  104 us
    reduce_scatter x1, waiting for transfers between devices, shards(): lax.psum_scatter(grad_mlp_out, 'fsdp', scatter_dimension=0, tiled=True)  80 us
    reduce_scatter x1, waiting for transfers between devices, shards(): lax.psum_scatter(grad_mlp_in, 'fsdp', scatter_dimension=0, tiled=True)  65.9 us
    dot_general x4, matrix products, against(): lax.dot_general(left, right, (((1,), (1,)), ((), ())), preferred_element_...  64.8 us
    dot_general x4, matrix products, across(): lax.dot_general(left, right, (((0,), (0,)), ((), ())), preferred_element_...  55.9 us
    unnamed x57, local copies, waits for them, and re-layouts  31.5 us
    unnamed x2, blocking collectives  29.8 us
    convert_element_type x2, local copies, waits for them, and re-layouts, shards(): grad_stacked.reshape(token_count, 3 * width).astype(jnp.bfloat16)  28.5 us
  transfers between devices with their start and end apart: 9, of which 4 were waited for; matrix products, arithmetic and copies ran while one was open for 48% of the time, Pallas kernels for 0%

commit v1 on v0

v1 whole, which is shorter than its diff:
```python
import functools, math
import jax, jax.numpy as jnp
from jax import lax
from jax.experimental import pallas as pl
from jax.experimental.pallas import tpu as pltpu
from jax.sharding import PartitionSpec as P
bf = jnp.bfloat16
f32 = jnp.float32
EPS = 1e-05
NEG = -1e30
SPAN = 128
TILE = 256
VMEM = 60 * 1024 * 1024
SCALE = 64 ** -0.5
LOG2E = math.log2(math.e)
GC = math.sqrt(2.0 / math.pi)
GK = 0.044715


def nn(a, b):
    return lax.dot_general(a, b, (((1,), (0,)), ((), ())), preferred_element_type=f32)


def nt(a, b):
    return lax.dot_general(a, b, (((1,), (1,)), ((), ())), preferred_element_type=f32)


def tn(a, b):
    return lax.dot_general(a, b, (((0,), (0,)), ((), ())), preferred_element_type=f32)


def moments(v):
    c = v - jnp.mean(v, axis=-1, keepdims=True)
    r = lax.rsqrt(jnp.mean(c * c, axis=-1, keepdims=True) + EPS)
    return c * r, r


def norm_back(e, n, r, g):
    s = e * g
    inner = s - jnp.mean(s, axis=-1, keepdims=True) - n * jnp.mean(s * n, axis=-1, keepdims=True)
    return inner * r


def split_heads(t):
    low = lax.broadcasted_iota(jnp.int32, t.shape, 1) < 64
    zero = jnp.zeros_like(t)
    return jnp.concatenate([jnp.where(low, t, zero), jnp.where(low, zero, t)], axis=0)


def stack_lanes(t):
    return jnp.concatenate([t[:, :SPAN], t[:, SPAN:]], axis=0)


def permitted(lengths, row):
    ends = []
    total = 0
    for k in range(4):
        total = total + lengths[row, k]
        ends.append(total)
    key = lax.broadcasted_iota(jnp.int32, (SPAN, SPAN), 0)
    query = lax.broadcasted_iota(jnp.int32, (SPAN, SPAN), 1)
    one, zero = jnp.int32(1), jnp.int32(0)
    seg_key = sum(jnp.where(key >= e, one, zero) for e in ends)
    seg_query = sum(jnp.where(query >= e, one, zero) for e in ends)
    return (seg_key == seg_query) & ((key < total) | (key == query))


def attend(qkv, mask):
    mask2 = jnp.concatenate([mask, mask], axis=1)
    probs, mixed = [], []
    for p in range(6):
        q2, k2, v2 = qkv(p * 128), qkv(768 + p * 128), qkv(1536 + p * 128)
        s = jnp.where(mask2, nt(k2, split_heads(q2)), NEG)
        top = jnp.max(s, axis=0, keepdims=True)
        e = jnp.exp2((s - top) * (SCALE * LOG2E))
        w = (e * (1.0 / jnp.sum(e, axis=0, keepdims=True))).astype(bf)
        probs.append(w)
        mixed.append(tn(stack_lanes(w), split_heads(v2)).astype(bf))
    return probs, mixed


def attend_back(qkv, w, do2, p):
    q2, k2, v2 = qkv(p * 128), qkv(768 + p * 128), qkv(1536 + p * 128)
    do_bd = split_heads(do2)
    dv = nn(w, do_bd)
    dp = nt(v2, do_bd)
    pf = w.astype(f32)
    pd = pf * dp
    inner = jnp.sum(pd, axis=0, keepdims=True)
    draw = ((pd - pf * inner) * SCALE).astype(bf)
    dq = tn(stack_lanes(draw), split_heads(k2))
    dk = nn(draw, split_heads(q2))
    return dq.astype(bf), dk.astype(bf), dv.astype(bf)


def kernel_ab(lengths, x, gain, w_qkv, qkv_out, probs_out, o_out):
    i = pl.program_id(0)
    n, _ = moments(x[...].astype(f32))
    u = (n * gain[...]).astype(bf)
    qkv_out[...] = nn(u, w_qkv[...]).astype(bf)
    for rr in range(TILE // SPAN):
        rows = slice(rr * SPAN, (rr + 1) * SPAN)
        mask = permitted(lengths, i * (TILE // SPAN) + rr)
        probs, mixed = attend(lambda c: qkv_out[rows, c : c + 128], mask)
        for p in range(6):
            probs_out[rr, p] = probs[p]
            o_out[rows, p * 128 : (p + 1) * 128] = mixed[p]


def gelu_both(t):
    t2 = t * t
    th = jnp.tanh(t * (GC + (GC * GK) * t2))
    half = 0.5 + 0.5 * th
    a = t * half
    slope = half + (0.5 * t) * (1.0 - th * th) * (GC + (3.0 * GC * GK) * t2)
    return a, slope


FC = 768


def kernel_c(x, o, dy, gain, w_ao, w_in, w_out, y_out, wn_out, a_out, dz_out, dh_out, do_out, gg_out):
    i = pl.program_id(0)
    h = x[...].astype(f32) + nn(o[...], w_ao[...])
    n, r = moments(h)
    g = gain[...]
    wn = (n * g).astype(bf)
    wn_out[...] = wn
    dm = dy[...]
    y = h
    dw = None
    for j in range(w_in.shape[1] // FC):
        cols = slice(j * FC, (j + 1) * FC)
        a, slope = gelu_both(nn(wn, w_in[:, cols]))
        a = a.astype(bf)
        a_out[:, cols] = a
        y = y + nn(a, w_out[cols, :])
        dz = (nt(dm, w_out[cols, :]) * slope).astype(bf)
        dz_out[:, cols] = dz
        t = nt(dz, w_in[:, cols])
        dw = t if dw is None else dw + t
    y_out[...] = y.astype(bf)
    dh = dm.astype(f32) + norm_back(dw, n, r, g)
    dh_out[...] = dh
    do_out[...] = nt(dh.astype(bf), w_ao[...]).astype(bf)
    part = jnp.sum((dw * n).reshape(-1, 8, dw.shape[1]), axis=0)

    @pl.when(i == 0)
    def _():
        gg_out[...] = part

    @pl.when(i > 0)
    def _():
        gg_out[...] += part


def kernel_d1(wn, dz, g):
    g[...] = tn(wn[...], dz[...]).astype(g.dtype)


def kernel_e(qkv, probs, do, dqkv):
    for rr in range(TILE // SPAN):
        rows = slice(rr * SPAN, (rr + 1) * SPAN)
        for p in range(6):
            cols = slice(p * 128, (p + 1) * 128)
            dq, dk, dv = attend_back(lambda c: qkv[rows, c : c + 128], probs[rr, p], do[rows, cols], p)
            dqkv[rows, p * 128 : p * 128 + 128] = dq
            dqkv[rows, 768 + p * 128 : 768 + p * 128 + 128] = dk
            dqkv[rows, 1536 + p * 128 : 1536 + p * 128 + 128] = dv


def kernel_f(x, dqkv, dh, gain, w_qkv, dx_out, gg_out):
    i = pl.program_id(0)
    n, r = moments(x[...].astype(f32))
    du = nt(dqkv[...], w_qkv[...])
    dx_out[...] = (dh[...] + norm_back(du, n, r, gain[...])).astype(bf)
    part = jnp.sum((du * n).reshape(-1, 8, du.shape[1]), axis=0)

    @pl.when(i == 0)
    def _():
        gg_out[...] = part

    @pl.when(i > 0)
    def _():
        gg_out[...] += part


def kernel_gq(x, gain, dqkv, g, u):
    @pl.when(pl.program_id(0) == 0)
    def _():
        for t in range(x.shape[0] // TILE):
            rows = slice(t * TILE, (t + 1) * TILE)
            n, _ = moments(x[rows].astype(f32))
            u[rows] = (n * gain[...]).astype(bf)

    g[...] = tn(u[...], dqkv[...]).astype(g.dtype)


def whole(shape):
    return pl.BlockSpec(shape, lambda i: (0,) * len(shape), pipeline_mode=pl.Buffered(1))


def rows_of(cols, tile=TILE):
    return pl.BlockSpec((tile, cols), lambda i: (i, 0))


def call(body, name, grid, in_specs, out_specs, out_shape, flops, nbytes, scratch=()):
    return pl.pallas_call(
        body,
        name=name,
        grid=grid,
        in_specs=in_specs,
        out_specs=out_specs,
        out_shape=out_shape,
        scratch_shapes=scratch,
        cost_estimate=pl.CostEstimate(flops=flops, bytes_accessed=nbytes, transcendentals=0),
        compiler_params=pltpu.CompilerParams(vmem_limit_bytes=VMEM),
    )


def sds(*shape, dtype=bf):
    return jax.ShapeDtypeStruct(shape, dtype)


def forward_attention(x, lengths, g1, w_qkv):
    T, D = x.shape
    rows = T // SPAN
    per = TILE // SPAN
    return call(
        kernel_ab, "attention_forward", (T // TILE,),
        [pl.BlockSpec(memory_space=pltpu.SMEM), rows_of(D), whole((1, D)), whole(w_qkv.shape)],
        [rows_of(3 * D), pl.BlockSpec((per, 6, SPAN, 2 * SPAN), lambda i: (i, 0, 0, 0)), rows_of(D)],
        [sds(T, 3 * D), sds(rows, 6, SPAN, 2 * SPAN), sds(T, D)],
        12 * T * D * D, 30 << 20,
    )(lengths, x, g1, w_qkv)


def mlp_both(x, o, dy, g2, w_ao, w_in, w_out):
    T, D = x.shape
    F = w_in.shape[1]
    return call(
        kernel_c, "mlp_both", (T // TILE,),
        [rows_of(D), rows_of(D), rows_of(D), whole((1, D)), whole(w_ao.shape), whole(w_in.shape), whole(w_out.shape)],
        [rows_of(D), rows_of(D), rows_of(F), rows_of(F), rows_of(D), rows_of(D), pl.BlockSpec((8, D), lambda i: (0, 0))],
        [sds(T, D), sds(T, D), sds(T, F), sds(T, F), sds(T, D, dtype=f32), sds(T, D), sds(8, D, dtype=f32)],
        8 * T * D * F + 4 * T * D * D, 60 << 20,
    )(x, o, dy, g2, w_ao, w_in, w_out)


def weight_grad(left, right, name, tile, out=bf, by="right"):
    T, M = left.shape
    N = right.shape[1]
    if by == "right":
        ins = [whole((T, M)), pl.BlockSpec((T, tile), lambda i: (0, i))]
        outs = pl.BlockSpec((M, tile), lambda i: (0, i))
        grid = (N // tile,)
    else:
        ins = [pl.BlockSpec((T, tile), lambda i: (0, i)), whole((T, N))]
        outs = pl.BlockSpec((tile, N), lambda i: (i, 0))
        grid = (M // tile,)
    return call(kernel_d1, name, grid, ins, outs, sds(M, N, dtype=out), 2 * T * M * N, 2 * (T * M + T * N + M * N))(left, right)


def attention_back(qkv, probs, do):
    T, D = do.shape
    per = TILE // SPAN
    return call(
        kernel_e, "attention_backward", (T // TILE,),
        [rows_of(3 * D), pl.BlockSpec((per, 6, SPAN, 2 * SPAN), lambda i: (i, 0, 0, 0)), rows_of(D)],
        rows_of(3 * D), sds(T, 3 * D), 8 * T * D * D, 30 << 20,
    )(qkv, probs, do)


def input_grad(x, dqkv, dh, g1, w_qkv):
    T, D = x.shape
    return call(
        kernel_f, "input_grad", (T // TILE,),
        [rows_of(D), rows_of(3 * D), rows_of(D), whole((1, D)), whole(w_qkv.shape)],
        [rows_of(D), pl.BlockSpec((8, D), lambda i: (0, 0))],
        [sds(T, D), sds(8, D, dtype=f32)],
        6 * T * D * D, 30 << 20,
    )(x, dqkv, dh, g1, w_qkv)


def qkv_grad(x, g1, dqkv, tile=768, out=bf):
    T, D = x.shape
    N = dqkv.shape[1]
    return call(
        kernel_gq, "qkv_grad", (N // tile,),
        [whole((T, D)), whole((1, D)), pl.BlockSpec((T, tile), lambda i: (0, i))],
        pl.BlockSpec((D, tile), lambda i: (0, i)), sds(D, N, dtype=out), 2 * T * D * N, 20 << 20,
        scratch=[pltpu.VMEM((T, D), bf)],
    )(x, g1, dqkv)


def shards(x, lengths, segments, gain_attn, w_qkv, w_attn_out, gain_mlp, w_mlp_in, w_mlp_out, dy):
    D = x.shape[1]
    gains = jnp.stack([gain_attn, gain_mlp], axis=1)
    packed = jnp.concatenate([w_qkv, jnp.pad(gains, ((0, 0), (0, 126)))], axis=1)
    gather = lambda v: lax.all_gather(v, "fsdp", axis=0, tiled=True)
    packed = gather(packed)
    wq = packed[:, : 3 * D]
    g1 = packed[:, 3 * D].astype(f32)[None]
    g2 = packed[:, 3 * D + 1].astype(f32)[None]
    wo, wi, wt = gather(w_attn_out), gather(w_mlp_in), gather(w_mlp_out)
    qkv, probs, o = forward_attention(x, lengths, g1, wq)
    y, wn, a, dz, dh, do, gg2 = mlp_both(x, o, dy, g2, wo, wi, wt)
    scatter = lambda v: lax.psum_scatter(v, "fsdp", scatter_dimension=0, tiled=True)
    gwt = scatter(weight_grad(a, dy, "mlp_out_grad", 768, bf, "left"))
    gwi = scatter(weight_grad(wn, dz, "mlp_in_grad", 768))
    gwo = scatter(weight_grad(o, dh.astype(bf), "attn_out_grad", 768))
    dqkv = attention_back(qkv, probs, do)
    gq = qkv_grad(x, g1, dqkv)
    dx, gg1 = input_grad(x, dqkv, dh, g1, wq)
    ends = jnp.stack([gg1.sum(0), gg2.sum(0)], axis=1).astype(bf)
    gq = scatter(jnp.concatenate([gq, jnp.pad(ends, ((0, 0), (0, 126)))], axis=1))
    gwt, gwi, gwo, gq = lax.psum((gwt, gwi, gwo, gq), "rep")
    gwt, gwi, gwo, gq = (v.astype(f32) for v in (gwt, gwi, gwo, gq))
    return y, dx, gq[:, 3 * D], gq[:, : 3 * D], gwo, gq[:, 3 * D + 1], gwi, gwt


def solution(mesh):
    tokens, cut, vec = P(("rep", "fsdp"), None), P("fsdp", None), P("fsdp")
    return jax.shard_map(
        shards,
        mesh=mesh,
        in_specs=(tokens, tokens, P(("rep", "fsdp")), vec, cut, cut, vec, cut, cut, tokens),
        out_specs=(tokens, tokens, vec, cut, cut, vec, cut, cut),
        check_vma=False,
    )
```

time: 769 us -> 549 us (0.71)
  matrix products: 270 us -> 0 us
  Pallas kernels: 0 us -> 177 us
  local copies, waits for them, and re-layouts: 143 us -> 9.64 us
  waiting for transfers between devices: 259 us -> 329 us
  blocking collectives: 42.7 us -> 0 us
  other arithmetic: 32.2 us -> 18.4 us
    dot_general x40 -> x0, matrix products: 270 us -> none  [the longest x4 64.8 us: against(): lax.dot_general(left, right, (((1,), (1,)), ((), ())), preferred_element_...]
    pallas_call x0 -> x8, Pallas kernels: none -> 177 us  [the longest x1 63.4 us: mlp_both(): call(kernel_c, 'mlp_both', (T // TILE,), [rows_of(D), rows_of(D), rows_of...]
    all_gather x4, waiting for transfers between devices: 5.8 us -> 112 us  [shards(): gather = lambda v: lax.all_gather(v, 'fsdp', axis=0, tiled=True)]
    convert_element_type x6 -> x2, local copies, waits for them, and re-layouts: 56.7 us -> 1.17 us  [the longest x1 0.59 us: shards(): g2 = packed[:, 3 * D + 1].astype(f32)[None]]
    unnamed x57 -> x7, local copies, waits for them, and re-layouts: 31.5 us -> 1.37 us
    unnamed x2 -> x0, blocking collectives: 29.8 us -> none
    psum x1, waiting for transfers between devices: 104 us -> 80.3 us  [shards(): gwt, gwi, gwo, gq = lax.psum((gwt, gwi, gwo, gq), 'rep')]
    reshape x2 -> x0, local copies, waits for them, and re-layouts: 19.8 us -> none  [the longest x1 16 us: shards(): projected.reshape(block_count, per_block, row_span, 3, HEADS, HEAD)]
  transfers between devices with their start and end apart: 9 -> 9, of which waited for: 4 -> 7; matrix products, arithmetic and copies ran while one was open for 48% -> 2% of each run, Pallas kernels for 0% -> 19%
where the time goes in v1:
time: 549 us; the launch traced here: 548 us
  waiting for transfers between devices  329 us (60%)
  Pallas kernels  177 us (32%)
  other arithmetic  18.4 us (3%)
  between operations  13.9 us (3%)
  local copies, waits for them, and re-layouts  9.64 us (2%)
    reduce_scatter x4, waiting for transfers between devices, shards(): lax.psum_scatter(v, 'fsdp', scatter_dimension=0, tiled=True)  135 us
    all_gather x4, waiting for transfers between devices, shards(): gather = lambda v: lax.all_gather(v, 'fsdp', axis=0, tiled=True)  112 us
    psum x1, waiting for transfers between devices, shards(): gwt, gwi, gwo, gq = lax.psum((gwt, gwi, gwo, gq), 'rep')  80.3 us
    pallas_call x1, Pallas kernels, mlp_both(): call(kernel_c, 'mlp_both', (T // TILE,), [rows_of(D), rows_of(D), rows_of...  63.4 us
    pallas_call x3, Pallas kernels, weight_grad(): call(kernel_d1, name, grid, ins, outs, sds(M, N, dtype=out), 2 * T * M *...  35.8 us
    pallas_call x1, Pallas kernels, forward_attention(): call(kernel_ab, 'attention_forward', (T // TILE,), [pl.BlockSpec(memory_s...  23.8 us
    pallas_call x1, Pallas kernels, attention_back(): call(kernel_e, 'attention_backward', (T // TILE,), [rows_of(3 * D), pl.Bl...  23.4 us
    pallas_call x1, Pallas kernels, input_grad(): call(kernel_f, 'input_grad', (T // TILE,), [rows_of(D), rows_of(3 * D), r...  16.4 us
  transfers between devices with their start and end apart: 9, of which 7 were waited for; matrix products, arithmetic and copies ran while one was open for 2% of the time, Pallas kernels for 19%

profile of v1, /device:TPU:0, one launch (start us, length us, event | category | flops | bytes accessed | tf_op | source)
XLA Modules:
  0.0 548.2 jit_solution(2819552660550013791)
XLA Ops:
  8.0 1.8 fusion.3
  12.0 1.4 copy.26.lengths
  13.3 34.7 %all-gather.5.cloned.1.call-done = bf16[768,2432]{1,0:T(8,128)(2,1)} async-done(((bf16[96,2432]{1,0:T(8,128)(2,1)}), bf16[768,2432]{1,0:T(8,128)(2,1)}) %all-gather.5.cloned.1.call-update) | async-done | bytes 3735568 | tf_op jit(solution)/shard_map/all_gather | solution.py:300
  48.0 1.3 convert_reduce_fusion
  50.5 4.0 slice.25.w_qkv
  54.5 23.8 %attention_forward.1 = (bf16[2048,2304]{1,0:T(8,128)(2,1)}, bf16[16,6,128,256]{3,2,1,0:T(8,128)(2,1)}, bf16[2048,768]{1,0:T(8,128)(2,1)}) custom-call(s32[16,4]{1,0:T(8,128)} %copy.26.lengths, bf16[2048,768]{1,0:T(8,128)(2,1)} %x.11, f32[1,768]{1,0:T(1,128)} %reshape.40.gain, bf16[768,2304]{1,0:T(8,128)(2,1)} %slice.25.w_qkv), custom_call_target="tpu_custom_call" | custom-call | flops 14495514624 | bytes 31457280 | tf_op jit(solution)/shard_map/attention_forward/pallas_call | solution.py:229
  78.3 36.6 %all-gather.9.cloned.1.call-done.w_in = bf16[768,3072]{1,0:T(8,128)(2,1)} async-done(((bf16[96,3072]{1,0:T(8,128)(2,1)}), bf16[768,3072]{1,0:T(8,128)(2,1)}) %all-gather.9.cloned.1.call-update) | async-done | bytes 4718608 | tf_op jit(solution)/shard_map/all_gather | solution.py:300
  114.8 40.7 %all-gather.11.cloned.1.call-done.w_out = bf16[3072,768]{1,0:T(8,128)(2,1)} async-done(((bf16[384,768]{1,0:T(8,128)(2,1)}), bf16[3072,768]{1,0:T(8,128)(2,1)}) %all-gather.11.cloned.1.call-update) | async-done | bytes 4718608 | tf_op jit(solution)/shard_map/all_gather | solution.py:300
  155.5 63.4 %mlp_both.1 = (bf16[2048,768]{1,0:T(8,128)(2,1)}, bf16[2048,768]{1,0:T(8,128)(2,1)}, bf16[2048,3072]{1,0:T(8,128)(2,1)}, bf16[2048,3072]{1,0:T(8,128)(2,1)}, f32...) custom-call(bf16[2048,768]{1,0:T(8,128)(2,1)} %x.11, bf16[2048,768]{1,0:T(8,128)(2,1)} %get-tuple-element.20.o.wn, ...), custom_call_target="tpu_custom_call" | custom-call | flops 43486543872 | bytes 62914560 | tf_op jit(solution)/shard_map/mlp_both/pallas_call | solution.py:241
  218.9 4.8 convert_element_type.51.dz
  223.7 6.5 %attn_out_grad.1 = bf16[768,768]{1,0:T(8,128)(2,1)} custom-call(bf16[2048,768]{1,0:T(8,128)(2,1)} %get-tuple-element.20.o.wn, bf16[2048,768]{1,0:T(8,128)(2,1)} %convert_element_type.51.dz), custom_call_target="tpu_custom_call" | custom-call | flops 2415919104 | bytes 7471104 | tf_op jit(solution)/shard_map/attn_out_grad/pallas_call | solution.py:261
  230.5 23.4 %attention_backward.1.dqkv = bf16[2048,2304]{1,0:T(8,128)(2,1)} custom-call(bf16[2048,2304]{1,0:T(8,128)(2,1)} %get-tuple-element.22.qkv, bf16[16,6,128,256]{3,2,1,0:T(8,128)(2,1)} %get-tuple-element.23.probs, bf16[2048,768]{1,0:T(8,128)(2,1)} %get-tuple-element.24.do), custom_call_target="tpu_custom_call" | custom-call | flops 9663676416 | bytes 31457280 | tf_op jit(solution)/shard_map/attention_backward/pallas_call | solution.py:267
  253.9 16.4 %input_grad.1 = (bf16[2048,768]{1,0:T(8,128)(2,1)}, f32[8,768]{1,0:T(8,128)}) custom-call(bf16[2048,768]{1,0:T(8,128)(2,1)} %x.11, bf16[2048,2304]{1,0:T(8,128)(2,1)} %attention_backward.1.dqkv, f32[2048,768]{1,0:T(8,128)} %get-tuple-element.25.dh, f32[1,768]{1,0:T(1,128)} %reshape.40.gain, bf16[768,2304]{1,0:T(8,128)(2,1)} %slice.25.w_qkv), custom_call_target="tpu_custom_call" | custom-call | flops 7247757312 | bytes 31457280 | tf_op jit(solution)/shard_map/input_grad/pallas_call | solution.py:276
  271.3 14.0 %qkv_grad.1 = bf16[768,2304]{1,0:T(8,128)(2,1)} custom-call(bf16[2048,768]{1,0:T(8,128)(2,1)} %x.11, f32[1,768]{1,0:T(1,128)} %reshape.40.gain, bf16[2048,2304]{1,0:T(8,128)(2,1)} %attention_backward.1.dqkv), custom_call_target="tpu_custom_call" | custom-call | flops 7247757312 | bytes 20971520 | tf_op jit(solution)/shard_map/qkv_grad/pallas_call | solution.py:288
  285.2 4.0 fusion.1
  289.4 14.7 %mlp_in_grad.1 = bf16[768,3072]{1,0:T(8,128)(2,1)} custom-call(bf16[2048,768]{1,0:T(8,128)(2,1)} %get-tuple-element.29.wn, bf16[2048,3072]{1,0:T(8,128)(2,1)} %get-tuple-element.30.dz), custom_call_target="tpu_custom_call" | custom-call | flops 9663676416 | bytes 20447232 | tf_op jit(solution)/shard_map/mlp_in_grad/pallas_call | solution.py:261
  304.1 14.7 %mlp_out_grad.1 = bf16[3072,768]{1,0:T(8,128)(2,1)} custom-call(bf16[2048,3072]{1,0:T(8,128)(2,1)} %get-tuple-element.31.wn, bf16[2048,768]{1,0:T(8,128)(2,1)} %dz.1), custom_call_target="tpu_custom_call" | custom-call | flops 9663676416 | bytes 20447232 | tf_op jit(solution)/shard_map/mlp_out_grad/pallas_call | solution.py:261
  318.9 19.7 %reduce-scatter.5.cloned.1.call-done = bf16[96,2432]{1,0:T(8,128)(2,1)} async-done(((bf16[768,2432]{1,0:T(8,128)(2,1)}), bf16[96,2432]{1,0:T(8,128)(2,1)}) %reduce-scatter.5.cloned.1.call-update) | async-done | bytes 466960 | tf_op jit(solution)/shard_map/reduce_scatter | solution.py:308
  338.5 57.4 %reduce-scatter.9.cloned.1.call-done = bf16[96,3072]{1,0:T(8,128)(2,1)} async-done(((bf16[768,3072]{1,0:T(8,128)(2,1)}), bf16[96,3072]{1,0:T(8,128)(2,1)}) %reduce-scatter.9.cloned.1.call-update) | async-done | bytes 589840 | tf_op jit(solution)/shard_map/reduce_scatter | solution.py:308
  395.9 57.7 %reduce-scatter.11.cloned.1.call-done = bf16[384,768]{1,0:T(8,128)(2,1)} async-done(((bf16[3072,768]{1,0:T(8,128)(2,1)}), bf16[384,768]{1,0:T(8,128)(2,1)}) %reduce-scatter.11.cloned.1.call-update) | async-done | bytes 589840 | tf_op jit(solution)/shard_map/reduce_scatter | solution.py:308
  453.7 80.3 %all-reduce.5.cloned.1.call-done = (bf16[96,2432]{1,0:T(8,128)(2,1)}, bf16[96,768]{1,0:T(8,128)(2,1)}, bf16[96,3072]{1,0:T(8,128)(2,1)}, bf16[384,768]{1,0:T(8,128)(2,1)}) async-done(((bf16[96,2432]{1,0:T(8,128)(2,1)}, bf16[96,768]{1,0:T(8,128)(2,1)}, bf16[96,3072]{1,0:T(8,128)(2,1)}, bf16[384,768]{1,0:T(8,128)(2,1)}), (bf16[96,2432]{1,0:T(8,128)(2,1)}, bf16[96,768]{1,0:T(8,128)(2,1)}, ...) | async-done | bytes 1794064 | tf_op jit(solution)/shard_map/psum | solution.py:317
  534.0 2.1 slice.28
  537.1 1.6 convert_element_type.52
  539.5 1.1 convert_element_type.53
  (39 shorter events, 8.4 us)
Async XLA Ops:
  7.2 40.8 %all-gather.5.cloned.1.call-start = ((), (), s32[]{:S(2)}) async-start(), calls=%async_computation.4 | async-start | bytes 4202496 | tf_op jit(solution)/shard_map/all_gather | solution.py:300
  9.9 68.4 %all-gather.7.cloned.1.call-start = ((), (), s32[]{:S(2)}) async-start(), calls=%async_computation.5 | async-start | bytes 1327104 | tf_op jit(solution)/shard_map/all_gather | solution.py:300
  10.6 104.2 %all-gather.9.cloned.1.call-start = ((), (), s32[]{:S(2)}) async-start(), calls=%async_computation.6 | async-start | bytes 5308416 | tf_op jit(solution)/shard_map/all_gather | solution.py:300
  11.4 144.2 %all-gather.11.cloned.1.call-start = ((), (), s32[]{:S(2)}) async-start(), calls=%async_computation.7 | async-start | bytes 5308416 | tf_op jit(solution)/shard_map/all_gather | solution.py:300
  11.9 306.9 %reduce-scatter.7.cloned.1.call-start = ((), (), s32[]{:S(2)}) async-start(), calls=%async_computation.9 | async-start | bytes 1327104 | tf_op jit(solution)/shard_map/reduce_scatter | solution.py:308
  230.2 108.3 %reduce-scatter.5.cloned.1.call-start = ((), (), s32[]{:S(2)}) async-start(), calls=%async_computation.8 | async-start | bytes 4202496 | tf_op jit(solution)/shard_map/reduce_scatter | solution.py:308
  253.9 17.1 %copy-start.2 = (f32[8,768]{1,0:T(8,128)S(1)}, f32[8,768]{1,0:T(8,128)}, u32[]{:S(2)}) copy-start(f32[8,768]{1,0:T(8,128)} %get-tuple-element.28) | copy-start | bytes 73732
  289.3 106.6 %reduce-scatter.9.cloned.1.call-start = ((), (), s32[]{:S(2)}) async-start(), calls=%async_computation.10 | async-start | bytes 5308416 | tf_op jit(solution)/shard_map/reduce_scatter | solution.py:308
  304.1 149.6 %reduce-scatter.11.cloned.1.call-start = ((), (), s32[]{:S(2)}) async-start(), calls=%async_computation.11 | async-start | bytes 5308416 | tf_op jit(solution)/shard_map/reduce_scatter | solution.py:308
  318.8 215.2 %all-reduce.5.cloned.1.call-start = ((), (), s32[]{:S(2)}) async-start(), calls=%async_computation.12 | async-start | bytes 3588096 | tf_op jit(solution)/shard_map/psum | solution.py:317
  534.0 5.5 %copy-start.1 = (bf16[96,3072]{1,0:T(8,128)(2,1)S(1)}, bf16[96,3072]{1,0:T(8,128)(2,1)}, u32[]{:S(2)}) copy-start(bf16[96,3072]{1,0:T(8,128)(2,1)} %get-tuple-element.38) | copy-start | bytes 1769476
  534.0 6.6 %copy-start = (bf16[384,768]{1,0:T(8,128)(2,1)S(1)}, bf16[384,768]{1,0:T(8,128)(2,1)}, u32[]{:S(2)}) copy-start(bf16[384,768]{1,0:T(8,128)(2,1)} %get-tuple-element.39) | copy-start | bytes 1769476
Sparse Core Ops, SparseCore 0:
  10.5 37.4 all-gather.4
  49.9 24.0 all-gather.6
  75.9 38.8 all-gather.8
  116.6 38.9 all-gather.10
  230.4 36.9 reduce-scatter.6
  289.4 49.0 reduce-scatter.4
  342.0 53.8 reduce-scatter.8
  399.8 53.8 reduce-scatter.10
  456.3 77.6 all-reduce.4

commit v2 on v1

--- a/solution.py
+++ b/solution.py
@@ -291,26 +291,278 @@
         pl.BlockSpec((D, tile), lambda i: (0, i)), sds(D, N, dtype=out), 2 * T * D * N, 20 << 20,
         scratch=[pltpu.VMEM((T, D), bf)],
     )(x, g1, dqkv)
+MESH = pl.DeviceIdType.MESH
+MESSAGES = {
+    "c0": (1, 0, None), "x0": (2, 0, None), "y0": (4, 0, None),
+    "xc": (1, 2, None), "yc": (1, 4, None), "xf": (4, 2, 0), "yf": (2, 4, 1),
+    "dA": (1, 6, 0), "dB": (1, 6, 1),
+}
+ORDER = list(MESSAGES)
+
+
+def halves(n):
+    left = (n // 256) * 128
+    return (left, n - left)
+
+
+class Gather:
+    def __init__(self, shard, full, send, recv, local, me, rep):
+        self.shard, self.full, self.send, self.recv, self.local, self.me, self.rep = shard, full, send, recv, local, me, rep
+
+    def copy(self, name):
+        k = ORDER.index(name)
+        partner, whose, part = MESSAGES[name]
+        piece = self.me ^ whose
+        src, dst = self.full.at[piece], self.full.at[piece]
+        if whose == 0:
+            src = self.shard
+        if part is not None:
+            left, right = halves(self.full.shape[2])
+            cols = pl.ds(0, left) if part == 0 else pl.ds(left, right)
+            src, dst = src.at[:, cols], dst.at[:, cols]
+        return pltpu.make_async_remote_copy(
+            src_ref=src, dst_ref=dst, send_sem=self.send.at[k], recv_sem=self.recv.at[k],
+            device_id=(self.rep, self.me ^ partner), device_id_type=MESH,
+        )
+
+    def own(self):
+        return pltpu.make_async_copy(self.shard, self.full.at[self.me], self.local)
+
+    def start(self, *names):
+        for name in names:
+            self.copy(name).start()
+
+    def arrived(self, *names):
+        for name in names:
+            self.copy(name).wait_recv()
+
+    def begin(self):
+        self.start("x0", "y0", "c0")
+        self.own().start()
+
+    def relay(self):
+        self.arrived("x0")
+        self.start("xf", "xc")
+        self.arrived("y0")
+        self.start("yf", "yc")
+
+    def last(self):
+        self.arrived("xf")
+        self.start("dA")
+        self.arrived("yf")
+        self.start("dB")
+
+    def complete(self):
+        self.own().wait()
+        self.arrived("c0", "xc", "yc", "dA", "dB")
+
+    def finish(self):
+        for name in ORDER:
+            self.copy(name).wait_send()
+
+
+class Local:
+    def __init__(self, whole_ref, full, local):
+        self.copy = pltpu.make_async_copy(whole_ref, full, local)
+
+    def begin(self):
+        self.copy.start()
+
+    def complete(self):
+        self.copy.wait()
+
+    def relay(self):
+        pass
+
+    last = finish = relay
+
+
+def flat(t):
+    return t.reshape(t.shape[0] * t.shape[1], t.shape[2])
+
+
+def kernel_one(
+    remote, lengths, x, dy, q_in, o_in, i_in, t_in,
+    qkv_out, probs_out, o_out, u_out, y_out, wn_out, a_out, dz_out, dh_out, do_out, gg_out, gains_out, gwo_out, wq_out,
+    wq, wo, wi, wt, mixed_all, gwo, gains, send, recv, local, wq_sem,
+):
+    step = pl.program_id(0)
+    tiles = pl.num_programs(0) // 2
+    D = x.shape[1]
+    refs = ((q_in, wq), (o_in, wo), (i_in, wi), (t_in, wt))
+    if remote:
+        me, rep = lax.axis_index("fsdp"), lax.axis_index("rep")
+        gq, go, gi, gt = (Gather(s, f, send.at[k], recv.at[k], local.at[k], me, rep) for k, (s, f) in enumerate(refs))
+    else:
+        gq, go, gi, gt = (Local(s, f, local.at[k]) for k, (s, f) in enumerate(refs))
+    export = pltpu.make_async_copy(wq, wq_out, wq_sem)
+
+    @pl.when(step == 0)
+    def _():
+        if remote:
+            barrier = pltpu.get_barrier_semaphore()
+            for partner in (1, 2, 4):
+                pl.semaphore_signal(barrier, inc=1, device_id=(rep, me ^ partner), device_id_type=MESH)
+            pl.semaphore_wait(barrier, 3)
+        gq.begin()
+        gq.relay()
+        go.begin()
+        gi.begin()
+        gq.last()
+        gq.complete()
+        export.start()
+        gains[...] = flat(wq[:, :, 3 * D :]).astype(f32).T[:8]
+        gains_out[...] = gains[...]
+
+    @pl.when(step == 1)
+    def _():
+        go.relay()
+
+    @pl.when(step == 3)
+    def _():
+        go.last()
+
+    @pl.when(step == 5)
+    def _():
+        gi.relay()
+        gt.begin()
+
+    @pl.when(step == 7)
+    def _():
+        gi.last()
+
+    @pl.when(step < tiles)
+    def _():
+        n, _ = moments(x[...].astype(f32))
+        u = (n * gains[0:1]).astype(bf)
+        u_out[...] = u
+        qkv_out[...] = nn(u, flat(wq[:, :, : 3 * D])).astype(bf)
+        for rr in range(TILE // SPAN):
+            rows = slice(rr * SPAN, (rr + 1) * SPAN)
+            mask = permitted(lengths, step * (TILE // SPAN) + rr)
+            probs, mixed = attend(lambda c: qkv_out[rows, c : c + 128], mask)
+            for p in range(6):
+                probs_out[rr, p] = probs[p]
+                o_out[rows, p * 128 : (p + 1) * 128] = mixed[p]
+        mixed_all[step] = o_out[...]
+
+    @pl.when(step == tiles)
+    def _():
+        go.complete()
+        gi.complete()
+        gt.relay()
+        gt.last()
+        gt.complete()
+
+    @pl.when(step >= tiles)
+    def _():
+        o = mixed_all[step - tiles]
+        h = x[...].astype(f32) + nn(o, flat(wo[...]))
+        n, r = moments(h)
+        g = gains[1:2]
+        wn = (n * g).astype(bf)
+        wn_out[...] = wn
+        dm = dy[...]
+        y = h
+        dw = None
+        per = FC // wt.shape[1]
+        for j in range(wi.shape[2] // FC):
+            cols = slice(j * FC, (j + 1) * FC)
+            w_in, w_out = flat(wi[:, :, cols]), flat(wt[j * per : (j + 1) * per])
+            a, slope = gelu_both(nn(wn, w_in))
+            a = a.astype(bf)
+            a_out[:, cols] = a
+            y = y + nn(a, w_out)
+            dz = (nt(dm, w_out) * slope).astype(bf)
+            dz_out[:, cols] = dz
+            t = nt(dz, w_in)
+            dw = t if dw is None else dw + t
+        y_out[...] = y.astype(bf)
+        dh = dm.astype(f32) + norm_back(dw, n, r, g)
+        dh_out[...] = dh
+        dt = dh.astype(bf)
+        do_out[...] = nt(dt, flat(wo[...])).astype(bf)
+        part = jnp.sum((dw * n).reshape(-1, 8, D), axis=0)
+        gw = tn(o, dt)
+
+        @pl.when(step == tiles)
+        def _():
+            gg_out[...] = part
+            gwo[...] = gw
+
+        @pl.when(step > tiles)
+        def _():
+            gg_out[...] += part
+            gwo[...] += gw
+
+    @pl.when(step == 2 * tiles - 1)
+    def _():
+        gwo_out[...] = gwo[...].astype(bf)
+        export.wait()
+        for g in (gq, go, gi, gt):
+            g.finish()
+
+
+def forward_and_mlp(remote, x, lengths, dy, packed, w_ao, w_in, w_out):
+    T, D = x.shape
+    tiles = T // TILE
+    per = TILE // SPAN
+    F = w_in.shape[-1]
+    rows = D // 8
+    early = lambda *shape: pl.BlockSpec(shape, lambda i: (jnp.minimum(i, tiles - 1),) + (0,) * (len(shape) - 1))
+    late = lambda *shape: pl.BlockSpec(shape, lambda i: (jnp.maximum(i - tiles, 0),) + (0,) * (len(shape) - 1))
+    both = lambda *shape: pl.BlockSpec(shape, lambda i: (lax.rem(i, tiles),) + (0,) * (len(shape) - 1))
+    fixed = lambda *shape: pl.BlockSpec(shape, lambda i: (0,) * len(shape))
+    hbm = pl.BlockSpec(memory_space=pl.ANY)
+    return pl.pallas_call(
+        functools.partial(kernel_one, remote),
+        name="forward_and_mlp",
+        grid=(2 * tiles,),
+        in_specs=[pl.BlockSpec(memory_space=pltpu.SMEM), both(TILE, D), late(TILE, D), hbm, hbm, hbm, hbm],
+        out_specs=[
+            early(TILE, 3 * D), early(per, 6, SPAN, 2 * SPAN), early(TILE, D), early(TILE, D),
+            late(TILE, D), late(TILE, D), late(TILE, F), late(TILE, F), late(TILE, D), late(TILE, D),
+            fixed(8, D), fixed(8, D), fixed(D, D), hbm,
+        ],
+        out_shape=[
+            sds(T, 3 * D), sds(T // SPAN, 6, SPAN, 2 * SPAN), sds(T, D), sds(T, D),
+            sds(T, D), sds(T, D), sds(T, F), sds(T, F), sds(T, D, dtype=f32), sds(T, D),
+            sds(8, D, dtype=f32), sds(8, D, dtype=f32), sds(D, D), sds(8, rows, packed.shape[-1]),
+        ],
+        scratch_shapes=[
+            pltpu.VMEM((8, rows, packed.shape[-1]), bf), pltpu.VMEM((8, rows, D), bf), pltpu.VMEM((8, rows, F), bf),
+            pltpu.VMEM((8, F // 8, D), bf), pltpu.VMEM((tiles, TILE, D), bf), pltpu.VMEM((D, D), f32), pltpu.VMEM((8, D), f32),
+            pltpu.SemaphoreType.DMA((4, len(ORDER))), pltpu.SemaphoreType.DMA((4, len(ORDER))), pltpu.SemaphoreType.DMA((4,)),
+            pltpu.SemaphoreType.DMA,
+        ],
+        cost_estimate=pl.CostEstimate(flops=12 * T * D * D + 8 * T * D * F + 6 * T * D * D, bytes_accessed=90 << 20, transcendentals=0),
+        compiler_params=pltpu.CompilerParams(
+            vmem_limit_bytes=VMEM, has_side_effects=remote, collective_id=1 if remote else None
+        ),
+    )(lengths, x, dy, packed, w_ao, w_in, w_out)
+
+
+def pack(w_qkv, gain_attn, gain_mlp):
+    gains = jnp.stack([gain_attn, gain_mlp], axis=1)
+    return jnp.concatenate([w_qkv, jnp.pad(gains, ((0, 0), (0, 126)))], axis=1)
 
 
 def shards(x, lengths, segments, gain_attn, w_qkv, w_attn_out, gain_mlp, w_mlp_in, w_mlp_out, dy):
     D = x.shape[1]
-    gains = jnp.stack([gain_attn, gain_mlp], axis=1)
-    packed = jnp.concatenate([w_qkv, jnp.pad(gains, ((0, 0), (0, 126)))], axis=1)
-    gather = lambda v: lax.all_gather(v, "fsdp", axis=0, tiled=True)
-    packed = gather(packed)
-    wq = packed[:, : 3 * D]
-    g1 = packed[:, 3 * D].astype(f32)[None]
-    g2 = packed[:, 3 * D + 1].astype(f32)[None]
-    wo, wi, wt = gather(w_attn_out), gather(w_mlp_in), gather(w_mlp_out)
-    qkv, probs, o = forward_attention(x, lengths, g1, wq)
-    y, wn, a, dz, dh, do, gg2 = mlp_both(x, o, dy, g2, wo, wi, wt)
+    remote = lax.axis_size("fsdp") == 8
+    weights = (pack(w_qkv, gain_attn, gain_mlp), w_attn_out, w_mlp_in, w_mlp_out)
+    if not remote:
+        weights = tuple(lax.all_gather(v, "fsdp", axis=0, tiled=True) for v in weights)
+        weights = tuple(v.reshape(8, v.shape[0] // 8, v.shape[1]) for v in weights)
+    qkv, probs, o, u, y, wn, a, dz, dh, do, gg2, gains, gwo, wq = forward_and_mlp(remote, x, lengths, dy, *weights)
+    g1 = gains[0:1]
+    wq = wq.reshape(D, wq.shape[2])[:, : 3 * D]
     scatter = lambda v: lax.psum_scatter(v, "fsdp", scatter_dimension=0, tiled=True)
     gwt = scatter(weight_grad(a, dy, "mlp_out_grad", 768, bf, "left"))
     gwi = scatter(weight_grad(wn, dz, "mlp_in_grad", 768))
-    gwo = scatter(weight_grad(o, dh.astype(bf), "attn_out_grad", 768))
+    gwo = scatter(gwo)
     dqkv = attention_back(qkv, probs, do)
-    gq = qkv_grad(x, g1, dqkv)
+    gq = weight_grad(u, dqkv, "qkv_grad", 768)
     dx, gg1 = input_grad(x, dqkv, dh, g1, wq)
     ends = jnp.stack([gg1.sum(0), gg2.sum(0)], axis=1).astype(bf)
     gq = scatter(jnp.concatenate([gq, jnp.pad(ends, ((0, 0), (0, 126)))], axis=1))

time: 549 us -> 478 us (0.87)
  waiting for transfers between devices: 329 us -> 217 us
  Pallas kernels: 177 us -> 220 us
    all_gather x4 -> x0, waiting for transfers between devices: 112 us -> none  [shards(): gather = lambda v: lax.all_gather(v, 'fsdp', axis=0, tiled=True)]
    pallas_call x3 -> x1, Pallas kernels: 101 us -> 139 us  [forward_and_mlp(): pl.pallas_call(functools.partial(kernel_one, remote), name='forward_and_m...]
    convert_element_type x2 -> x0, other arithmetic: 6.17 us -> none  [the longest x1 4.83 us: shards(): gwo = scatter(weight_grad(o, dh.astype(bf), 'attn_out_grad', 768))]
  transfers between devices with their start and end apart: 9 -> 5, of which waited for: 7 -> 4; matrix products, arithmetic and copies ran while one was open for 2% -> 2% of each run, Pallas kernels for 19% -> 17%
where the time goes in v2:
time: 478 us; the launch traced here: 477 us
  Pallas kernels  220 us (46%)
  waiting for transfers between devices  217 us (45%)
  other arithmetic  14.1 us (3%)
  between operations  13.8 us (3%)
  local copies, waits for them, and re-layouts  11.4 us (2%)
    pallas_call x1, Pallas kernels, forward_and_mlp(): pl.pallas_call(functools.partial(kernel_one, remote), name='forward_and_m...  139 us
    reduce_scatter x4, waiting for transfers between devices, shards(): lax.psum_scatter(v, 'fsdp', scatter_dimension=0, tiled=True)  137 us
    psum x1, waiting for transfers between devices, shards(): gwt, gwi, gwo, gq = lax.psum((gwt, gwi, gwo, gq), 'rep')  80.1 us
    pallas_call x3, Pallas kernels, weight_grad(): call(kernel_d1, name, grid, ins, outs, sds(M, N, dtype=out), 2 * T * M *...  41.2 us
    pallas_call x1, Pallas kernels, attention_back(): call(kernel_e, 'attention_backward', (T // TILE,), [rows_of(3 * D), pl.Bl...  23.5 us
    pallas_call x1, Pallas kernels, input_grad(): call(kernel_f, 'input_grad', (T // TILE,), [rows_of(D), rows_of(3 * D), r...  16.2 us
  transfers between devices with their start and end apart: 5, of which 4 were waited for; matrix products, arithmetic and copies ran while one was open for 2% of the time, Pallas kernels for 17%

profile of v2, /device:TPU:0, one launch (start us, length us, event | category | flops | bytes accessed | tf_op | source)
XLA Modules:
  0.0 476.9 jit_solution(5334976181994910347)
XLA Ops:
  7.2 1.4 copy.26.lengths
  9.4 1.8 fusion.3.q_in
  11.2 139.4 %forward_and_mlp.1 = (bf16[2048,2304]{1,0:T(8,128)(2,1)}, bf16[16,6,128,256]{3,2,1,0:T(8,128)(2,1)}, bf16[2048,768]{1,0:T(8,128)(2,1)}, bf16[2048,768]{1,0:T(8,1...) custom-call(s32[16,4]{1,0:T(8,128)} %copy.26.lengths, ...), custom_call_target="tpu_custom_call" | custom-call | flops 60397977600 | bytes 94371840 | tf_op jit(solution)/shard_map/forward_and_mlp/pallas_call | solution.py:517
  150.9 0.8 reduce_sum.19
  151.6 1.3 slice.15.gain
  152.9 4.0 slice.20.w_qkv
  156.9 23.5 %attention_backward.1.dqkv.dz = bf16[2048,2304]{1,0:T(8,128)(2,1)} custom-call(bf16[2048,2304]{1,0:T(8,128)(2,1)} %get-tuple-element.24.qkv, bf16[16,6,128,256]{3,2,1,0:T(8,128)(2,1)} %get-tuple-element.25.probs, bf16[2048,768]{1,0:T(8,128)(2,1)} %get-tuple-element.26.do), custom_call_target="tpu_custom_call" | custom-call | flops 9663676416 | bytes 31457280 | tf_op jit(solution)/shard_map/attention_backward/pallas_call | solution.py:267
  180.4 16.2 %input_grad.1 = (bf16[2048,768]{1,0:T(8,128)(2,1)}, f32[8,768]{1,0:T(8,128)}) custom-call(bf16[2048,768]{1,0:T(8,128)(2,1)} %x.7, bf16[2048,2304]{1,0:T(8,128)(2,1)} %attention_backward.1.dqkv.dz, f32[2048,768]{1,0:T(8,128)} %get-tuple-element.27.dh, f32[1,768]{1,0:T(1,128)} %slice.15.gain, bf16[768,2304]{1,0:T(8,128)(2,1)} %slice.20.w_qkv), custom_call_target="tpu_custom_call" | custom-call | flops 7247757312 | bytes 31457280 | tf_op jit(solution)/shard_map/input_grad/pallas_call | solution.py:276
  196.7 0.8 reduce_sum.18
  197.6 11.9 %qkv_grad.1 = bf16[768,2304]{1,0:T(8,128)(2,1)} custom-call(bf16[2048,768]{1,0:T(8,128)(2,1)} %get-tuple-element.31.wn, bf16[2048,2304]{1,0:T(8,128)(2,1)} %attention_backward.1.dqkv.dz), custom_call_target="tpu_custom_call" | custom-call | flops 7247757312 | bytes 16121856 | tf_op jit(solution)/shard_map/qkv_grad/pallas_call | solution.py:261
  209.6 4.1 fusion.1
  213.7 14.7 %mlp_in_grad.1 = bf16[768,3072]{1,0:T(8,128)(2,1)} custom-call(bf16[2048,768]{1,0:T(8,128)(2,1)} %get-tuple-element.35.wn, bf16[2048,3072]{1,0:T(8,128)(2,1)} %get-tuple-element.36.dz), custom_call_target="tpu_custom_call" | custom-call | flops 9663676416 | bytes 20447232 | tf_op jit(solution)/shard_map/mlp_in_grad/pallas_call | solution.py:261
  228.4 14.7 %mlp_out_grad.1 = bf16[3072,768]{1,0:T(8,128)(2,1)} custom-call(bf16[2048,3072]{1,0:T(8,128)(2,1)} %get-tuple-element.37.wn, bf16[2048,768]{1,0:T(8,128)(2,1)} %dz.1), custom_call_target="tpu_custom_call" | custom-call | flops 9663676416 | bytes 20447232 | tf_op jit(solution)/shard_map/mlp_out_grad/pallas_call | solution.py:261
  243.2 21.6 %reduce-scatter.5.cloned.1.call-done = bf16[96,2432]{1,0:T(8,128)(2,1)} async-done(((bf16[768,2432]{1,0:T(8,128)(2,1)}), bf16[96,2432]{1,0:T(8,128)(2,1)}) %reduce-scatter.5.cloned.1.call-update) | async-done | bytes 466960 | tf_op jit(solution)/shard_map/reduce_scatter | solution.py:560
  264.8 57.4 %reduce-scatter.9.cloned.1.call-done = bf16[96,3072]{1,0:T(8,128)(2,1)} async-done(((bf16[768,3072]{1,0:T(8,128)(2,1)}), bf16[96,3072]{1,0:T(8,128)(2,1)}) %reduce-scatter.9.cloned.1.call-update) | async-done | bytes 589840 | tf_op jit(solution)/shard_map/reduce_scatter | solution.py:560
  322.1 57.6 %reduce-scatter.11.cloned.1.call-done = bf16[384,768]{1,0:T(8,128)(2,1)} async-done(((bf16[3072,768]{1,0:T(8,128)(2,1)}), bf16[384,768]{1,0:T(8,128)(2,1)}) %reduce-scatter.11.cloned.1.call-update) | async-done | bytes 589840 | tf_op jit(solution)/shard_map/reduce_scatter | solution.py:560
  379.8 80.1 %all-reduce.5.cloned.1.call-done = (bf16[96,2432]{1,0:T(8,128)(2,1)}, bf16[96,768]{1,0:T(8,128)(2,1)}, bf16[96,3072]{1,0:T(8,128)(2,1)}, bf16[384,768]{1,0:T(8,128)(2,1)}) async-done(((bf16[96,2432]{1,0:T(8,128)(2,1)}, bf16[96,768]{1,0:T(8,128)(2,1)}, bf16[96,3072]{1,0:T(8,128)(2,1)}, bf16[384,768]{1,0:T(8,128)(2,1)}), (bf16[96,2432]{1,0:T(8,128)(2,1)}, bf16[96,768]{1,0:T(8,128)(2,1)}, ...) | async-done | bytes 1794064 | tf_op jit(solution)/shard_map/psum | solution.py:569
  459.9 2.0 slice.22
  462.0 1.1 convert_element_type.17
  463.0 1.6 convert_element_type.18
  464.7 0.7 slice_reduce_fusion
  465.4 2.2 convert_element_type.19
  467.6 1.1 convert_element_type.20
  468.7 1.7 copy.33
  (21 shorter events, 1.5 us)
Async XLA Ops:
  7.2 236.0 %reduce-scatter.7.cloned.1.call-start = ((), (), s32[]{:S(2)}) async-start(), calls=%async_computation.5 | async-start | bytes 1327104 | tf_op jit(solution)/shard_map/reduce_scatter | solution.py:560
  150.6 114.2 %reduce-scatter.5.cloned.1.call-start = ((), (), s32[]{:S(2)}) async-start(), calls=%async_computation.4 | async-start | bytes 4202496 | tf_op jit(solution)/shard_map/reduce_scatter | solution.py:560
  213.7 108.5 %reduce-scatter.9.cloned.1.call-start = ((), (), s32[]{:S(2)}) async-start(), calls=%async_computation.6 | async-start | bytes 5308416 | tf_op jit(solution)/shard_map/reduce_scatter | solution.py:560
  228.4 151.4 %reduce-scatter.11.cloned.1.call-start = ((), (), s32[]{:S(2)}) async-start(), calls=%async_computation.7 | async-start | bytes 5308416 | tf_op jit(solution)/shard_map/reduce_scatter | solution.py:560
  243.1 216.8 %all-reduce.5.cloned.1.call-start = ((), (), s32[]{:S(2)}) async-start(), calls=%async_computation.8 | async-start | bytes 3588096 | tf_op jit(solution)/shard_map/psum | solution.py:569
  379.8 88.9 %copy-start = (bf16[2048,768]{1,0:T(8,128)(2,1)S(1)}, bf16[2048,768]{1,0:T(8,128)(2,1)}, u32[]{:S(2)}) copy-start(bf16[2048,768]{1,0:T(8,128)(2,1)} %get-tuple-element.52) | copy-start | bytes 9437188
  459.9 7.7 %copy-start.1 = (bf16[384,768]{1,0:T(8,128)(2,1)S(1)}, bf16[384,768]{1,0:T(8,128)(2,1)}, u32[]{:S(2)}) copy-start(bf16[384,768]{1,0:T(8,128)(2,1)} %get-tuple-element.43) | copy-start | bytes 1769476
Sparse Core Ops, SparseCore 0:
  150.7 38.6 reduce-scatter.6
  213.8 50.9 reduce-scatter.4
  268.2 53.8 reduce-scatter.8
  325.8 53.8 reduce-scatter.10
  382.3 77.5 all-reduce.4

commit v3 on v2

--- a/solution.py
+++ b/solution.py
@@ -93,20 +93,6 @@
     return dq.astype(bf), dk.astype(bf), dv.astype(bf)
 
 
-def kernel_ab(lengths, x, gain, w_qkv, qkv_out, probs_out, o_out):
-    i = pl.program_id(0)
-    n, _ = moments(x[...].astype(f32))
-    u = (n * gain[...]).astype(bf)
-    qkv_out[...] = nn(u, w_qkv[...]).astype(bf)
-    for rr in range(TILE // SPAN):
-        rows = slice(rr * SPAN, (rr + 1) * SPAN)
-        mask = permitted(lengths, i * (TILE // SPAN) + rr)
-        probs, mixed = attend(lambda c: qkv_out[rows, c : c + 128], mask)
-        for p in range(6):
-            probs_out[rr, p] = probs[p]
-            o_out[rows, p * 128 : (p + 1) * 128] = mixed[p]
-
-
 def gelu_both(t):
     t2 = t * t
     th = jnp.tanh(t * (GC + (GC * GK) * t2))
@@ -117,41 +103,6 @@
 
 
 FC = 768
-
-
-def kernel_c(x, o, dy, gain, w_ao, w_in, w_out, y_out, wn_out, a_out, dz_out, dh_out, do_out, gg_out):
-    i = pl.program_id(0)
-    h = x[...].astype(f32) + nn(o[...], w_ao[...])
-    n, r = moments(h)
-    g = gain[...]
-    wn = (n * g).astype(bf)
-    wn_out[...] = wn
-    dm = dy[...]
-    y = h
-    dw = None
-    for j in range(w_in.shape[1] // FC):
-        cols = slice(j * FC, (j + 1) * FC)
-        a, slope = gelu_both(nn(wn, w_in[:, cols]))
-        a = a.astype(bf)
-        a_out[:, cols] = a
-        y = y + nn(a, w_out[cols, :])
-        dz = (nt(dm, w_out[cols, :]) * slope).astype(bf)
-        dz_out[:, cols] = dz
-        t = nt(dz, w_in[:, cols])
-        dw = t if dw is None else dw + t
-    y_out[...] = y.astype(bf)
-    dh = dm.astype(f32) + norm_back(dw, n, r, g)
-    dh_out[...] = dh
-    do_out[...] = nt(dh.astype(bf), w_ao[...]).astype(bf)
-    part = jnp.sum((dw * n).reshape(-1, 8, dw.shape[1]), axis=0)
-
-    @pl.when(i == 0)
-    def _():
-        gg_out[...] = part
-
-    @pl.when(i > 0)
-    def _():
-        gg_out[...] += part
 
 
 def kernel_d1(wn, dz, g):
@@ -169,31 +120,10 @@
             dqkv[rows, 1536 + p * 128 : 1536 + p * 128 + 128] = dv
 
 
-def kernel_f(x, dqkv, dh, gain, w_qkv, dx_out, gg_out):
-    i = pl.program_id(0)
+def kernel_f(x, dqkv, dh, gain, w_qkv, dx_out):
     n, r = moments(x[...].astype(f32))
     du = nt(dqkv[...], w_qkv[...])
     dx_out[...] = (dh[...] + norm_back(du, n, r, gain[...])).astype(bf)
-    part = jnp.sum((du * n).reshape(-1, 8, du.shape[1]), axis=0)
-
-    @pl.when(i == 0)
-    def _():
-        gg_out[...] = part
-
-    @pl.when(i > 0)
-    def _():
-        gg_out[...] += part
-
-
-def kernel_gq(x, gain, dqkv, g, u):
-    @pl.when(pl.program_id(0) == 0)
-    def _():
-        for t in range(x.shape[0] // TILE):
-            rows = slice(t * TILE, (t + 1) * TILE)
-            n, _ = moments(x[rows].astype(f32))
-            u[rows] = (n * gain[...]).astype(bf)
-
-    g[...] = tn(u[...], dqkv[...]).astype(g.dtype)
 
 
 def whole(shape):
@@ -222,31 +152,6 @@
     return jax.ShapeDtypeStruct(shape, dtype)
 
 
-def forward_attention(x, lengths, g1, w_qkv):
-    T, D = x.shape
-    rows = T // SPAN
-    per = TILE // SPAN
-    return call(
-        kernel_ab, "attention_forward", (T // TILE,),
-        [pl.BlockSpec(memory_space=pltpu.SMEM), rows_of(D), whole((1, D)), whole(w_qkv.shape)],
-        [rows_of(3 * D), pl.BlockSpec((per, 6, SPAN, 2 * SPAN), lambda i: (i, 0, 0, 0)), rows_of(D)],
-        [sds(T, 3 * D), sds(rows, 6, SPAN, 2 * SPAN), sds(T, D)],
-        12 * T * D * D, 30 << 20,
-    )(lengths, x, g1, w_qkv)
-
-
-def mlp_both(x, o, dy, g2, w_ao, w_in, w_out):
-    T, D = x.shape
-    F = w_in.shape[1]
-    return call(
-        kernel_c, "mlp_both", (T // TILE,),
-        [rows_of(D), rows_of(D), rows_of(D), whole((1, D)), whole(w_ao.shape), whole(w_in.shape), whole(w_out.shape)],
-        [rows_of(D), rows_of(D), rows_of(F), rows_of(F), rows_of(D), rows_of(D), pl.BlockSpec((8, D), lambda i: (0, 0))],
-        [sds(T, D), sds(T, D), sds(T, F), sds(T, F), sds(T, D, dtype=f32), sds(T, D), sds(8, D, dtype=f32)],
-        8 * T * D * F + 4 * T * D * D, 60 << 20,
-    )(x, o, dy, g2, w_ao, w_in, w_out)
-
-
 def weight_grad(left, right, name, tile, out=bf, by="right"):
     T, M = left.shape
     N = right.shape[1]
@@ -276,21 +181,11 @@
     return call(
         kernel_f, "input_grad", (T // TILE,),
         [rows_of(D), rows_of(3 * D), rows_of(D), whole((1, D)), whole(w_qkv.shape)],
-        [rows_of(D), pl.BlockSpec((8, D), lambda i: (0, 0))],
-        [sds(T, D), sds(8, D, dtype=f32)],
+        rows_of(D), sds(T, D),
         6 * T * D * D, 30 << 20,
     )(x, dqkv, dh, g1, w_qkv)
 
 
-def qkv_grad(x, g1, dqkv, tile=768, out=bf):
-    T, D = x.shape
-    N = dqkv.shape[1]
-    return call(
-        kernel_gq, "qkv_grad", (N // tile,),
-        [whole((T, D)), whole((1, D)), pl.BlockSpec((T, tile), lambda i: (0, i))],
-        pl.BlockSpec((D, tile), lambda i: (0, i)), sds(D, N, dtype=out), 2 * T * D * N, 20 << 20,
-        scratch=[pltpu.VMEM((T, D), bf)],
-    )(x, g1, dqkv)
 MESH = pl.DeviceIdType.MESH
 MESSAGES = {
     "c0": (1, 0, None), "x0": (2, 0, None), "y0": (4, 0, None),
@@ -383,7 +278,7 @@
 
 def kernel_one(
     remote, lengths, x, dy, q_in, o_in, i_in, t_in,
-    qkv_out, probs_out, o_out, u_out, y_out, wn_out, a_out, dz_out, dh_out, do_out, gg_out, gains_out, gwo_out, wq_out,
+    qkv_out, probs_out, o_out, u_out, y_out, wn_out, za_out, dh_out, do_out, gains_out, gwo_out, wq_out,
     wq, wo, wi, wt, mixed_all, gwo, gains, send, recv, local, wq_sem,
 ):
     step = pl.program_id(0)
@@ -471,10 +366,10 @@
             w_in, w_out = flat(wi[:, :, cols]), flat(wt[j * per : (j + 1) * per])
             a, slope = gelu_both(nn(wn, w_in))
             a = a.astype(bf)
-            a_out[:, cols] = a
+            za_out[1, :, cols] = a
             y = y + nn(a, w_out)
             dz = (nt(dm, w_out) * slope).astype(bf)
-            dz_out[:, cols] = dz
+            za_out[0, :, cols] = dz
             t = nt(dz, w_in)
             dw = t if dw is None else dw + t
         y_out[...] = y.astype(bf)
@@ -482,17 +377,14 @@
         dh_out[...] = dh
         dt = dh.astype(bf)
         do_out[...] = nt(dt, flat(wo[...])).astype(bf)
-        part = jnp.sum((dw * n).reshape(-1, 8, D), axis=0)
         gw = tn(o, dt)
 
         @pl.when(step == tiles)
         def _():
-            gg_out[...] = part
             gwo[...] = gw
 
         @pl.when(step > tiles)
         def _():
-            gg_out[...] += part
             gwo[...] += gw
 
     @pl.when(step == 2 * tiles - 1)
@@ -521,13 +413,12 @@
         in_specs=[pl.BlockSpec(memory_space=pltpu.SMEM), both(TILE, D), late(TILE, D), hbm, hbm, hbm, hbm],
         out_specs=[
             early(TILE, 3 * D), early(per, 6, SPAN, 2 * SPAN), early(TILE, D), early(TILE, D),
-            late(TILE, D), late(TILE, D), late(TILE, F), late(TILE, F), late(TILE, D), late(TILE, D),
-            fixed(8, D), fixed(8, D), fixed(D, D), hbm,
+            late(TILE, D), late(TILE, D), pl.BlockSpec((2, TILE, F), lambda i: (0, jnp.maximum(i - tiles, 0), 0)),
+            late(TILE, D), late(TILE, D), fixed(8, D), fixed(D, D), hbm,
         ],
         out_shape=[
             sds(T, 3 * D), sds(T // SPAN, 6, SPAN, 2 * SPAN), sds(T, D), sds(T, D),
-            sds(T, D), sds(T, D), sds(T, F), sds(T, F), sds(T, D, dtype=f32), sds(T, D),
-            sds(8, D, dtype=f32), sds(8, D, dtype=f32), sds(D, D), sds(8, rows, packed.shape[-1]),
+            sds(T, D), sds(T, D), sds(2, T, F), sds(T, D, dtype=f32), sds(T, D), sds(8, D, dtype=f32), sds(D, D), sds(8, rows, packed.shape[-1]),
         ],
         scratch_shapes=[
             pltpu.VMEM((8, rows, packed.shape[-1]), bf), pltpu.VMEM((8, rows, D), bf), pltpu.VMEM((8, rows, F), bf),
@@ -547,28 +438,292 @@
     return jnp.concatenate([w_qkv, jnp.pad(gains, ((0, 0), (0, 126)))], axis=1)
 
 
+CHUNK = 96
+WIDE = 768
+RING = 6
+N_CHUNKS = 12
+SLAB = 16
+
+
+def add_rows(pairs):
+    for target, other in pairs:
+        def slab(k, carry, target=target, other=other):
+            rows = pl.ds(pl.multiple_of(k * SLAB, SLAB), SLAB)
+            target[rows, :] = (target[rows, :].astype(f32) + other[rows, :].astype(f32)).astype(bf)
+            return carry
+
+        lax.fori_loop(0, target.shape[0] // SLAB, slab, 0)
+
+
+class Reduce:
+    def __init__(self, k, grads, bufs, send, recv, place):
+        self.k, self.g = k, grads
+        self.first, self.x2, self.y2, self.y3, self.x3, self.half, self.quarter, self.out = bufs
+        self.send, self.recv = send, recv
+        self.y, self.x, self.c, self.me, self.rep = place
+
+    def copy(self, m):
+        k, g, y, x, c, rep = self.k, self.g, self.y, self.x, self.c, self.rep
+        mid = WIDE // 2
+        left, right = pl.ds(0, mid), pl.ds(mid, mid)
+        own = g.at[y, x, c]
+        low, high = rep % 2, rep // 2
+        half = CHUNK // 2
+        keep = pl.ds(pl.multiple_of(low * half, half), half)
+        give = pl.ds(pl.multiple_of((1 - low) * half, half), half)
+        keep_cols = pl.ds(pl.multiple_of(high * mid, mid), mid)
+        give_cols = pl.ds(pl.multiple_of((1 - high) * mid, mid), mid)
+        src, dst, rep_to, me_to = {
+            "s1": lambda: (g.at[:, :, 1 - c], self.first.at[k % RING], 0, 1),
+            "s2x": lambda: (g.at[:, 1 - x, c, :, left], self.x2.at[k % RING], 0, 2),
+            "s2y": lambda: (g.at[1 - y, :, c, :, right], self.y2.at[k % RING], 0, 4),
+            "s3y": lambda: (g.at[1 - y, x, c, :, left], self.y3.at[k], 0, 4),
+            "s3x": lambda: (g.at[y, 1 - x, c, :, right], self.x3.at[k], 0, 2),
+            "z1": lambda: (own.at[give], self.half.at[k], 1, 0),
+            "z2": lambda: (own.at[keep, give_cols], self.quarter.at[k], 2, 0),
+            "z3": lambda: (self.out.at[k, keep, keep_cols], self.out.at[k, keep, keep_cols], 2, 0),
+            "z4": lambda: (self.out.at[k, keep], self.out.at[k, keep], 1, 0),
+        }[m]()
+        n = REDUCE.index(m)
+        return pltpu.make_async_remote_copy(
+            src_ref=src, dst_ref=dst, send_sem=self.send.at[k, n], recv_sem=self.recv.at[k, n],
+            device_id=(rep ^ rep_to, self.me ^ me_to), device_id_type=MESH,
+        )
+
+    def start(self, *names):
+        for m in names:
+            self.copy(m).start()
+
+    def arrived(self, *names):
+        for m in names:
+            self.copy(m).wait_recv()
+
+    def stage(self, n):
+        k, g, y, x, c = self.k, self.g, self.y, self.x, self.c
+        mid = WIDE // 2
+        left, right = pl.ds(0, mid), pl.ds(mid, mid)
+        low, high = self.rep % 2, self.rep // 2
+        half = CHUNK // 2
+        keep = pl.ds(pl.multiple_of(low * half, half), half)
+        keep_cols = pl.ds(pl.multiple_of(high * mid, mid), mid)
+        if n == 1:
+            self.start("s1")
+        elif n == 2:
+            self.arrived("s1")
+            add_rows([(g.at[b, a, c], self.first.at[k % RING, b, a]) for b in range(2) for a in range(2)])
+            self.start("s2x", "s2y")
+        elif n == 3:
+            self.arrived("s2x", "s2y")
+            add_rows([(g.at[b, x, c, :, left], self.x2.at[k % RING, b]) for b in range(2)])
+            add_rows([(g.at[y, a, c, :, right], self.y2.at[k % RING, a]) for a in range(2)])
+            self.start("s3y", "s3x")
+        elif n == 4:
+            self.arrived("s3y", "s3x")
+            add_rows([(g.at[y, x, c, :, left], self.y3.at[k]), (g.at[y, x, c, :, right], self.x3.at[k])])
+            self.start("z1")
+        elif n == 5:
+            self.arrived("z1")
+            add_rows([(g.at[y, x, c, keep], self.half.at[k])])
+            self.start("z2")
+        elif n == 6:
+            self.arrived("z2")
+            own = g.at[y, x, c, keep, keep_cols]
+            self.out[k, keep, keep_cols] = (own[...].astype(f32) + self.quarter[k].astype(f32)).astype(bf)
+            self.start("z3")
+        elif n == 7:
+            self.arrived("z3")
+            self.start("z4")
+        elif n == 8:
+            self.arrived("z4")
+
+    def sent(self):
+        for m in REDUCE:
+            self.copy(m).wait_send()
+
+
+REDUCE = ["s1", "s2x", "s2y", "s3y", "s3x", "z1", "z2", "z3", "z4"]
+P_IN, P_OUT, P_ATT, P_QKV = 0, 4, 8, 16
+P_DX = 19
+SLOT = [0, 1, 2, 3, 4, 5, 6, 7, 8, 0, 1, 2]
+FIRST = [0, 1, 2, 4, 5, 8, 9, 11, 13, 17, 18, 19]
+GAPS = [0, 1, 3, 5, 6, 7, 8, 9]
+
+
+def schedule():
+    acts = {}
+    for k in range(N_CHUNKS):
+        for n, gap in enumerate(GAPS):
+            acts.setdefault(FIRST[k] + gap, []).append((k, n + 1))
+    return acts
+
+
+def kernel_two(
+    gwo_in, wn, dm, u, wq, gains, za, qkv, probs, do, x, dh,
+    dx_out, out_hbm,
+    out, big_a, big_b, wq_s, dqkv, grads, first, x2, y2, y3, x3, half, quarter, send, recv, local,
+):
+    step = pl.program_id(0)
+    T, D = big_a.shape
+    steps = P_DX + T // TILE
+    me, rep = lax.axis_index("fsdp"), lax.axis_index("rep")
+    place = (me // 4, (me // 2) % 2, me % 2, me, rep)
+    bufs = (first, x2, y2, y3, x3, half, quarter, out)
+    chunks = [Reduce(k, grads.at[SLOT[k]], bufs, send, recv, place) for k in range(N_CHUNKS)]
+    load_gwo = pltpu.make_async_copy(gwo_in, grads.at[0], local.at[0])
+    load_wn = pltpu.make_async_copy(wn, big_a, local.at[1])
+    load_dm = pltpu.make_async_copy(dm, big_b, local.at[2])
+    load_u = pltpu.make_async_copy(u, big_a, local.at[3])
+    load_wq = pltpu.make_async_copy(wq, wq_s, local.at[4])
+    store_out = pltpu.make_async_copy(out, out_hbm, local.at[5])
+
+    @pl.when(step == 0)
+    def _():
+        load_wn.start()
+        load_gwo.start()
+        load_dm.start()
+        load_wq.start()
+        barrier = pltpu.get_barrier_semaphore()
+        for to in ((rep, me ^ 1), (rep, me ^ 2), (rep, me ^ 4), (rep ^ 1, me), (rep ^ 2, me)):
+            pl.semaphore_signal(barrier, inc=1, device_id=to, device_id_type=MESH)
+        pl.semaphore_wait(barrier, 5)
+        load_gwo.wait()
+
+    acts = schedule()
+    for at in range(steps):
+        if at in acts:
+            @pl.when(step == at)
+            def _(at=at):
+                for k, n in sorted(acts[at], key=lambda kn: -kn[1]):
+                    chunks[k].stage(n)
+
+    @pl.when(step == 0)
+    def _():
+        load_wn.wait()
+
+    @pl.when(step < P_OUT)
+    def _():
+        g = tn(big_a[...], za[0]).astype(bf)
+        grads[1 + step] = g.reshape(2, 2, 2, CHUNK, WIDE)
+
+    @pl.when(step == P_OUT)
+    def _():
+        load_u.start()
+        load_dm.wait()
+
+    @pl.when((step >= P_OUT) & (step < P_ATT))
+    def _():
+        j = step - P_OUT
+        g = tn(za[0], big_b[...]).astype(bf).reshape(2, 4, CHUNK, WIDE)
+        for part in range(4):
+            grads[5 + part, j // 2, j % 2] = g[:, part]
+
+    @pl.when((step >= P_ATT) & (step < P_QKV))
+    def _():
+        t = step - P_ATT
+        for rr in range(TILE // SPAN):
+            rows = slice(rr * SPAN, (rr + 1) * SPAN)
+            for p in range(6):
+                cols = slice(p * 128, (p + 1) * 128)
+                back = attend_back(lambda c: qkv[rows, c : c + 128], probs[rr, p], do[rows, cols], p)
+                for j in range(3):
+                    dqkv[j, t, rows, cols] = back[j]
+
+    @pl.when(step == P_QKV)
+    def _():
+        load_u.wait()
+        load_wq.wait()
+        for k in range(3):
+            chunks[k].sent()
+
+    @pl.when((step >= P_QKV) & (step < P_DX))
+    def _():
+        j = step - P_QKV
+        g = tn(big_a[...], dqkv[j].reshape(T, D)).astype(bf)
+        grads[j] = g.reshape(2, 2, 2, CHUNK, WIDE)
+
+    @pl.when(step >= P_DX)
+    def _():
+        t = step - P_DX
+        n, r = moments(x[...].astype(f32))
+        du = nt(jnp.concatenate([dqkv[j, t] for j in range(3)], axis=1), flat(wq_s[:, :, : 3 * D]))
+        dx_out[...] = (dh[...] + norm_back(du, n, r, gains[0:1])).astype(bf)
+
+    @pl.when(step == steps - 1)
+    def _():
+        for at in sorted(acts):
+            if at >= steps:
+                for k, n in sorted(acts[at], key=lambda kn: -kn[1]):
+                    chunks[k].stage(n)
+        for k in range(3, N_CHUNKS):
+            chunks[k].sent()
+        store_out.start()
+        store_out.wait()
+
+
+def gradients(gwo, wn, dy, u, wq, gains, za, qkv, probs, do, x, dh):
+    T, D = x.shape
+    tiles = T // TILE
+    per = TILE // SPAN
+    steps = P_DX + tiles
+    hbm = pl.BlockSpec(memory_space=pl.ANY)
+
+    def tile_from(start, *shape):
+        return pl.BlockSpec(shape, lambda i: (jnp.clip(i - start, 0, tiles - 1),) + (0,) * (len(shape) - 1))
+
+    return pl.pallas_call(
+        kernel_two,
+        name="gradients",
+        grid=(steps,),
+        in_specs=[
+            hbm, hbm, hbm, hbm, hbm, pl.BlockSpec((8, D), lambda i: (0, 0)),
+            pl.BlockSpec((1, T, WIDE), lambda i: (jnp.where(i < P_OUT, 0, 1), 0, jnp.where(i < P_OUT, i, jnp.minimum(i - P_OUT, 3)))),
+            tile_from(P_ATT, TILE, 3 * D), tile_from(P_ATT, per, 6, SPAN, 2 * SPAN), tile_from(P_ATT, TILE, D),
+            tile_from(P_DX, TILE, D), tile_from(P_DX, TILE, D),
+        ],
+        out_specs=[tile_from(P_DX, TILE, D), hbm],
+        out_shape=[sds(T, D), sds(N_CHUNKS, CHUNK, WIDE)],
+        scratch_shapes=[
+            pltpu.VMEM((N_CHUNKS, CHUNK, WIDE), bf),
+            pltpu.VMEM((T, D), bf), pltpu.VMEM((T, D), bf), pltpu.VMEM(wq.shape, bf), pltpu.VMEM((3, tiles, TILE, D), bf),
+            pltpu.VMEM((9, 2, 2, 2, CHUNK, WIDE), bf), pltpu.VMEM((RING, 2, 2, CHUNK, WIDE), bf),
+            pltpu.VMEM((RING, 2, CHUNK, WIDE // 2), bf), pltpu.VMEM((RING, 2, CHUNK, WIDE // 2), bf),
+            pltpu.VMEM((N_CHUNKS, CHUNK, WIDE // 2), bf), pltpu.VMEM((N_CHUNKS, CHUNK, WIDE // 2), bf),
+            pltpu.VMEM((N_CHUNKS, CHUNK // 2, WIDE), bf), pltpu.VMEM((N_CHUNKS, CHUNK // 2, WIDE // 2), bf),
+            pltpu.SemaphoreType.DMA((N_CHUNKS, len(REDUCE))), pltpu.SemaphoreType.DMA((N_CHUNKS, len(REDUCE))),
+            pltpu.SemaphoreType.DMA((6,)),
+        ],
+        cost_estimate=pl.CostEstimate(flops=8 * T * D * D + 4 * T * D * 4 * D + 20 * T * D * D, bytes_accessed=90 << 20, transcendentals=0),
+        compiler_params=pltpu.CompilerParams(vmem_limit_bytes=VMEM, has_side_effects=True, collective_id=2),
+    )(gwo.reshape(2, 2, 2, CHUNK, WIDE), wn, dy, u, wq, gains, za, qkv, probs, do, x, dh)
+
+
 def shards(x, lengths, segments, gain_attn, w_qkv, w_attn_out, gain_mlp, w_mlp_in, w_mlp_out, dy):
     D = x.shape[1]
-    remote = lax.axis_size("fsdp") == 8
+    remote = lax.axis_size("fsdp") == 8 and lax.axis_size("rep") == 4
     weights = (pack(w_qkv, gain_attn, gain_mlp), w_attn_out, w_mlp_in, w_mlp_out)
     if not remote:
         weights = tuple(lax.all_gather(v, "fsdp", axis=0, tiled=True) for v in weights)
         weights = tuple(v.reshape(8, v.shape[0] // 8, v.shape[1]) for v in weights)
-    qkv, probs, o, u, y, wn, a, dz, dh, do, gg2, gains, gwo, wq = forward_and_mlp(remote, x, lengths, dy, *weights)
-    g1 = gains[0:1]
-    wq = wq.reshape(D, wq.shape[2])[:, : 3 * D]
-    scatter = lambda v: lax.psum_scatter(v, "fsdp", scatter_dimension=0, tiled=True)
-    gwt = scatter(weight_grad(a, dy, "mlp_out_grad", 768, bf, "left"))
-    gwi = scatter(weight_grad(wn, dz, "mlp_in_grad", 768))
-    gwo = scatter(gwo)
-    dqkv = attention_back(qkv, probs, do)
-    gq = weight_grad(u, dqkv, "qkv_grad", 768)
-    dx, gg1 = input_grad(x, dqkv, dh, g1, wq)
-    ends = jnp.stack([gg1.sum(0), gg2.sum(0)], axis=1).astype(bf)
-    gq = scatter(jnp.concatenate([gq, jnp.pad(ends, ((0, 0), (0, 126)))], axis=1))
-    gwt, gwi, gwo, gq = lax.psum((gwt, gwi, gwo, gq), "rep")
-    gwt, gwi, gwo, gq = (v.astype(f32) for v in (gwt, gwi, gwo, gq))
-    return y, dx, gq[:, 3 * D], gq[:, : 3 * D], gwo, gq[:, 3 * D + 1], gwi, gwt
+    qkv, probs, o, u, y, wn, za, dh, do, gains, gwo, wq = forward_and_mlp(remote, x, lengths, dy, *weights)
+    if remote:
+        dx, sums = gradients(gwo, wn, dy, u, wq, gains, za, qkv, probs, do, x, dh)
+        sums = sums.astype(f32)
+        wide = lambda v: v.transpose(1, 0, 2).reshape(v.shape[1], -1)
+        gwo, gwi, gwt, gq = sums[0], wide(sums[1:5]), sums[5:9].reshape(-1, D), wide(sums[9:12])
+    else:
+        g1 = gains[0:1]
+        scatter = lambda v: lax.psum_scatter(v, "fsdp", scatter_dimension=0, tiled=True)
+        gwt = scatter(weight_grad(za[1], dy, "mlp_out_grad", 768, bf, "left"))
+        gwi = scatter(weight_grad(wn, za[0], "mlp_in_grad", 768))
+        gwo = scatter(gwo)
+        dqkv = attention_back(qkv, probs, do)
+        gq = scatter(weight_grad(u, dqkv, "qkv_grad", 768))
+        dx = input_grad(x, dqkv, dh, g1, wq.reshape(D, wq.shape[2])[:, : 3 * D])
+        gwt, gwi, gwo, gq = lax.psum((gwt, gwi, gwo, gq), "rep")
+        gwt, gwi, gwo, gq = (v.astype(f32) for v in (gwt, gwi, gwo, gq))
+    gg1 = jnp.sum(w_qkv.astype(f32) * gq, axis=1) / gain_attn.astype(f32)
+    gg2 = jnp.sum(w_mlp_in.astype(f32) * gwi, axis=1) / gain_mlp.astype(f32)
+    return y, dx, gg1, gq, gwo, gg2, gwi, gwt
 
 
 def solution(mesh):

time: 478 us -> 280 us (0.59)
  waiting for transfers between devices: 217 us -> 0 us
  Pallas kernels: 220 us -> 264 us
  between operations: 13.8 us -> 0.77 us
  other arithmetic: 14.1 us -> 3.8 us
    reduce_scatter x4 -> x0, waiting for transfers between devices: 137 us -> none  [shards(): lax.psum_scatter(v, 'fsdp', scatter_dimension=0, tiled=True)]
    psum x1 -> x0, waiting for transfers between devices: 80.1 us -> none  [shards(): gwt, gwi, gwo, gq = lax.psum((gwt, gwi, gwo, gq), 'rep')]
    pallas_call x5 -> x1, Pallas kernels: 81 us -> 125 us  [gradients(): pl.pallas_call(kernel_two, name='gradients', grid=(steps,), in_specs=[hbm...]
    slice x4 -> x1, local copies, waits for them, and re-layouts: 8.05 us -> 2.3 us  [shards(): sums[5:9].reshape(-1, D)]
    convert_element_type x4 -> x1, other arithmetic: 5.99 us -> 0.32 us  [shards(): sums = sums.astype(f32)]
    unnamed x6 -> x23, local copies, waits for them, and re-layouts: 3.03 us -> 7.9 us
  transfers between devices with their start and end apart: 5 -> 0, of which waited for: 4 -> 0; matrix products, arithmetic and copies ran while one was open for 2% -> 0% of each run, Pallas kernels for 17% -> 0%
where the time goes in v3:
time: 280 us
  Pallas kernels  264 us (94%)
  local copies, waits for them, and re-layouts  11.2 us (4%)
  other arithmetic  3.8 us (1%)
    pallas_call x1, Pallas kernels, forward_and_mlp(): pl.pallas_call(functools.partial(kernel_one, remote), name='forward_and_m...  139 us
    pallas_call x1, Pallas kernels, gradients(): pl.pallas_call(kernel_two, name='gradients', grid=(steps,), in_specs=[hbm...  125 us
    unnamed x23, local copies, waits for them, and re-layouts  7.9 us

profile of v3, /device:TPU:0, one launch (start us, length us, event | category | flops | bytes accessed | tf_op | source)
XLA Modules:
  0.0 280.1 jit_solution(11191078162965884684)
XLA Ops:
  0.6 0.7 pad_maximum_fusion
  1.3 1.4 copy.26.lengths
  2.7 0.1 copy.25
  2.8 1.8 fusion.1.q_in
  4.6 139.0 %forward_and_mlp.1 = (bf16[2048,2304]{1,0:T(8,128)(2,1)}, bf16[16,6,128,256]{3,2,1,0:T(8,128)(2,1)}, bf16[2048,768]{1,0:T(8,128)(2,1)}, bf16[2048,768]{1,0:T(8,1...) custom-call(s32[16,4]{1,0:T(8,128)} %copy.26.lengths, ...), custom_call_target="tpu_custom_call" | custom-call | flops 60397977600 | bytes 94371840 | tf_op jit(solution)/shard_map/forward_and_mlp/pallas_call | solution.py:409
  143.7 125.2 %gradients.1 = (bf16[2048,768]{1,0:T(8,128)(2,1)}, bf16[12,96,768]{2,1,0:T(8,128)(2,1)}) custom-call(bf16[2,2,2,96,768]{4,3,2,1,0:T(8,128)(2,1)} %bitcast.21, bf16[2048,768]{1,0:T(8,128)(2,1)} %get-tuple-element.23.wn, bf16[2048,768]{1,0:T(8,128)(2,1)} %dm.1, bf16[2048,768]{1,0:T(8,128)(2,1)} %get-tuple-element.24.u, ...), custom_call_target="tpu_custom_call" | custom-call | flops 53150220288 | bytes 94371840 | tf_op jit(solution)/shard_map/gradients/pallas_call | solution.py:673
  268.9 2.3 slice.19
  271.2 0.3 convert_element_type.18
  271.5 0.7 slice_bitcast_fusion.2
  272.3 0.1 slice_bitcast_fusion.1
  272.3 0.0 copy-start.5
  272.4 0.1 slice_bitcast_fusion
  272.5 0.1 copy.30
  272.6 0.0 copy-start.1
  272.6 0.1 copy.29
  272.7 0.7 copy-done.5
  273.4 0.2 multiply_reduce_fusion.1
  273.6 0.1 copy-done.6
  273.6 0.2 multiply_reduce_fusion
  273.9 0.5 convert_divide_fusion
  274.4 1.0 copy-done.3
  275.4 1.7 copy.33
  277.0 1.4 copy-done.4
  278.4 1.7 copy.34
  (12 shorter events, 0.0 us)
Async XLA Ops:
  268.9 2.3 copy-start
  272.3 1.0 copy-start.5
  272.5 1.2 copy-start.6
  272.5 1.4 copy-start.7
  272.5 1.4 copy-start.8
  272.5 2.9 %copy-start.3 = (bf16[2048,768]{1,0:T(8,128)(2,1)S(1)}, bf16[2048,768]{1,0:T(8,128)(2,1)}, u32[]{:S(2)}) copy-start(bf16[2048,768]{1,0:T(8,128)(2,1)} %get-tuple-element.44) | copy-start | bytes 9437188
  272.6 4.4 %copy-start.1 = (f32[4,12,8,768]{3,2,0,1:T(8,128)}, f32[4,12,8,768]{3,2,0,1:T(8,128)S(1)}, u32[]{:S(2)}) copy-start(f32[4,12,8,768]{3,2,0,1:T(8,128)S(1)} %copy.30) | copy-start | bytes 3538948
  272.7 4.3 %copy-start.2 = (f32[3,12,8,768]{3,2,0,1:T(8,128)}, f32[3,12,8,768]{3,2,0,1:T(8,128)S(1)}, u32[]{:S(2)}) copy-start(f32[3,12,8,768]{3,2,0,1:T(8,128)S(1)} %copy.29) | copy-start | bytes 2654212
  275.4 3.0 %copy-start.4 = (bf16[2048,768]{1,0:T(8,128)(2,1)S(1)}, bf16[2048,768]{1,0:T(8,128)(2,1)}, u32[]{:S(2)}) copy-start(bf16[2048,768]{1,0:T(8,128)(2,1)} %get-tuple-element.45) | copy-start | bytes 9437188

commit v4 on v1

v4 whole, which is shorter than its diff:
```python
import functools, math
import jax, jax.numpy as jnp
from jax import lax
from jax.experimental import pallas as pl
from jax.experimental.pallas import tpu as pltpu
from jax.sharding import PartitionSpec as P
bf = jnp.bfloat16
f32 = jnp.float32
EPS = 1e-05
NEG = -1e30
SPAN = 128
TILE = 256
VMEM = 63 * 1024 * 1024
SCALE = 64 ** -0.5
LOG2E = math.log2(math.e)
GC = math.sqrt(2.0 / math.pi)
GK = 0.044715


def nn(a, b):
    return lax.dot_general(a, b, (((1,), (0,)), ((), ())), preferred_element_type=f32)


def nt(a, b):
    return lax.dot_general(a, b, (((1,), (1,)), ((), ())), preferred_element_type=f32)


def tn(a, b):
    return lax.dot_general(a, b, (((0,), (0,)), ((), ())), preferred_element_type=f32)


def moments(v):
    c = v - jnp.mean(v, axis=-1, keepdims=True)
    r = lax.rsqrt(jnp.mean(c * c, axis=-1, keepdims=True) + EPS)
    return c * r, r


def norm_back(e, n, r, g):
    s = e * g
    inner = s - jnp.mean(s, axis=-1, keepdims=True) - n * jnp.mean(s * n, axis=-1, keepdims=True)
    return inner * r


def split_heads(t):
    low = lax.broadcasted_iota(jnp.int32, t.shape, 1) < 64
    zero = jnp.zeros_like(t)
    return jnp.concatenate([jnp.where(low, t, zero), jnp.where(low, zero, t)], axis=0)


def stack_lanes(t):
    return jnp.concatenate([t[:, :SPAN], t[:, SPAN:]], axis=0)


def permitted(lengths, row):
    ends = []
    total = 0
    for k in range(4):
        total = total + lengths[row, k]
        ends.append(total)
    key = lax.broadcasted_iota(jnp.int32, (SPAN, SPAN), 0)
    query = lax.broadcasted_iota(jnp.int32, (SPAN, SPAN), 1)
    one, zero = jnp.int32(1), jnp.int32(0)
    seg_key = sum(jnp.where(key >= e, one, zero) for e in ends)
    seg_query = sum(jnp.where(query >= e, one, zero) for e in ends)
    return (seg_key == seg_query) & ((key < total) | (key == query))


def attend(qkv, mask):
    mask2 = jnp.concatenate([mask, mask], axis=1)
    probs, mixed = [], []
    for p in range(6):
        q2, k2, v2 = qkv(p * 128), qkv(768 + p * 128), qkv(1536 + p * 128)
        s = jnp.where(mask2, nt(k2, split_heads(q2)), NEG)
        top = jnp.max(s, axis=0, keepdims=True)
        e = jnp.exp2((s - top) * (SCALE * LOG2E))
        w = (e * (1.0 / jnp.sum(e, axis=0, keepdims=True))).astype(bf)
        probs.append(w)
        mixed.append(tn(stack_lanes(w), split_heads(v2)).astype(bf))
    return probs, mixed


def attend_back(q2, k2, v2, w, do2):
    do_bd = split_heads(do2)
    dv = nn(w, do_bd)
    dp = nt(v2, do_bd)
    pf = w.astype(f32)
    pd = pf * dp
    inner = jnp.sum(pd, axis=0, keepdims=True)
    draw = ((pd - pf * inner) * SCALE).astype(bf)
    dq = tn(stack_lanes(draw), split_heads(k2))
    dk = nn(draw, split_heads(q2))
    return dq.astype(bf), dk.astype(bf), dv.astype(bf)


def gelu(t):
    return t * (0.5 + 0.5 * jnp.tanh(t * (GC + (GC * GK) * (t * t))))


def gelu_slope(t):
    t2 = t * t
    s = 0.5 + 0.5 * jnp.tanh(t * (GC + (GC * GK) * t2))
    a = t * s
    return s + (a - a * s) * (2.0 * GC + (6.0 * GC * GK) * t2)


FC = 768


def kernel_d1(wn, dz, g):
    g[...] = tn(wn[...], dz[...]).astype(g.dtype)


def kernel_e(qkv, probs, do, dqkv):
    for rr in range(TILE // SPAN):
        rows = slice(rr * SPAN, (rr + 1) * SPAN)
        for p in range(6):
            cols = slice(p * 128, (p + 1) * 128)
            q2, k2, v2 = (qkv[rows, j * 768 + p * 128 : j * 768 + p * 128 + 128] for j in range(3))
            dq, dk, dv = attend_back(q2, k2, v2, probs[rr, p], do[rows, cols])
            dqkv[rows, p * 128 : p * 128 + 128] = dq
            dqkv[rows, 768 + p * 128 : 768 + p * 128 + 128] = dk
            dqkv[rows, 1536 + p * 128 : 1536 + p * 128 + 128] = dv


def kernel_f(x, dqkv, dh, gain, w_qkv, dx_out):
    n, r = moments(x[...].astype(f32))
    du = nt(dqkv[...], w_qkv[...])
    dx_out[...] = (dh[...] + norm_back(du, n, r, gain[...])).astype(bf)


def whole(shape):
    return pl.BlockSpec(shape, lambda i: (0,) * len(shape), pipeline_mode=pl.Buffered(1))


def rows_of(cols, tile=TILE):
    return pl.BlockSpec((tile, cols), lambda i: (i, 0))


def call(body, name, grid, in_specs, out_specs, out_shape, flops, nbytes, scratch=()):
    return pl.pallas_call(
        body,
        name=name,
        grid=grid,
        in_specs=in_specs,
        out_specs=out_specs,
        out_shape=out_shape,
        scratch_shapes=scratch,
        cost_estimate=pl.CostEstimate(flops=flops, bytes_accessed=nbytes, transcendentals=0),
        compiler_params=pltpu.CompilerParams(vmem_limit_bytes=VMEM),
    )


def sds(*shape, dtype=bf):
    return jax.ShapeDtypeStruct(shape, dtype)


def weight_grad(left, right, name, tile, out=bf, by="right"):
    T, M = left.shape
    N = right.shape[1]
    if by == "right":
        ins = [whole((T, M)), pl.BlockSpec((T, tile), lambda i: (0, i))]
        outs = pl.BlockSpec((M, tile), lambda i: (0, i))
        grid = (N // tile,)
    else:
        ins = [pl.BlockSpec((T, tile), lambda i: (0, i)), whole((T, N))]
        outs = pl.BlockSpec((tile, N), lambda i: (i, 0))
        grid = (M // tile,)
    return call(kernel_d1, name, grid, ins, outs, sds(M, N, dtype=out), 2 * T * M * N, 2 * (T * M + T * N + M * N))(left, right)


def attention_back(qkv, probs, do):
    T, D = do.shape
    per = TILE // SPAN
    return call(
        kernel_e, "attention_backward", (T // TILE,),
        [rows_of(3 * D), pl.BlockSpec((per, 6, SPAN, 2 * SPAN), lambda i: (i, 0, 0, 0)), rows_of(D)],
        rows_of(3 * D), sds(T, 3 * D), 8 * T * D * D, 30 << 20,
    )(qkv, probs, do)


def input_grad(x, dqkv, dh, g1, w_qkv):
    T, D = x.shape
    return call(
        kernel_f, "input_grad", (T // TILE,),
        [rows_of(D), rows_of(3 * D), rows_of(D), whole((1, D)), whole(w_qkv.shape)],
        rows_of(D), sds(T, D),
        6 * T * D * D, 30 << 20,
    )(x, dqkv, dh, g1, w_qkv)


MESH = pl.DeviceIdType.MESH
D_MODEL = 768
P_B = 3
EARLY = 6
MESSAGES = {
    "x0s": (0, 2, 0, "mine", None), "y0s": (0, 4, 0, "mine", None), "x0c": (0, 2, 0, "middle", None), "y0c": (0, 4, 0, "middle", None),
    "c0": (0, 1, 0, "all", None),
    "xf": (0, 4, 2, "mine", "x0s"), "xz": (1, 0, 2, "mine", "x0s"), "xcs": (0, 1, 2, "mine", "x0s"),
    "yz": (1, 0, 4, "mine", "y0s"), "ycs": (0, 1, 4, "mine", "y0s"),
    "xcc": (0, 1, 2, "middle", "x0c"), "yf": (0, 2, 4, "middle", "y0c"), "ycc": (0, 1, 4, "middle", "y0c"),
    "dz": (1, 0, 6, "mine", "xf"), "dcs": (0, 1, 6, "mine", "xf"), "dcc": (0, 1, 6, "middle", "yf"),
    "xcm": (0, 1, 2, "other", "xz"), "ycm": (0, 1, 4, "other", "yz"), "dcm": (0, 1, 6, "other", "dz"),
}
ARRIVALS = [None, "x0s", "y0s", "x0c", "y0c", "xf", "yf", "xz", "yz", "dz"]
RELAYS = {
    0: [0, 10, 1, 2, 20, 3, 4, 11, 12, 7, 13, 14, 8, 21, 5, 17, 30, 23, 22, 18, 6, 24, 27, 16, 15, 9, 40, 31, 25, 28, 33, 32],
    1: [19, 26, 34, 37, 41, 42, 29, 50, 60, 43, 44, 38, 35, 70],
    2: [36, 45, 47, 51, 52, 48, 80],
    3: [53, 54, 39, 61, 62, 63, 64, 49, 90],
    4: [46, 72, 57, 71, 74, 58],
    5: [73, 55, 67, 81, 82],
    6: [68, 83, 84, 78, 100, 56, 65],
    7: [77, 66, 92, 59, 110],
    8: [91, 94, 87, 93, 75, 88],
    9: [76, 85, 69, 86, 102],
    10: [98, 101, 104, 97, 103],
    11: [112, 79, 111, 114, 89],
    12: [113, 95, 108, 96, 105, 107, 106],
    13: [115, 118, 116, 117],
    14: [99, 109],
    15: [119],
}


class Gather:
    def __init__(self, shard, piece, send, recv, local, me, rep):
        self.shard, self.piece, self.send, self.recv, self.me, self.rep = shard, piece, send, recv, me, rep
        self.own = pltpu.make_async_copy(shard, piece(me), local)

    def copy(self, name):
        rep_to, me_to, whose, what, _ = MESSAGES[name]
        s = ARRIVALS.index(name) if name in ARRIVALS else 0
        third = D_MODEL // 3
        parity = self.rep % 2
        cols = {
            "all": lambda: pl.ds(0, D_MODEL),
            "mine": lambda: pl.ds(pl.multiple_of(parity * 2 * third, 128), third),
            "middle": lambda: pl.ds(third, third),
            "other": lambda: pl.ds(pl.multiple_of((1 - parity) * 2 * third, 128), third),
        }[what]()
        piece = self.piece(self.me ^ whose)
        src = self.shard if whose == 0 else piece
        return pltpu.make_async_remote_copy(
            src_ref=src.at[:, cols], dst_ref=piece.at[:, cols], send_sem=self.send, recv_sem=self.recv.at[s],
            device_id=(self.rep ^ rep_to, self.me ^ me_to), device_id_type=MESH,
        )

    def relay(self, arrival):
        if arrival is None:
            self.own.start()
        else:
            self.copy(arrival).wait_recv()
        for name, message in MESSAGES.items():
            if message[4] == arrival:
                self.copy(name).start()

    def complete(self):
        self.own.wait()
        four = self.piece(pl.ds(0, 4))
        pltpu.make_async_copy(four, four, self.recv.at[0]).wait()

    def finish(self):
        seven = self.piece(pl.ds(0, 7))
        pltpu.make_async_copy(seven, seven, self.send).wait()


class Local:
    def __init__(self, shard, place, local):
        self.own = pltpu.make_async_copy(shard, place, local)

    def relay(self, arrival):
        if arrival is None:
            self.own.start()

    def complete(self):
        self.own.wait()

    def finish(self):
        pass


def dispatch(step, table):
    keys = sorted(table)
    if len(keys) < 4:
        for k in keys:
            pl.when(step == k)(table[k])
    else:
        middle = keys[len(keys) // 2]
        pl.when(step < middle)(lambda: dispatch(step, {k: table[k] for k in keys if k < middle}))
        pl.when(step >= middle)(lambda: dispatch(step, {k: table[k] for k in keys if k >= middle}))


def flat(t):
    return t.reshape(t.shape[0] * t.shape[1], t.shape[2])


def spread(pieces):
    width = D_MODEL // 8
    lane = lax.broadcasted_iota(jnp.int32, (128, D_MODEL), 0)
    place = lax.broadcasted_iota(jnp.int32, (128, D_MODEL), 1)
    total = jnp.zeros((16, D_MODEL), f32)
    for d in range(8):
        hit = (place == lane + d * width) & (lane < width)
        total = total + nn(pieces[d], jnp.where(hit, 1.0, 0.0).astype(bf))
    return total[:8]


def kernel_one(
    remote, lengths, x, dy, gain_in, q_in, o_in, i_in, t_in,
    qkv_out, probs_out, u_out, y_out, wn_out, za_out, dh_out, do_out, gains_out, gwo_out, wq_out,
    wq, wo, wi, wt, gain_parts, gains, high, low, qa, zs, mixed_all, wn, send, recv, gain_send, gain_recv, local, out_sem, a_sem, dz_sem,
):
    step = pl.program_id(0)
    T, D = high.shape
    tiles = T // TILE
    p_h = P_B + tiles
    p_in, p_back = p_h + 2, p_h + 10
    steps = p_back + tiles
    me, rep = lax.axis_index("fsdp"), lax.axis_index("rep")
    part = lambda j: pl.ds(j * D, D)
    rows_of_part = lambda j: pl.ds(j * 96, 96)
    if remote:
        refs = [(q_in.at[:, part(j)], lambda p, j=j: wq.at[j, p]) for j in range(3)]
        refs += [(o_in, lambda p: wo.at[p])]
        refs += [(i_in.at[:, part(j)], lambda p, j=j: wi.at[j, p]) for j in range(4)]
        refs += [(t_in.at[rows_of_part(j)], lambda p, j=j: wt.at[p, rows_of_part(j)]) for j in range(4)]
        blocks = [Gather(s, f, send.at[k], recv.at[k], local.at[k], me, rep) for k, (s, f) in enumerate(refs)]
    else:
        refs = [(q_in.at[:, :, part(j)], wq.at[j]) for j in range(3)] + [(o_in, wo)]
        refs += [(i_in.at[:, :, part(j)], wi.at[j]) for j in range(4)]
        refs += [(t_in.at[:, rows_of_part(j)], wt.at[:, rows_of_part(j)]) for j in range(4)]
        blocks = [Local(s, f, local.at[k]) for k, (s, f) in enumerate(refs)]

    def gain_copy(d):
        return pltpu.make_async_remote_copy(
            src_ref=gain_in, dst_ref=gain_parts.at[me], send_sem=gain_send.at[d], recv_sem=gain_recv.at[d],
            device_id=(rep, me ^ d), device_id_type=MESH,
        )

    own_gain = pltpu.make_async_copy(gain_in, gain_parts.at[me] if remote else gain_parts, local.at[12])
    load_x = pltpu.make_async_copy(x, high, local.at[13])
    export = pltpu.make_async_copy(wq, wq_out, out_sem.at[0])
    store_u = pltpu.make_async_copy(low, u_out, out_sem.at[1])
    store_wn = pltpu.make_async_copy(wn, wn_out, out_sem.at[2])
    store_gwo = pltpu.make_async_copy(mixed_all.at[pl.ds(0, D)], gwo_out, out_sem.at[3])

    def store_qkv(j):
        cols = pl.ds(pl.multiple_of(j * D, D), D)
        return pltpu.make_async_copy(qa.at[:, cols], qkv_out.at[:, cols], out_sem.at[4 + j])

    def rows_at(t, n):
        return pl.ds(pl.multiple_of(t * n, n), n)

    def store_a(e):
        place = (rows_at(lax.rem(e, 2), T // 2), pl.ds(pl.multiple_of(lax.div(e, 2) * FC, FC), FC))
        return pltpu.make_async_copy(qa.at[place], za_out.at[(1, *place)], a_sem.at[e])

    def store_dz(t):
        return pltpu.make_async_copy(zs.at[rows_at(t, TILE)], za_out.at[0, rows_at(t, TILE)], dz_sem.at[t])

    def relay(code):
        blocks[code // 10].relay(ARRIVALS[code % 10])

    @pl.when(step == 0)
    def _():
        load_x.start()
        if remote:
            barrier = pltpu.get_barrier_semaphore()
            for d in range(1, 8):
                pl.semaphore_signal(barrier, inc=1, device_id=(rep, me ^ d), device_id_type=MESH)
            pl.semaphore_signal(barrier, inc=1, device_id=(rep ^ 1, me), device_id_type=MESH)
            pl.semaphore_wait(barrier, 8)
            for d in range(1, 8):
                gain_copy(d).start()
        own_gain.start()
        for code in RELAYS[0][:EARLY]:
            relay(code)
        own_gain.wait()
        if remote:
            for d in range(1, 8):
                gain_copy(d).wait_recv()
        gains[...] = spread(gain_parts)
        gains_out[...] = gains[...]
        load_x.wait()
        later = RELAYS[0][EARLY:]
        for t in range(max(tiles, len(later))):
            if t < tiles:
                rows = pl.ds(t * TILE, TILE)
                n, _ = moments(high[rows, :].astype(f32))
                low[rows, :] = (n * gains[0:1]).astype(bf)
            if t < len(later):
                relay(later[t])
        store_u.start()
        blocks[0].complete()

    completes = {1: [1], 2: [2], p_h: [3], p_back: [8, 9, 10, 11]}
    completes.update({p_in + 2 * j: [4 + j] for j in range(4)})

    def begin(at):
        for code in RELAYS.get(at, []):
            relay(code)
        for k in completes.get(at, []):
            blocks[k].complete()
        if at == P_B:
            export.start()
        if at == p_h:
            store_u.wait()
        if at == p_in:
            store_wn.start()
            for j in range(3):
                store_qkv(j).wait()

    dispatch(step, {at: functools.partial(begin, at) for at in {*RELAYS, *completes, P_B} - {0}})

    @pl.when(step < P_B)
    def _():
        w = flat(wq[step])
        block = 2 * TILE
        cols = pl.ds(pl.multiple_of(step * D, D), D)
        for t in range(T // block):
            qa[t * block : (t + 1) * block, cols] = nn(low[t * block : (t + 1) * block], w).astype(bf)
        store_qkv(step).start()

    @pl.when((step >= P_B) & (step < p_h))
    def _():
        t = step - P_B
        for rr in range(TILE // SPAN):
            rows = pl.ds(pl.multiple_of(t * TILE + rr * SPAN, SPAN), SPAN)
            mask = permitted(lengths, t * (TILE // SPAN) + rr)
            probs, mixed = attend(lambda c: qa[rows, c : c + 128], mask)
            for p in range(6):
                probs_out[rr, p] = probs[p]
                mixed_all[rows, p * 128 : (p + 1) * 128] = mixed[p]

    @pl.when((step >= p_h) & (step < p_in))
    def _():
        for s in range(tiles // 2):
            rows = rows_at((step - p_h) * (tiles // 2) + s, TILE)
            h = high[rows, :].astype(f32) + nn(mixed_all[rows, :], flat(wo[...]))
            top = h.astype(bf)
            high[rows, :] = top
            low[rows, :] = (h - top.astype(f32)).astype(bf)
            n, _ = moments(h)
            wn[rows, :] = (n * gains[1:2]).astype(bf)

    @pl.when((step >= p_in) & (step < p_back))
    def _():
        e = step - p_in
        j, half = lax.div(e, 2), lax.rem(e, 2)
        cols = pl.ds(pl.multiple_of(j * FC, FC), FC)
        w = flat(wi[j])
        block = 2 * TILE
        for s in range(T // 2 // block):
            rows = rows_at(half * (T // 2 // block) + s, block)
            z = nn(wn[rows, :], w)
            qa[rows, cols] = gelu(z).astype(bf)
            zs[rows, cols] = z.astype(bf)
        store_a(e).start()

    per = FC // wt.shape[1]

    @pl.when(step >= p_back)
    def _():
        t = step - p_back
        rows = rows_at(t, TILE)
        h = high[rows, :].astype(f32) + low[rows, :].astype(f32)
        n, r = moments(h)
        dm = dy[...]
        y = h
        dw = None
        for j in range(wi.shape[0]):
            cols = slice(j * FC, (j + 1) * FC)
            w_out = flat(wt[j * per : (j + 1) * per])
            y = y + nn(qa[rows, cols], w_out)
            dz = (nt(dm, w_out) * gelu_slope(zs[rows, cols].astype(f32))).astype(bf)
            zs[rows, cols] = dz
            add = nt(dz, flat(wi[j]))
            dw = add if dw is None else dw + add
        store_dz(t).start()
        y_out[...] = y.astype(bf)
        dh = dm.astype(f32) + norm_back(dw, n, r, gains[1:2])
        dh_out[...] = dh
        dt = dh.astype(bf)
        high[rows, :] = dt
        do_out[...] = nt(dt, flat(wo[...])).astype(bf)

    @pl.when(step == steps - 1)
    def _():
        gwo = tn(mixed_all[...], high[...]).astype(bf)
        mixed_all[0:D, :] = gwo
        store_gwo.start()
        export.wait()
        store_wn.wait()
        for t in range(tiles):
            store_a(t).wait()
            store_dz(t).wait()
        if remote:
            for d in range(1, 8):
                gain_copy(d).wait_send()
        for b in blocks:
            b.finish()
        store_gwo.wait()


def forward_and_mlp(remote, x, lengths, dy, gain, w_qkv, w_ao, w_in, w_out):
    T, D = x.shape
    tiles = T // TILE
    per = TILE // SPAN
    F = w_in.shape[-1]
    rows = D // 8

    def tile_from(start, *shape):
        return pl.BlockSpec(shape, lambda i: (jnp.clip(i - start, 0, tiles - 1),) + (0,) * (len(shape) - 1))

    p_back = P_B + tiles + 10
    hbm = pl.BlockSpec(memory_space=pl.ANY)

    return pl.pallas_call(
        functools.partial(kernel_one, remote),
        name="forward_and_mlp",
        grid=(p_back + tiles,),
        in_specs=[pl.BlockSpec(memory_space=pltpu.SMEM), hbm, tile_from(p_back, TILE, D), hbm, hbm, hbm, hbm, hbm],
        out_specs=[
            hbm, tile_from(P_B, per, 6, SPAN, 2 * SPAN), hbm, tile_from(p_back, TILE, D), hbm, hbm,
            tile_from(p_back, TILE, D), tile_from(p_back, TILE, D), pl.BlockSpec((8, D), lambda i: (0, 0)), hbm, hbm,
        ],
        out_shape=[
            sds(T, 3 * D), sds(T // SPAN, 6, SPAN, 2 * SPAN), sds(T, D),
            sds(T, D), sds(T, D), sds(2, T, F), sds(T, D, dtype=f32), sds(T, D), sds(8, D, dtype=f32), sds(D, D), sds(3, 8, rows, D),
        ],
        scratch_shapes=[
            pltpu.VMEM((3, 8, rows, D), bf), pltpu.VMEM((8, rows, D), bf), pltpu.VMEM((F // FC, 8, rows, FC), bf),
            pltpu.VMEM((8, F // 8, D), bf), pltpu.VMEM((8, 16, 128), bf), pltpu.VMEM((8, D), f32), pltpu.VMEM((T, D), bf),
            pltpu.VMEM((T, D), bf), pltpu.VMEM((T, F), bf), pltpu.VMEM((T, F), bf), pltpu.VMEM((T, D), bf), pltpu.VMEM((T, D), bf),
            pltpu.SemaphoreType.DMA((12,)), pltpu.SemaphoreType.DMA((12, len(ARRIVALS))), pltpu.SemaphoreType.DMA((8,)), pltpu.SemaphoreType.DMA((8,)),
            pltpu.SemaphoreType.DMA((14,)), pltpu.SemaphoreType.DMA((7,)), pltpu.SemaphoreType.DMA((tiles,)), pltpu.SemaphoreType.DMA((tiles,)),
        ],
        cost_estimate=pl.CostEstimate(flops=12 * T * D * D + 8 * T * D * F + 6 * T * D * D, bytes_accessed=90 << 20, transcendentals=0),
        compiler_params=pltpu.CompilerParams(
            vmem_limit_bytes=VMEM, has_side_effects=remote, collective_id=1 if remote else None
        ),
    )(lengths, x, dy, gain, w_qkv, w_ao, w_in, w_out)


def gain_piece(gain_attn, gain_mlp):
    pair = jnp.stack([gain_attn, gain_mlp])
    return jnp.pad(pair, ((0, 14), (0, 128 - pair.shape[1])))


CHUNK = 96
WIDE = 768
RING = 6
N_WIDE = 12
P_IN, P_OUT, P_ATT = 0, 4, 8
P_DX = P_ATT + 18
REUSE = {P_ATT + 8: 0, P_ATT + 14: 1}
START = [
    [0, 1, 3, 6, 9, 12, 21], [2, 3, 7, 10, 14, 17, 21], [5, 6, 8, 12, 16, 19, 36], [3, 5, 8, 11, 18, 20, 28],
    [4, 6, 10, 13, 19, 22, 26], [10, 12, 15, 17, 20, 23, 41], [8, 10, 13, 16, 21, 25, 28], [11, 15, 18, 21, 23, 27, 40],
    [14, 19, 22, 24, 26, 29, 35], [11, 14, 17, 19, 22, 26, 29], [14, 16, 19, 22, 25, 27, 34], [17, 21, 24, 25, 28, 30, 42],
    [21, 22, 25, 27, 29, 31, 38], [24, 25, 27, 29, 31, 33, 40], [26, 27, 29, 30, 32, 38, 39],
]
RECEIVE = {"s1": 0, "s2x": 1, "s2y": 1, "s3y": 2, "s3x": 2, "z1": 3, "z2": 4, "z3": 3}


def slot_of(k):
    return k if k < 10 else k - 10


class Reduce:
    def __init__(self, n, grads, bufs, send, recv, place):
        self.n = n
        k = self.k = n if n < 9 else 9 + (n - 9) // 2
        self.cols = cols = pl.ds(0, WIDE) if n < 9 else pl.ds((n - 9) % 2 * (WIDE // 2), WIDE // 2)
        first, x2, y2, y3, x3, outer, inner, out = bufs
        r = k % RING
        self.g = grads.at[slot_of(k), :, :, :, :, cols]
        self.first = first.at[r, :, :, :, cols]
        self.x2, self.y2 = x2.at[r, :, :, cols], y2.at[r, :, :, cols]
        self.x3, self.y3 = x3.at[k, :, cols], y3.at[k, :, cols]
        self.outer, self.inner, self.out = outer.at[k, :, cols], inner.at[k, :, cols], out.at[k, :, cols]
        self.send, self.recv = send, recv
        self.y, self.x, self.c, self.me, self.rep = place
        self.is_inner = (self.rep == 1) | (self.rep == 2)

    def copy(self, m):
        g, y, x, c = self.g, self.y, self.x, self.c
        upper, lower = pl.ds(0, CHUNK // 2), pl.ds(CHUNK // 2, CHUNK // 2)
        src, dst, rep_to, me_to = {
            "s1": lambda: (g.at[:, :, 1 - c], self.first, 0, 1),
            "s2x": lambda: (g.at[:, 1 - x, c, upper], self.x2, 0, 2),
            "s2y": lambda: (g.at[1 - y, :, c, lower], self.y2, 0, 4),
            "s3y": lambda: (g.at[1 - y, x, c, upper], self.y3, 0, 4),
            "s3x": lambda: (g.at[y, 1 - x, c, lower], self.x3, 0, 2),
            "z1": lambda: (g.at[y, x, c], self.outer, 1, 0),
            "z2": lambda: (g.at[y, x, c], self.inner, 3, 0),
            "z3": lambda: (self.out, self.out, 1, 0),
        }[m]()
        return pltpu.make_async_remote_copy(
            src_ref=src, dst_ref=dst, send_sem=self.send.at[self.n, int(m == "z3")], recv_sem=self.recv.at[self.n, RECEIVE[m]],
            device_id=(self.rep ^ rep_to, self.me ^ me_to), device_id_type=MESH,
        )

    def start(self, *names):
        for m in names:
            self.copy(m).start()

    def arrived(self, m, ref):
        pltpu.make_async_copy(ref, ref, self.recv.at[self.n, RECEIVE[m]]).wait()

    def stage(self, s):
        g, y, x, c = self.g, self.y, self.x, self.c
        upper, lower = pl.ds(0, CHUNK // 2), pl.ds(CHUNK // 2, CHUNK // 2)
        if s == 1:
            self.start("s1")
        elif s == 2:
            self.arrived("s1", self.first)
            for b in range(2):
                for a in range(2):
                    g[b, a, c] += self.first[b, a]
            self.start("s2x", "s2y")
        elif s == 3:
            self.arrived("s2x", g.at[0, 0])
            for b in range(2):
                g[b, x, c, upper] += self.x2[b]
                g[y, b, c, lower] += self.y2[b]
            self.start("s3y", "s3x")
        elif s == 4:
            self.arrived("s3y", g.at[0, 0, 0])
            g[y, x, c, upper] += self.y3[...]
            g[y, x, c, lower] += self.x3[...]

            @pl.when(jnp.logical_not(self.is_inner))
            def _():
                self.start("z1")
        elif s == 5:
            @pl.when(self.is_inner)
            def _():
                self.arrived("z1", self.outer)
                g[y, x, c] += self.outer[...]
                self.start("z2")
        elif s == 6:
            @pl.when(self.is_inner)
            def _():
                self.arrived("z2", self.inner)
                self.out[...] = g[y, x, c] + self.inner[...]
                self.start("z3")
        elif s == 7:
            @pl.when(jnp.logical_not(self.is_inner))
            def _():
                self.arrived("z3", self.out)

    def sent(self):
        pltpu.make_async_copy(self.g, self.g, self.send.at[self.n, 0]).wait()

    def sum_sent(self):
        @pl.when(self.is_inner)
        def _():
            pltpu.make_async_copy(self.out, self.out, self.send.at[self.n, 1]).wait()


def part_of(e):
    return lax.div(e, 3), jnp.minimum(lax.rem(e, 3), 1), lax.rem(e, 3) == 2


def kernel_two(
    gwo_in, wn, dm, u, wq, gains, za, qs, ks, vs, probs, do, x, dh,
    dx_out, out_hbm,
    out, big_a, big_b, wq_s, dqkv, grads, first, x2, y2, y3, x3, outer, inner, send, recv, local,
):
    step = pl.program_id(0)
    T, D = big_a.shape
    steps = P_DX + T // TILE
    me, rep = lax.axis_index("fsdp"), lax.axis_index("rep")
    place = (me // 4, (me // 2) % 2, me % 2, me, rep)
    bufs = (first, x2, y2, y3, x3, outer, inner, out)
    chunks = [Reduce(n, grads, bufs, send, recv, place) for n in range(len(START))]
    load_gwo = pltpu.make_async_copy(gwo_in, grads.at[0], local.at[0])
    load_wn = pltpu.make_async_copy(wn, big_a, local.at[1])
    load_dm = pltpu.make_async_copy(dm, big_b, local.at[2])
    load_u = pltpu.make_async_copy(u, big_a, local.at[3])
    load_wq = pltpu.make_async_copy(wq, wq_s, local.at[4])
    store_out = pltpu.make_async_copy(out, out_hbm, local.at[5])

    @pl.when(step == 0)
    def _():
        load_wn.start()
        load_gwo.start()
        barrier = pltpu.get_barrier_semaphore()
        for to in ((rep, me ^ 1), (rep, me ^ 2), (rep, me ^ 4), (rep ^ 1, me), (rep ^ 3, me)):
            pl.semaphore_signal(barrier, inc=1, device_id=to, device_id_type=MESH)
        pl.semaphore_wait(barrier, 5)
        load_gwo.wait()

    acts = {}
    for n, starts in enumerate(START):
        for s, at in enumerate(starts):
            acts.setdefault(at, []).append((n, s + 1))

    def act(at):
        for n, s in sorted(acts[at], key=lambda ns: -ns[1]):
            chunks[n].stage(s)

    def begin(at):
        if at in acts:
            act(at)
        if at == 0:
            load_wn.wait()
        if at == 1:
            load_dm.start()
        if at == P_OUT:
            load_u.start()
            load_dm.wait()
        if at == P_OUT + 1:
            load_wq.start()
        if at == P_ATT + 2:
            load_u.wait()
            load_wq.wait()
        if at in REUSE:
            chunks[REUSE[at]].sent()

    dispatch(step, {at: functools.partial(begin, at) for at in {*acts, *REUSE, 0, 1, P_OUT, P_OUT + 1, P_ATT + 2} if at < steps})

    @pl.when(step < P_OUT)
    def _():
        g = tn(big_a[...], za[0]).astype(bf)
        grads[1 + step] = g.reshape(2, 2, 2, CHUNK, WIDE)

    @pl.when((step >= P_OUT) & (step < P_ATT))
    def _():
        j = step - P_OUT
        g = tn(za[0], big_b[...]).astype(bf).reshape(2, 4, CHUNK, WIDE)
        for part in range(4):
            grads[5 + part, j // 2, j % 2] = g[:, part]

    pair, half, product = part_of(step - P_ATT)
    attention = (step >= P_ATT) & (step < P_DX)

    @pl.when(attention & jnp.logical_not(product))
    def _():
        for rr in range(probs.shape[0]):
            rows = slice(rr * SPAN, (rr + 1) * SPAN)
            to = pl.ds(pl.multiple_of((half * probs.shape[0] + rr) * SPAN, SPAN), SPAN)
            back = attend_back(qs[rows], ks[rows], vs[rows], probs[rr, 0], do[rows])
            for j in range(3):
                dqkv[pair, to, j * 128 : (j + 1) * 128] = back[j]

    @pl.when(attention & product)
    def _():
        k = pair // 2
        g = tn(big_a[...], dqkv[pair]).astype(bf)
        cols = pl.ds(pl.multiple_of(lax.rem(pair, 2) * (WIDE // 2), WIDE // 2), WIDE // 2)
        grads[jnp.where(k == 0, 9, k - 1), :, :, :, :, cols] = g.reshape(2, 2, 2, CHUNK, WIDE // 2)

    @pl.when(step >= P_DX)
    def _():
        rows = pl.ds(pl.multiple_of((step - P_DX) * TILE, TILE), TILE)
        n, r = moments(x[...].astype(f32))
        d = jnp.concatenate([dqkv[p, rows, j * 128 : (j + 1) * 128] for j in range(3) for p in range(D // 128)], axis=1)
        du = sum(nt(d[:, j * D : (j + 1) * D], flat(wq_s[j])) for j in range(3))
        dx_out[...] = (dh[...] + norm_back(du, n, r, gains[0:1])).astype(bf)

    @pl.when(step == steps - 1)
    def _():
        for at in sorted(acts):
            if at >= steps:
                act(at)
        store_out.start()
        for n in range(len(START)):
            if n not in REUSE.values():
                chunks[n].sent()
            chunks[n].sum_sent()
        store_out.wait()


def gradients(gwo, wn, dy, u, wq, gains, za, qkv, probs, do, x, dh):
    T, D = x.shape
    tiles = T // TILE
    steps = P_DX + tiles
    pairs = D // 128
    hbm = pl.BlockSpec(memory_space=pl.ANY)

    def tile_from(start, *shape):
        return pl.BlockSpec(shape, lambda i: (jnp.clip(i - start, 0, tiles - 1),) + (0,) * (len(shape) - 1))

    def part(i):
        return part_of(jnp.clip(i - P_ATT, 0, 3 * pairs - 1))[:2]

    def head_cols(which):
        def index(i):
            pair, half = part(i)
            return half, which * pairs + pair

        return pl.BlockSpec((T // 2, 128), index)

    def probs_index(i):
        pair, half = part(i)
        return half, pair, 0, 0

    wide = lambda *shape: pltpu.VMEM(shape + (WIDE,), bf)
    return pl.pallas_call(
        kernel_two,
        name="gradients",
        grid=(steps,),
        in_specs=[
            hbm, hbm, hbm, hbm, hbm, pl.BlockSpec((8, D), lambda i: (0, 0)),
            pl.BlockSpec((1, T, WIDE), lambda i: (jnp.where(i < P_OUT, 0, 1), 0, jnp.where(i < P_OUT, i, jnp.minimum(i - P_OUT, 3)))),
            head_cols(0), head_cols(1), head_cols(2), pl.BlockSpec((T // SPAN // 2, 1, SPAN, 2 * SPAN), probs_index), head_cols(0),
            tile_from(P_DX, TILE, D), tile_from(P_DX, TILE, D),
        ],
        out_specs=[tile_from(P_DX, TILE, D), hbm],
        out_shape=[sds(T, D), sds(N_WIDE, CHUNK, WIDE)],
        scratch_shapes=[
            wide(N_WIDE, CHUNK), pltpu.VMEM((T, D), bf), pltpu.VMEM((T, D), bf), pltpu.VMEM(wq.shape, bf),
            pltpu.VMEM((pairs, T, 3 * 128), bf), wide(10, 2, 2, 2, CHUNK), wide(RING, 2, 2, CHUNK), wide(RING, 2, CHUNK // 2),
            wide(RING, 2, CHUNK // 2), wide(N_WIDE, CHUNK // 2), wide(N_WIDE, CHUNK // 2), wide(N_WIDE, CHUNK), wide(N_WIDE, CHUNK),
            pltpu.SemaphoreType.DMA((len(START), 2)), pltpu.SemaphoreType.DMA((len(START), 5)),
            pltpu.SemaphoreType.DMA((6,)),
        ],
        cost_estimate=pl.CostEstimate(flops=8 * T * D * D + 4 * T * D * 4 * D + 20 * T * D * D, bytes_accessed=90 << 20, transcendentals=0),
        compiler_params=pltpu.CompilerParams(vmem_limit_bytes=VMEM, has_side_effects=True, collective_id=2),
    )(gwo.reshape(2, 2, 2, CHUNK, WIDE), wn, dy, u, wq, gains, za, qkv, qkv, qkv, probs, do, x, dh)


def shards(x, lengths, segments, gain_attn, w_qkv, w_attn_out, gain_mlp, w_mlp_in, w_mlp_out, dy):
    D = x.shape[1]
    remote = lax.axis_size("fsdp") == 8 and lax.axis_size("rep") == 4
    gain = gain_piece(gain_attn, gain_mlp)
    weights = (w_qkv, w_attn_out, w_mlp_in, w_mlp_out)
    if not remote:
        weights = tuple(lax.all_gather(v, "fsdp", axis=0, tiled=True) for v in weights)
        weights = tuple(v.reshape(8, v.shape[0] // 8, v.shape[1]) for v in weights)
        gains = [lax.all_gather(v, "fsdp", axis=0, tiled=True).reshape(8, -1) for v in (gain_attn, gain_mlp)]
        gain = jnp.stack([gain_piece(a, b) for a, b in zip(*gains)])
    qkv, probs, u, y, wn, za, dh, do, gains, gwo, wq = forward_and_mlp(remote, x, lengths, dy, gain, *weights)
    if remote:
        dx, sums = gradients(gwo, wn, dy, u, wq, gains, za, qkv, probs, do, x, dh)
        sums = sums.astype(f32)
        wide = lambda v: v.transpose(1, 0, 2).reshape(v.shape[1], -1)
        gq = sums[9:12].reshape(3, CHUNK, 2, 3, 128).transpose(1, 3, 0, 2, 4).reshape(CHUNK, 3 * D)
        gwo, gwi, gwt = sums[0], wide(sums[1:5]), sums[5:9].reshape(-1, D)
    else:
        scatter = lambda v: lax.psum_scatter(v, "fsdp", scatter_dimension=0, tiled=True)
        gwt = scatter(weight_grad(za[1], dy, "mlp_out_grad", 768, bf, "left"))
        gwi = scatter(weight_grad(wn, za[0], "mlp_in_grad", 768))
        gwo = scatter(gwo)
        dqkv = attention_back(qkv, probs, do)
        gq = scatter(weight_grad(u, dqkv, "qkv_grad", 768))
        dx = input_grad(x, dqkv, dh, gains[0:1], wq.transpose(1, 2, 0, 3).reshape(D, 3 * D))
        gwt, gwi, gwo, gq = lax.psum((gwt, gwi, gwo, gq), "rep")
        gwt, gwi, gwo, gq = (v.astype(f32) for v in (gwt, gwi, gwo, gq))
    gg1 = jnp.sum(w_qkv.astype(f32) * gq, axis=1) / gain_attn.astype(f32)
    gg2 = jnp.sum(w_mlp_in.astype(f32) * gwi, axis=1) / gain_mlp.astype(f32)
    return y, dx, gg1, gq, gwo, gg2, gwi, gwt


def solution(mesh):
    tokens, cut, vec = P(("rep", "fsdp"), None), P("fsdp", None), P("fsdp")
    return jax.shard_map(
        shards,
        mesh=mesh,
        in_specs=(tokens, tokens, P(("rep", "fsdp")), vec, cut, cut, vec, cut, cut, tokens),
        out_specs=(tokens, tokens, vec, cut, cut, vec, cut, cut),
        check_vma=False,
    )
```

time: 549 us -> 230 us (0.42)
  waiting for transfers between devices: 329 us -> 0 us
  Pallas kernels: 177 us -> 209 us
  other arithmetic: 18.4 us -> 2.55 us
  between operations: 13.9 us -> 0.73 us
  local copies, waits for them, and re-layouts: 9.64 us -> 16.5 us
    reduce_scatter x4 -> x0, waiting for transfers between devices: 135 us -> none  [shards(): lax.psum_scatter(v, 'fsdp', scatter_dimension=0, tiled=True)]
    all_gather x4 -> x0, waiting for transfers between devices: 112 us -> none  [shards(): gather = lambda v: lax.all_gather(v, 'fsdp', axis=0, tiled=True)]
    psum x1 -> x0, waiting for transfers between devices: 80.3 us -> none  [shards(): gwt, gwi, gwo, gq = lax.psum((gwt, gwi, gwo, gq), 'rep')]
    pallas_call x8 -> x2, Pallas kernels: 177 us -> 209 us  [the longest x1 115 us: forward_and_mlp(): pl.pallas_call(functools.partial(kernel_one, remote), name='forward_and_m...]
    convert_element_type x6 -> x1, other arithmetic: 11.1 us -> 0.32 us  [shards(): sums = sums.astype(f32)]
    unnamed x7 -> x22, local copies, waits for them, and re-layouts: 1.37 us -> 7.55 us
    concatenate x2 -> x0, other arithmetic: 5.86 us -> none  [the longest x1 4.04 us: shards(): jnp.concatenate([gq, jnp.pad(ends, ((0, 0), (0, 126)))], axis=1)]
  transfers between devices with their start and end apart: 9 -> 0, of which waited for: 7 -> 0; matrix products, arithmetic and copies ran while one was open for 2% -> 0% of each run, Pallas kernels for 19% -> 0%
where the time goes in v4:
time: 230 us; the launch traced here: 229 us
  Pallas kernels  209 us (91%)
  local copies, waits for them, and re-layouts  16.5 us (7%)
  other arithmetic  2.55 us (1%)
    pallas_call x1, Pallas kernels, forward_and_mlp(): pl.pallas_call(functools.partial(kernel_one, remote), name='forward_and_m...  115 us
    pallas_call x1, Pallas kernels, gradients(): pl.pallas_call(kernel_two, name='gradients', grid=(steps,), in_specs=[hbm...  94.1 us
    unnamed x22, local copies, waits for them, and re-layouts  7.55 us

profile of v4, /device:TPU:0, one launch (start us, length us, event | category | flops | bytes accessed | tf_op | source)
XLA Modules:
  0.0 229.2 jit_solution(9610200268771803711)
XLA Ops:
  0.6 1.3 fusion.5.gain_in
  1.9 1.4 copy.21.lengths
  3.3 115.3 %forward_and_mlp.1 = (bf16[2048,2304]{1,0:T(8,128)(2,1)}, bf16[16,6,128,256]{3,2,1,0:T(8,128)(2,1)}, bf16[2048,768]{1,0:T(8,128)(2,1)}, bf16[2048,768]{1,0:T(8,1...) custom-call(s32[16,4]{1,0:T(8,128)} %copy.21.lengths, ...), custom_call_target="tpu_custom_call" | custom-call | flops 60397977600 | bytes 94371840 | tf_op jit(solution)/shard_map/forward_and_mlp/pallas_call | solution.py:518
  118.6 94.1 %gradients.1 = (bf16[2048,768]{1,0:T(8,128)(2,1)}, bf16[12,96,768]{2,1,0:T(8,128)(2,1)}) custom-call(bf16[2,2,2,96,768]{4,3,2,1,0:T(8,128)(2,1)} %bitcast.17, bf16[2048,768]{1,0:T(8,128)(2,1)} %get-tuple-element.23.wn, bf16[2048,768]{1,0:T(8,128)(2,1)} %dm.1, bf16[2048,768]{1,0:T(8,128)(2,1)} %get-tuple-element.24.u, ...), custom_call_target="tpu_custom_call" | custom-call | flops 53150220288 | bytes 94371840 | tf_op jit(solution)/shard_map/gradients/pallas_call | solution.py:801
  212.8 2.0 slice.16
  214.8 1.7 reshape.32
  216.5 1.4 copy.22
  217.9 1.9 reshape.33
  219.8 0.2 multiply_reduce_fusion.1
  219.9 1.1 slice.19
  221.1 0.3 convert_element_type.18
  221.4 0.7 slice_bitcast_fusion.1
  222.1 0.1 slice_bitcast_fusion
  222.2 0.1 copy.24
  222.4 0.0 copy-start.1
  222.4 0.2 copy-done.5
  222.6 0.2 multiply_reduce_fusion
  222.8 0.0 copy-done.7
  222.8 0.0 copy-done.8
  222.9 0.5 convert_divide_fusion
  223.4 1.2 copy-done.3
  224.5 1.7 copy.27
  226.2 1.4 copy-done.4
  227.6 1.7 copy.28
  (12 shorter events, 0.0 us)
Async XLA Ops:
  214.8 5.0 %copy-start.6 = (bf16[96,2304]{1,0:T(8,128)(2,1)S(1)}, bf16[96,2304]{1,0:T(8,128)(2,1)}, u32[]{:S(2)}) copy-start(bf16[96,2304]{1,0:T(8,128)(2,1)} %q_in.1) | copy-start | bytes 1327108
  214.8 5.2 %copy-start = (bf16[12,96,768]{2,1,0:T(8,128)(2,1)S(1)}, bf16[12,96,768]{2,1,0:T(8,128)(2,1)}, u32[]{:S(2)}) copy-start(bf16[12,96,768]{2,1,0:T(8,128)(2,1)} %get-tuple-element.33) | copy-start | bytes 5308420
  219.7 1.6 copy-start.2
  221.4 1.2 copy-start.5
  222.1 0.7 copy-start.7
  222.1 0.7 copy-start.8
  222.1 2.4 %copy-start.3 = (bf16[2048,768]{1,0:T(8,128)(2,1)S(1)}, bf16[2048,768]{1,0:T(8,128)(2,1)}, u32[]{:S(2)}) copy-start(bf16[2048,768]{1,0:T(8,128)(2,1)} %get-tuple-element.44) | copy-start | bytes 9437188
  222.4 3.8 %copy-start.1 = (f32[4,12,8,768]{3,2,0,1:T(8,128)}, f32[4,12,8,768]{3,2,0,1:T(8,128)S(1)}, u32[]{:S(2)}) copy-start(f32[4,12,8,768]{3,2,0,1:T(8,128)S(1)} %copy.24) | copy-start | bytes 3538948
  224.5 3.0 %copy-start.4 = (bf16[2048,768]{1,0:T(8,128)(2,1)S(1)}, bf16[2048,768]{1,0:T(8,128)(2,1)}, u32[]{:S(2)}) copy-start(bf16[2048,768]{1,0:T(8,128)(2,1)} %get-tuple-element.45) | copy-start | bytes 9437188

commit v5 on v4

--- a/solution.py
+++ b/solution.py
@@ -55,7 +55,7 @@
     ends = []
     total = 0
     for k in range(4):
-        total = total + lengths[row, k]
+        total = total + lengths[k, row]
         ends.append(total)
     key = lax.broadcasted_iota(jnp.int32, (SPAN, SPAN), 0)
     query = lax.broadcasted_iota(jnp.int32, (SPAN, SPAN), 1)
@@ -116,7 +116,7 @@
         for p in range(6):
             cols = slice(p * 128, (p + 1) * 128)
             q2, k2, v2 = (qkv[rows, j * 768 + p * 128 : j * 768 + p * 128 + 128] for j in range(3))
-            dq, dk, dv = attend_back(q2, k2, v2, probs[rr, p], do[rows, cols])
+            dq, dk, dv = attend_back(q2, k2, v2, probs[rows, p * 2 * SPAN : (p + 1) * 2 * SPAN], do[rows, cols])
             dqkv[rows, p * 128 : p * 128 + 128] = dq
             dqkv[rows, 768 + p * 128 : 768 + p * 128 + 128] = dk
             dqkv[rows, 1536 + p * 128 : 1536 + p * 128 + 128] = dv
@@ -170,10 +170,9 @@
 
 def attention_back(qkv, probs, do):
     T, D = do.shape
-    per = TILE // SPAN
     return call(
         kernel_e, "attention_backward", (T // TILE,),
-        [rows_of(3 * D), pl.BlockSpec((per, 6, SPAN, 2 * SPAN), lambda i: (i, 0, 0, 0)), rows_of(D)],
+        [rows_of(3 * D), rows_of(2 * D), rows_of(D)],
         rows_of(3 * D), sds(T, 3 * D), 8 * T * D * D, 30 << 20,
     )(qkv, probs, do)
 
@@ -294,6 +293,13 @@
     return t.reshape(t.shape[0] * t.shape[1], t.shape[2])
 
 
+def gain_rows(ga, gm):
+    n = ga.shape[1]
+    row = lax.broadcasted_iota(jnp.int32, (16, n), 0)
+    pair = jnp.where(row == 0, ga.astype(f32), jnp.where(row == 1, gm.astype(f32), 0.0))
+    return jnp.concatenate([pair, jnp.zeros((16, 128 - n), f32)], axis=1).astype(bf)
+
+
 def spread(pieces):
     width = D_MODEL // 8
     lane = lax.broadcasted_iota(jnp.int32, (128, D_MODEL), 0)
@@ -306,9 +312,9 @@
 
 
 def kernel_one(
-    remote, lengths, x, dy, gain_in, q_in, o_in, i_in, t_in,
-    qkv_out, probs_out, u_out, y_out, wn_out, za_out, dh_out, do_out, gains_out, gwo_out, wq_out,
-    wq, wo, wi, wt, gain_parts, gains, high, low, qa, zs, mixed_all, wn, send, recv, gain_send, gain_recv, local, out_sem, a_sem, dz_sem,
+    remote, lengths, x, dy, ga, gm, q_in, o_in, i_in, t_in,
+    qkv_out, probs_out, u_out, h_out, wn_out, za_out, dh_out, do_out, gains_out, gwo_out, wq_out, wt_out,
+    wq, wo, wi, wt, gain_piece, gain_parts, gains, high, low, qa, zs, mixed_all, wn, send, recv, gain_send, gain_recv, local, out_sem, a_sem, dz_sem,
 ):
     step = pl.program_id(0)
     T, D = high.shape
@@ -333,15 +339,16 @@
 
     def gain_copy(d):
         return pltpu.make_async_remote_copy(
-            src_ref=gain_in, dst_ref=gain_parts.at[me], send_sem=gain_send.at[d], recv_sem=gain_recv.at[d],
+            src_ref=gain_piece, dst_ref=gain_parts.at[me], send_sem=gain_send.at[d], recv_sem=gain_recv.at[d],
             device_id=(rep, me ^ d), device_id_type=MESH,
         )
 
-    own_gain = pltpu.make_async_copy(gain_in, gain_parts.at[me] if remote else gain_parts, local.at[12])
     load_x = pltpu.make_async_copy(x, high, local.at[13])
     export = pltpu.make_async_copy(wq, wq_out, out_sem.at[0])
     store_u = pltpu.make_async_copy(low, u_out, out_sem.at[1])
     store_wn = pltpu.make_async_copy(wn, wn_out, out_sem.at[2])
+    store_h = [pltpu.make_async_copy(v, h_out.at[k], out_sem.at[7 + k]) for k, v in enumerate((high, low))]
+    export_wt = pltpu.make_async_copy(wt, wt_out, out_sem.at[9])
     store_gwo = pltpu.make_async_copy(mixed_all.at[pl.ds(0, D)], gwo_out, out_sem.at[3])
 
     def store_qkv(j):
@@ -365,6 +372,7 @@
     def _():
         load_x.start()
         if remote:
+            gain_piece[...] = gain_rows(ga[...], gm[...])
             barrier = pltpu.get_barrier_semaphore()
             for d in range(1, 8):
                 pl.semaphore_signal(barrier, inc=1, device_id=(rep, me ^ d), device_id_type=MESH)
@@ -372,13 +380,15 @@
             pl.semaphore_wait(barrier, 8)
             for d in range(1, 8):
                 gain_copy(d).start()
-        own_gain.start()
         for code in RELAYS[0][:EARLY]:
             relay(code)
-        own_gain.wait()
         if remote:
+            gain_parts[me] = gain_piece[...]
             for d in range(1, 8):
                 gain_copy(d).wait_recv()
+        else:
+            for d in range(8):
+                gain_parts[d] = gain_rows(ga[d : d + 1], gm[d : d + 1])
         gains[...] = spread(gain_parts)
         gains_out[...] = gains[...]
         load_x.wait()
@@ -405,8 +415,14 @@
             export.start()
         if at == p_h:
             store_u.wait()
+        if at == p_back:
+            export_wt.start()
+            for store in store_h:
+                store.wait()
         if at == p_in:
             store_wn.start()
+            for store in store_h:
+                store.start()
             for j in range(3):
                 store_qkv(j).wait()
 
@@ -429,7 +445,7 @@
             mask = permitted(lengths, t * (TILE // SPAN) + rr)
             probs, mixed = attend(lambda c: qa[rows, c : c + 128], mask)
             for p in range(6):
-                probs_out[rr, p] = probs[p]
+                probs_out[rr * SPAN : (rr + 1) * SPAN, p * 2 * SPAN : (p + 1) * 2 * SPAN] = probs[p]
                 mixed_all[rows, p * 128 : (p + 1) * 128] = mixed[p]
 
     @pl.when((step >= p_h) & (step < p_in))
@@ -466,21 +482,17 @@
         h = high[rows, :].astype(f32) + low[rows, :].astype(f32)
         n, r = moments(h)
         dm = dy[...]
-        y = h
         dw = None
         for j in range(wi.shape[0]):
             cols = slice(j * FC, (j + 1) * FC)
             w_out = flat(wt[j * per : (j + 1) * per])
-            y = y + nn(qa[rows, cols], w_out)
             dz = (nt(dm, w_out) * gelu_slope(zs[rows, cols].astype(f32))).astype(bf)
             zs[rows, cols] = dz
             add = nt(dz, flat(wi[j]))
             dw = add if dw is None else dw + add
         store_dz(t).start()
-        y_out[...] = y.astype(bf)
-        dh = dm.astype(f32) + norm_back(dw, n, r, gains[1:2])
-        dh_out[...] = dh
-        dt = dh.astype(bf)
+        dt = (dm.astype(f32) + norm_back(dw, n, r, gains[1:2])).astype(bf)
+        dh_out[...] = dt
         high[rows, :] = dt
         do_out[...] = nt(dt, flat(wo[...])).astype(bf)
 
@@ -490,6 +502,7 @@
         mixed_all[0:D, :] = gwo
         store_gwo.start()
         export.wait()
+        export_wt.wait()
         store_wn.wait()
         for t in range(tiles):
             store_a(t).wait()
@@ -502,10 +515,9 @@
         store_gwo.wait()
 
 
-def forward_and_mlp(remote, x, lengths, dy, gain, w_qkv, w_ao, w_in, w_out):
+def forward_and_mlp(remote, x, lengths, dy, ga, gm, w_qkv, w_ao, w_in, w_out):
     T, D = x.shape
     tiles = T // TILE
-    per = TILE // SPAN
     F = w_in.shape[-1]
     rows = D // 8
 
@@ -513,38 +525,34 @@
         return pl.BlockSpec(shape, lambda i: (jnp.clip(i - start, 0, tiles - 1),) + (0,) * (len(shape) - 1))
 
     p_back = P_B + tiles + 10
+    whole = pl.BlockSpec(ga.shape, lambda i: (0, 0))
     hbm = pl.BlockSpec(memory_space=pl.ANY)
 
     return pl.pallas_call(
         functools.partial(kernel_one, remote),
         name="forward_and_mlp",
         grid=(p_back + tiles,),
-        in_specs=[pl.BlockSpec(memory_space=pltpu.SMEM), hbm, tile_from(p_back, TILE, D), hbm, hbm, hbm, hbm, hbm],
+        in_specs=[pl.BlockSpec(memory_space=pltpu.SMEM), hbm, tile_from(p_back, TILE, D), whole, whole, hbm, hbm, hbm, hbm],
         out_specs=[
-            hbm, tile_from(P_B, per, 6, SPAN, 2 * SPAN), hbm, tile_from(p_back, TILE, D), hbm, hbm,
-            tile_from(p_back, TILE, D), tile_from(p_back, TILE, D), pl.BlockSpec((8, D), lambda i: (0, 0)), hbm, hbm,
+            hbm, tile_from(P_B, TILE, 2 * D), hbm, hbm, hbm, hbm,
+            tile_from(p_back, TILE, D), tile_from(p_back, TILE, D), pl.BlockSpec((8, D), lambda i: (0, 0)), hbm, hbm, hbm,
         ],
         out_shape=[
-            sds(T, 3 * D), sds(T // SPAN, 6, SPAN, 2 * SPAN), sds(T, D),
-            sds(T, D), sds(T, D), sds(2, T, F), sds(T, D, dtype=f32), sds(T, D), sds(8, D, dtype=f32), sds(D, D), sds(3, 8, rows, D),
+            sds(T, 3 * D), sds(T, 2 * D), sds(T, D),
+            sds(2, T, D), sds(T, D), sds(2, T, F), sds(T, D), sds(T, D), sds(8, D, dtype=f32), sds(D, D), sds(3, 8, rows, D), sds(8, F // 8, D),
         ],
         scratch_shapes=[
             pltpu.VMEM((3, 8, rows, D), bf), pltpu.VMEM((8, rows, D), bf), pltpu.VMEM((F // FC, 8, rows, FC), bf),
-            pltpu.VMEM((8, F // 8, D), bf), pltpu.VMEM((8, 16, 128), bf), pltpu.VMEM((8, D), f32), pltpu.VMEM((T, D), bf),
+            pltpu.VMEM((8, F // 8, D), bf), pltpu.VMEM((16, 128), bf), pltpu.VMEM((8, 16, 128), bf), pltpu.VMEM((8, D), f32), pltpu.VMEM((T, D), bf),
             pltpu.VMEM((T, D), bf), pltpu.VMEM((T, F), bf), pltpu.VMEM((T, F), bf), pltpu.VMEM((T, D), bf), pltpu.VMEM((T, D), bf),
             pltpu.SemaphoreType.DMA((12,)), pltpu.SemaphoreType.DMA((12, len(ARRIVALS))), pltpu.SemaphoreType.DMA((8,)), pltpu.SemaphoreType.DMA((8,)),
-            pltpu.SemaphoreType.DMA((14,)), pltpu.SemaphoreType.DMA((7,)), pltpu.SemaphoreType.DMA((tiles,)), pltpu.SemaphoreType.DMA((tiles,)),
+            pltpu.SemaphoreType.DMA((14,)), pltpu.SemaphoreType.DMA((10,)), pltpu.SemaphoreType.DMA((tiles,)), pltpu.SemaphoreType.DMA((tiles,)),
         ],
         cost_estimate=pl.CostEstimate(flops=12 * T * D * D + 8 * T * D * F + 6 * T * D * D, bytes_accessed=90 << 20, transcendentals=0),
         compiler_params=pltpu.CompilerParams(
             vmem_limit_bytes=VMEM, has_side_effects=remote, collective_id=1 if remote else None
         ),
-    )(lengths, x, dy, gain, w_qkv, w_ao, w_in, w_out)
-
-
-def gain_piece(gain_attn, gain_mlp):
-    pair = jnp.stack([gain_attn, gain_mlp])
-    return jnp.pad(pair, ((0, 14), (0, 128 - pair.shape[1])))
+    )(lengths.T, x, dy, ga, gm, w_qkv, w_ao, w_in, w_out)
 
 
 CHUNK = 96
@@ -552,13 +560,15 @@
 RING = 6
 N_WIDE = 12
 P_IN, P_OUT, P_ATT = 0, 4, 8
-P_DX = P_ATT + 18
-REUSE = {P_ATT + 8: 0, P_ATT + 14: 1}
+P_DX = P_ATT + 9
+P_Y = P_DX + 4
+STEPS = P_Y + 4
+BLOCK = 512
+REUSE = {P_ATT + 5: [0], P_ATT + 8: [1], P_DX + 2: [2, 3, 4, 5]}
 START = [
-    [0, 1, 3, 6, 9, 12, 21], [2, 3, 7, 10, 14, 17, 21], [5, 6, 8, 12, 16, 19, 36], [3, 5, 8, 11, 18, 20, 28],
-    [4, 6, 10, 13, 19, 22, 26], [10, 12, 15, 17, 20, 23, 41], [8, 10, 13, 16, 21, 25, 28], [11, 15, 18, 21, 23, 27, 40],
-    [14, 19, 22, 24, 26, 29, 35], [11, 14, 17, 19, 22, 26, 29], [14, 16, 19, 22, 25, 27, 34], [17, 21, 24, 25, 28, 30, 42],
-    [21, 22, 25, 27, 29, 31, 38], [24, 25, 27, 29, 31, 33, 40], [26, 27, 29, 30, 32, 38, 39],
+    [1, 2, 5, 7, 10, 13, 15], [1, 3, 7, 9, 12, 14, 19], [2, 4, 7, 9, 12, 15, 25], [3, 5, 8, 10, 13, 16, 20],
+    [6, 8, 10, 12, 14, 16, 26], [8, 9, 12, 14, 16, 18, 27], [8, 11, 13, 15, 17, 19, 29], [11, 12, 15, 17, 19, 21, 24],
+    [8, 10, 13, 16, 18, 20, 25], [12, 14, 16, 18, 20, 22, 28], [15, 16, 19, 20, 22, 23, 32], [17, 18, 20, 21, 22, 24, 28],
 ]
 RECEIVE = {"s1": 0, "s2x": 1, "s2y": 1, "s3y": 2, "s3x": 2, "z1": 3, "z2": 4, "z3": 3}
 
@@ -568,17 +578,13 @@
 
 
 class Reduce:
-    def __init__(self, n, grads, bufs, send, recv, place):
-        self.n = n
-        k = self.k = n if n < 9 else 9 + (n - 9) // 2
-        self.cols = cols = pl.ds(0, WIDE) if n < 9 else pl.ds((n - 9) % 2 * (WIDE // 2), WIDE // 2)
+    def __init__(self, k, grads, bufs, send, recv, place):
+        self.n = k
         first, x2, y2, y3, x3, outer, inner, out = bufs
         r = k % RING
-        self.g = grads.at[slot_of(k), :, :, :, :, cols]
-        self.first = first.at[r, :, :, :, cols]
-        self.x2, self.y2 = x2.at[r, :, :, cols], y2.at[r, :, :, cols]
-        self.x3, self.y3 = x3.at[k, :, cols], y3.at[k, :, cols]
-        self.outer, self.inner, self.out = outer.at[k, :, cols], inner.at[k, :, cols], out.at[k, :, cols]
+        self.g = grads.at[slot_of(k)]
+        self.first, self.x2, self.y2 = first.at[r], x2.at[r], y2.at[r]
+        self.x3, self.y3, self.outer, self.inner, self.out = x3.at[k], y3.at[k], outer.at[k], inner.at[k], out.at[k]
         self.send, self.recv = send, recv
         self.y, self.x, self.c, self.me, self.rep = place
         self.is_inner = (self.rep == 1) | (self.rep == 2)
@@ -660,17 +666,17 @@
 
 
 def part_of(e):
-    return lax.div(e, 3), jnp.minimum(lax.rem(e, 3), 1), lax.rem(e, 3) == 2
+    return 2 * lax.div(e, 3) + jnp.minimum(lax.rem(e, 3), 1), lax.rem(e, 3) == 2
 
 
 def kernel_two(
-    gwo_in, wn, dm, u, wq, gains, za, qs, ks, vs, probs, do, x, dh,
-    dx_out, out_hbm,
-    out, big_a, big_b, wq_s, dqkv, grads, first, x2, y2, y3, x3, outer, inner, send, recv, local,
+    gwo_in, wn, dm, u, wq, wt, gains, za, qkv, probs, do, x, dh, h,
+    dx_out, y_out, out_hbm,
+    out, big_a, big_b, wq_s, dqkv, grads, first, x2, y2, y3, x3, outer, inner, stream, halves, result,
+    send, recv, local, load_sem, store_sem,
 ):
     step = pl.program_id(0)
     T, D = big_a.shape
-    steps = P_DX + T // TILE
     me, rep = lax.axis_index("fsdp"), lax.axis_index("rep")
     place = (me // 4, (me // 2) % 2, me % 2, me, rep)
     bufs = (first, x2, y2, y3, x3, outer, inner, out)
@@ -681,16 +687,33 @@
     load_u = pltpu.make_async_copy(u, big_a, local.at[3])
     load_wq = pltpu.make_async_copy(wq, wq_s, local.at[4])
     store_out = pltpu.make_async_copy(out, out_hbm, local.at[5])
-
-    @pl.when(step == 0)
-    def _():
-        load_wn.start()
-        load_gwo.start()
-        barrier = pltpu.get_barrier_semaphore()
-        for to in ((rep, me ^ 1), (rep, me ^ 2), (rep, me ^ 4), (rep ^ 1, me), (rep ^ 3, me)):
-            pl.semaphore_signal(barrier, inc=1, device_id=to, device_id_type=MESH)
-        pl.semaphore_wait(barrier, 5)
-        load_gwo.wait()
+    load_wt = pltpu.make_async_copy(wt, grads.at[pl.ds(2, 4)], local.at[6])
+
+    def loads(at):
+        s = at % 2
+        to = stream.at[s]
+        if at < P_ATT:
+            pairs = [(za.at[at // 4, :, pl.ds(at % 4 * WIDE, WIDE)], to)]
+        elif at < P_DX:
+            e = at - P_ATT
+            if e % 3 == 2:
+                return []
+            p = e // 3 * 2 + e % 3
+            pairs = [(qkv.at[:, pl.ds(j * D + p * 128, 128)], to.at[:, pl.ds(j * 128, 128)]) for j in range(3)]
+            pairs.append((do.at[:, pl.ds(p * 128, 128)], to.at[:, pl.ds(384, 128)]))
+            pairs.append((probs.at[:, pl.ds(p * 256, 256)], to.at[:, pl.ds(512, 256)]))
+        elif at < P_Y:
+            rows = pl.ds((at - P_DX) * BLOCK, BLOCK)
+            pairs = [(x.at[rows], to.at[pl.ds(0, BLOCK)]), (dh.at[rows], to.at[pl.ds(BLOCK, BLOCK)])]
+        else:
+            rows = pl.ds((at - P_Y) * BLOCK, BLOCK)
+            pairs = [(za.at[1, rows, pl.ds(j * WIDE, WIDE)], to.at[pl.ds(j * BLOCK, BLOCK)]) for j in range(4)]
+            pairs.append((h.at[:, rows], halves.at[s]))
+        return [pltpu.make_async_copy(src, dst, load_sem.at[s, k]) for k, (src, dst) in enumerate(pairs)]
+
+    def store(at):
+        to, t = (dx_out, at - P_DX) if at < P_Y else (y_out, at - P_Y)
+        return pltpu.make_async_copy(result.at[at % 2], to.at[pl.ds(t * BLOCK, BLOCK)], store_sem.at[at % 2])
 
     acts = {}
     for n, starts in enumerate(START):
@@ -702,12 +725,27 @@
             chunks[n].stage(s)
 
     def begin(at):
+        if at == 0:
+            load_wn.start()
+            for load in loads(0):
+                load.start()
+            barrier = pltpu.get_barrier_semaphore()
+            for to in ((rep, me ^ 1), (rep, me ^ 2), (rep, me ^ 4), (rep ^ 1, me), (rep ^ 3, me)):
+                pl.semaphore_signal(barrier, inc=1, device_id=to, device_id_type=MESH)
+            pl.semaphore_wait(barrier, 5)
+            load_wn.wait()
+        for load in loads(at):
+            load.wait()
+        if at == 0:
+            load_gwo.start()
+        if at + 1 < STEPS:
+            for load in loads(at + 1):
+                load.start()
+        if at == 1:
+            load_dm.start()
+            load_gwo.wait()
         if at in acts:
             act(at)
-        if at == 0:
-            load_wn.wait()
-        if at == 1:
-            load_dm.start()
         if at == P_OUT:
             load_u.start()
             load_dm.wait()
@@ -716,139 +754,189 @@
         if at == P_ATT + 2:
             load_u.wait()
             load_wq.wait()
-        if at in REUSE:
-            chunks[REUSE[at]].sent()
-
-    dispatch(step, {at: functools.partial(begin, at) for at in {*acts, *REUSE, 0, 1, P_OUT, P_OUT + 1, P_ATT + 2} if at < steps})
+        for k in REUSE.get(at, []):
+            chunks[k].sent()
+        if at == P_DX + 2:
+            load_wt.start()
+        if at == P_Y:
+            load_wt.wait()
+        if at >= P_DX + 2:
+            store(at - 2).wait()
+
+    dispatch(step, {at: functools.partial(begin, at) for at in range(STEPS)})
+
+    slot = lax.rem(step, 2)
 
     @pl.when(step < P_OUT)
     def _():
-        g = tn(big_a[...], za[0]).astype(bf)
+        g = tn(big_a[...], stream[slot]).astype(bf)
         grads[1 + step] = g.reshape(2, 2, 2, CHUNK, WIDE)
 
     @pl.when((step >= P_OUT) & (step < P_ATT))
     def _():
         j = step - P_OUT
-        g = tn(za[0], big_b[...]).astype(bf).reshape(2, 4, CHUNK, WIDE)
+        g = tn(stream[slot], big_b[...]).astype(bf).reshape(2, 4, CHUNK, WIDE)
         for part in range(4):
             grads[5 + part, j // 2, j % 2] = g[:, part]
 
-    pair, half, product = part_of(step - P_ATT)
+    pair, product = part_of(step - P_ATT)
     attention = (step >= P_ATT) & (step < P_DX)
 
     @pl.when(attention & jnp.logical_not(product))
     def _():
-        for rr in range(probs.shape[0]):
+        for rr in range(T // SPAN):
             rows = slice(rr * SPAN, (rr + 1) * SPAN)
-            to = pl.ds(pl.multiple_of((half * probs.shape[0] + rr) * SPAN, SPAN), SPAN)
-            back = attend_back(qs[rows], ks[rows], vs[rows], probs[rr, 0], do[rows])
+            q2, k2, v2, do2 = (stream[slot, rows, j * 128 : (j + 1) * 128] for j in range(4))
+            back = attend_back(q2, k2, v2, stream[slot, rows, 512:768], do2)
             for j in range(3):
-                dqkv[pair, to, j * 128 : (j + 1) * 128] = back[j]
+                to_cols = pl.ds(pl.multiple_of(lax.rem(pair, 2) * (WIDE // 2) + j * 128, 128), 128)
+                dqkv[lax.div(pair, 2), rows, to_cols] = back[j]
 
     @pl.when(attention & product)
     def _():
-        k = pair // 2
-        g = tn(big_a[...], dqkv[pair]).astype(bf)
-        cols = pl.ds(pl.multiple_of(lax.rem(pair, 2) * (WIDE // 2), WIDE // 2), WIDE // 2)
-        grads[jnp.where(k == 0, 9, k - 1), :, :, :, :, cols] = g.reshape(2, 2, 2, CHUNK, WIDE // 2)
-
-    @pl.when(step >= P_DX)
-    def _():
-        rows = pl.ds(pl.multiple_of((step - P_DX) * TILE, TILE), TILE)
-        n, r = moments(x[...].astype(f32))
-        d = jnp.concatenate([dqkv[p, rows, j * 128 : (j + 1) * 128] for j in range(3) for p in range(D // 128)], axis=1)
-        du = sum(nt(d[:, j * D : (j + 1) * D], flat(wq_s[j])) for j in range(3))
-        dx_out[...] = (dh[...] + norm_back(du, n, r, gains[0:1])).astype(bf)
-
-    @pl.when(step == steps - 1)
+        k = lax.div(pair, 2)
+        g = tn(big_a[...], dqkv[k]).astype(bf)
+        grads[jnp.where(k == 0, 9, k - 1)] = g.reshape(2, 2, 2, CHUNK, WIDE)
+
+    @pl.when((step >= P_DX) & (step < P_Y))
+    def _():
+        for part in range(BLOCK // TILE):
+            here = slice(part * TILE, (part + 1) * TILE)
+            rows = pl.ds(pl.multiple_of((step - P_DX) * BLOCK + part * TILE, TILE), TILE)
+            n, r = moments(stream[slot, here].astype(f32))
+            du = 0.0
+            for j in range(3):
+                at = [(p // 2, (p % 2) * (WIDE // 2) + j * 128) for p in range(D // 128)]
+                du = du + nt(jnp.concatenate([dqkv[k, rows, c : c + 128] for k, c in at], axis=1), flat(wq_s[j]))
+            dt = stream[slot, BLOCK + part * TILE : BLOCK + (part + 1) * TILE].astype(f32)
+            result[slot, here] = (dt + norm_back(du, n, r, gains[0:1])).astype(bf)
+        for at in range(P_DX, P_Y):
+            @pl.when(step == at)
+            def _(at=at):
+                store(at).start()
+
+    @pl.when(step >= P_Y)
+    def _():
+        y = halves[slot, 0].astype(f32) + halves[slot, 1].astype(f32)
+        for j in range(4):
+            y = y + nn(stream[slot, j * BLOCK : (j + 1) * BLOCK], grads[2 + j].reshape(WIDE, WIDE))
+        result[slot] = y.astype(bf)
+        for at in range(P_Y, STEPS):
+            @pl.when(step == at)
+            def _(at=at):
+                store(at).start()
+
+    @pl.when(step == STEPS - 1)
     def _():
         for at in sorted(acts):
-            if at >= steps:
+            if at >= STEPS:
                 act(at)
         store_out.start()
         for n in range(len(START)):
-            if n not in REUSE.values():
+            if n not in sum(REUSE.values(), []):
                 chunks[n].sent()
             chunks[n].sum_sent()
+        for at in (STEPS - 2, STEPS - 1):
+            store(at).wait()
         store_out.wait()
 
 
-def gradients(gwo, wn, dy, u, wq, gains, za, qkv, probs, do, x, dh):
+def gradients(gwo, wn, dy, u, wq, wt, gains, za, qkv, probs, do, x, dh, h):
     T, D = x.shape
-    tiles = T // TILE
-    steps = P_DX + tiles
-    pairs = D // 128
     hbm = pl.BlockSpec(memory_space=pl.ANY)
-
-    def tile_from(start, *shape):
-        return pl.BlockSpec(shape, lambda i: (jnp.clip(i - start, 0, tiles - 1),) + (0,) * (len(shape) - 1))
-
-    def part(i):
-        return part_of(jnp.clip(i - P_ATT, 0, 3 * pairs - 1))[:2]
-
-    def head_cols(which):
-        def index(i):
-            pair, half = part(i)
-            return half, which * pairs + pair
-
-        return pl.BlockSpec((T // 2, 128), index)
-
-    def probs_index(i):
-        pair, half = part(i)
-        return half, pair, 0, 0
-
     wide = lambda *shape: pltpu.VMEM(shape + (WIDE,), bf)
     return pl.pallas_call(
         kernel_two,
         name="gradients",
-        grid=(steps,),
-        in_specs=[
-            hbm, hbm, hbm, hbm, hbm, pl.BlockSpec((8, D), lambda i: (0, 0)),
-            pl.BlockSpec((1, T, WIDE), lambda i: (jnp.where(i < P_OUT, 0, 1), 0, jnp.where(i < P_OUT, i, jnp.minimum(i - P_OUT, 3)))),
-            head_cols(0), head_cols(1), head_cols(2), pl.BlockSpec((T // SPAN // 2, 1, SPAN, 2 * SPAN), probs_index), head_cols(0),
-            tile_from(P_DX, TILE, D), tile_from(P_DX, TILE, D),
-        ],
-        out_specs=[tile_from(P_DX, TILE, D), hbm],
-        out_shape=[sds(T, D), sds(N_WIDE, CHUNK, WIDE)],
+        grid=(STEPS,),
+        in_specs=[hbm] * 6 + [pl.BlockSpec((8, D), lambda i: (0, 0))] + [hbm] * 7,
+        out_specs=[hbm] * 3,
+        out_shape=[sds(T, D), sds(T, D), sds(N_WIDE, CHUNK, WIDE)],
         scratch_shapes=[
-            wide(N_WIDE, CHUNK), pltpu.VMEM((T, D), bf), pltpu.VMEM((T, D), bf), pltpu.VMEM(wq.shape, bf),
-            pltpu.VMEM((pairs, T, 3 * 128), bf), wide(10, 2, 2, 2, CHUNK), wide(RING, 2, 2, CHUNK), wide(RING, 2, CHUNK // 2),
+            wide(N_WIDE, CHUNK), wide(T), wide(T), pltpu.VMEM(wq.shape, bf), wide(3, T),
+            wide(10, 2, 2, 2, CHUNK), wide(RING, 2, 2, CHUNK), wide(RING, 2, CHUNK // 2),
             wide(RING, 2, CHUNK // 2), wide(N_WIDE, CHUNK // 2), wide(N_WIDE, CHUNK // 2), wide(N_WIDE, CHUNK), wide(N_WIDE, CHUNK),
-            pltpu.SemaphoreType.DMA((len(START), 2)), pltpu.SemaphoreType.DMA((len(START), 5)),
-            pltpu.SemaphoreType.DMA((6,)),
+            wide(2, T), wide(2, 2, BLOCK), wide(2, BLOCK),
+            pltpu.SemaphoreType.DMA((len(START), 2)), pltpu.SemaphoreType.DMA((len(START), 5)), pltpu.SemaphoreType.DMA((7,)),
+            pltpu.SemaphoreType.DMA((2, 5)), pltpu.SemaphoreType.DMA((2,)),
         ],
         cost_estimate=pl.CostEstimate(flops=8 * T * D * D + 4 * T * D * 4 * D + 20 * T * D * D, bytes_accessed=90 << 20, transcendentals=0),
         compiler_params=pltpu.CompilerParams(vmem_limit_bytes=VMEM, has_side_effects=True, collective_id=2),
-    )(gwo.reshape(2, 2, 2, CHUNK, WIDE), wn, dy, u, wq, gains, za, qkv, qkv, qkv, probs, do, x, dh)
+    )(gwo.reshape(2, 2, 2, CHUNK, WIDE), wn, dy, u, wq, wt.reshape(4, 2, 2, 2, CHUNK, WIDE), gains, za, qkv, probs, do, x, dh, h)
+
+
+def kernel_finish(sums, wq, wi, ga, gm, y, dx, y_out, dx_out, gq, gwo, gwi, gwt, gg1, gg2, hold, sem):
+    parts = sem.shape[2]
+    n = y.shape[0] // parts
+    moves = []
+    for p in range(parts):
+        for k, (src, dst) in enumerate(((y, y_out), (dx, dx_out))):
+            rows = pl.ds(p * n, n)
+            there = pltpu.make_async_copy(src.at[rows], hold.at[k, rows], sem.at[0, k, p])
+            moves.append((there, pltpu.make_async_copy(hold.at[k, rows], dst.at[rows], sem.at[1, k, p])))
+            there.start()
+    D = gwo.shape[1]
+    gwo[...] = sums[0].astype(f32)
+    for j in range(4):
+        gwi[:, j * D : (j + 1) * D] = sums[1 + j].astype(f32)
+        gwt[j * CHUNK : (j + 1) * CHUNK, :] = sums[5 + j].astype(f32)
+    for pair in range(D // 128):
+        for j in range(3):
+            cols = (pair % 2) * (WIDE // 2) + j * 128
+            gq[:, j * D + pair * 128 : j * D + pair * 128 + 128] = sums[9 + pair // 2, :, cols : cols + 128].astype(f32)
+    for there, out in moves:
+        there.wait()
+        out.start()
+    for grad, w, gain, out in ((gq, wq, ga, gg1), (gwi, wi, gm, gg2)):
+        acc = jnp.zeros((CHUNK, 128), f32)
+        for c in range(0, w.shape[1], 128):
+            acc = acc + w[:, c : c + 128].astype(f32) * grad[:, c : c + 128]
+        out[...] = jnp.sum(acc.T, axis=0, keepdims=True) / gain[...].astype(f32)
+    for _, out in moves:
+        out.wait()
+
+
+def finish(sums, w_qkv, w_mlp_in, gain_attn, gain_mlp, y, dx):
+    rows, D = w_qkv.shape[0], w_qkv.shape[1] // 3
+    vmem, hbm = pl.BlockSpec(memory_space=pltpu.VMEM), pl.BlockSpec(memory_space=pl.ANY)
+    fs = functools.partial(sds, dtype=f32)
+    y, dx, gq, gwo, gwi, gwt, gg1, gg2 = pl.pallas_call(
+        kernel_finish,
+        name="finish",
+        in_specs=[vmem] * 5 + [hbm] * 2,
+        out_specs=[hbm] * 2 + [vmem] * 6,
+        out_shape=[sds(*y.shape), sds(*dx.shape), fs(rows, 3 * D), fs(rows, D), fs(rows, 4 * D), fs(4 * rows, D), fs(1, rows), fs(1, rows)],
+        scratch_shapes=[pltpu.VMEM((2, *y.shape), bf), pltpu.SemaphoreType.DMA((2, 2, 4))],
+        cost_estimate=pl.CostEstimate(flops=1 << 20, bytes_accessed=20 << 20, transcendentals=0),
+        compiler_params=pltpu.CompilerParams(vmem_limit_bytes=VMEM),
+    )(sums, w_qkv, w_mlp_in, gain_attn.reshape(1, rows), gain_mlp.reshape(1, rows), y, dx)
+    return y, dx, gg1.reshape(rows), gq, gwo, gg2.reshape(rows), gwi, gwt
 
 
 def shards(x, lengths, segments, gain_attn, w_qkv, w_attn_out, gain_mlp, w_mlp_in, w_mlp_out, dy):
     D = x.shape[1]
     remote = lax.axis_size("fsdp") == 8 and lax.axis_size("rep") == 4
-    gain = gain_piece(gain_attn, gain_mlp)
+    ga, gm = gain_attn.reshape(1, -1), gain_mlp.reshape(1, -1)
     weights = (w_qkv, w_attn_out, w_mlp_in, w_mlp_out)
     if not remote:
         weights = tuple(lax.all_gather(v, "fsdp", axis=0, tiled=True) for v in weights)
         weights = tuple(v.reshape(8, v.shape[0] // 8, v.shape[1]) for v in weights)
-        gains = [lax.all_gather(v, "fsdp", axis=0, tiled=True).reshape(8, -1) for v in (gain_attn, gain_mlp)]
-        gain = jnp.stack([gain_piece(a, b) for a, b in zip(*gains)])
-    qkv, probs, u, y, wn, za, dh, do, gains, gwo, wq = forward_and_mlp(remote, x, lengths, dy, gain, *weights)
+        ga, gm = (lax.all_gather(v, "fsdp", axis=0, tiled=True).reshape(8, -1) for v in (gain_attn, gain_mlp))
+    qkv, probs, u, h, wn, za, dh, do, gains, gwo, wq, wt = forward_and_mlp(remote, x, lengths, dy, ga, gm, *weights)
     if remote:
-        dx, sums = gradients(gwo, wn, dy, u, wq, gains, za, qkv, probs, do, x, dh)
-        sums = sums.astype(f32)
-        wide = lambda v: v.transpose(1, 0, 2).reshape(v.shape[1], -1)
-        gq = sums[9:12].reshape(3, CHUNK, 2, 3, 128).transpose(1, 3, 0, 2, 4).reshape(CHUNK, 3 * D)
-        gwo, gwi, gwt = sums[0], wide(sums[1:5]), sums[5:9].reshape(-1, D)
-    else:
-        scatter = lambda v: lax.psum_scatter(v, "fsdp", scatter_dimension=0, tiled=True)
-        gwt = scatter(weight_grad(za[1], dy, "mlp_out_grad", 768, bf, "left"))
-        gwi = scatter(weight_grad(wn, za[0], "mlp_in_grad", 768))
-        gwo = scatter(gwo)
-        dqkv = attention_back(qkv, probs, do)
-        gq = scatter(weight_grad(u, dqkv, "qkv_grad", 768))
-        dx = input_grad(x, dqkv, dh, gains[0:1], wq.transpose(1, 2, 0, 3).reshape(D, 3 * D))
-        gwt, gwi, gwo, gq = lax.psum((gwt, gwi, gwo, gq), "rep")
-        gwt, gwi, gwo, gq = (v.astype(f32) for v in (gwt, gwi, gwo, gq))
+        dx, y, sums = gradients(gwo, wn, dy, u, wq, wt, gains, za, qkv, probs, do, x, dh, h)
+        return finish(sums, w_qkv, w_mlp_in, gain_attn, gain_mlp, y, dx)
+    scatter = lambda v: lax.psum_scatter(v, "fsdp", scatter_dimension=0, tiled=True)
+    gwt = scatter(weight_grad(za[1], dy, "mlp_out_grad", 768, bf, "left"))
+    gwi = scatter(weight_grad(wn, za[0], "mlp_in_grad", 768))
+    gwo = scatter(gwo)
+    dqkv = attention_back(qkv, probs, do)
+    gq = scatter(weight_grad(u, dqkv, "qkv_grad", 768))
+    dx = input_grad(x, dqkv, dh.astype(f32), gains[0:1], wq.transpose(1, 2, 0, 3).reshape(D, 3 * D))
+    y = jnp.sum(h.astype(f32), axis=0) + jnp.dot(za[1], wt.reshape(-1, D), preferred_element_type=f32)
+    y = y.astype(bf)
+    gwt, gwi, gwo, gq = lax.psum((gwt, gwi, gwo, gq), "rep")
+    gwt, gwi, gwo, gq = (v.astype(f32) for v in (gwt, gwi, gwo, gq))
     gg1 = jnp.sum(w_qkv.astype(f32) * gq, axis=1) / gain_attn.astype(f32)
     gg2 = jnp.sum(w_mlp_in.astype(f32) * gwi, axis=1) / gain_mlp.astype(f32)
     return y, dx, gg1, gq, gwo, gg2, gwi, gwt

time: 230 us -> 204 us (0.89)
  local copies, waits for them, and re-layouts: 16.5 us -> 0 us
  Pallas kernels: 209 us -> 203 us
  other arithmetic: 2.55 us -> 0 us
    pallas_call x1, Pallas kernels: 115 us -> 106 us  [forward_and_mlp(): pl.pallas_call(functools.partial(kernel_one, remote), name='forward_and_m...]
    unnamed x22 -> x0, local copies, waits for them, and re-layouts: 7.55 us -> none
    reshape x3 -> x0, local copies, waits for them, and re-layouts: 3.71 us -> none  [the longest x2 3.6 us: shards(): sums[9:12].reshape(3, CHUNK, 2, 3, 128).transpose(1, 3, 0, 2, 4)]
    pallas_call x1 -> x2, Pallas kernels: 94.1 us -> 97.8 us  [the longest x1 88.8 us: gradients(): pl.pallas_call(kernel_two, name='gradients', grid=(STEPS,), in_specs=[hbm...]
    slice x2 -> x0, local copies, waits for them, and re-layouts: 3.1 us -> none  [the longest x1 1.99 us: shards(): sums[9:12].reshape(3, CHUNK, 2, 3, 128).transpose(1, 3, 0, 2, 4)]
where the time goes in v5:
time: 204 us
  Pallas kernels  203 us (100%)
    pallas_call x1, Pallas kernels, forward_and_mlp(): pl.pallas_call(functools.partial(kernel_one, remote), name='forward_and_m...  106 us
    pallas_call x1, Pallas kernels, gradients(): pl.pallas_call(kernel_two, name='gradients', grid=(STEPS,), in_specs=[hbm...  88.8 us
    pallas_call x1, Pallas kernels, finish(): pl.pallas_call(kernel_finish, name='finish', in_specs=[vmem] * 5 + [hbm]...  9.06 us

profile of v5, /device:TPU:0, one launch (start us, length us, event | category | flops | bytes accessed | tf_op | source)
XLA Modules:
  0.0 204.2 jit_solution(732330587944075956)
XLA Ops:
  0.6 105.5 %forward_and_mlp.1 = (bf16[2048,2304]{1,0:T(8,128)(2,1)}, bf16[2048,1536]{1,0:T(8,128)(2,1)}, bf16[2048,768]{1,0:T(8,128)(2,1)}, bf16[2,2048,768]{2,1,0:T(8,128)...) custom-call(s32[4,16]{1,0:T(4,128)} %bitcast.11, ...), custom_call_target="tpu_custom_call" | custom-call | flops 60397977600 | bytes 94371840 | tf_op jit(solution)/shard_map/forward_and_mlp/pallas_call | solution.py:531
  106.2 88.8 %gradients.1 = (bf16[2048,768]{1,0:T(8,128)(2,1)}, bf16[2048,768]{1,0:T(8,128)(2,1)}, bf16[12,96,768]{2,1,0:T(8,128)(2,1)}) custom-call(bf16[2,2,2,96,768]{4,3,2,1,0:T(8,128)(2,1)} %bitcast.15, bf16[2048,768]{1,0:T(8,128)(2,1)} %get-tuple-element.32.wn, bf16[2048,768]{1,0:T(8,128)(2,1)} %dm.1, bf16[2048,768]{1,0:T(8,128)(2,1)} %get-tuple-element.33.u, ...), custom_call_target="tpu_custom_call" | custom-call | flops 53150220288 | bytes 94371840 | tf_op jit(solution)/shard_map/gradients/pallas_call | solution.py:848
  194.9 9.1 %finish.1 = (bf16[2048,768]{1,0:T(8,128)(2,1)}, bf16[2048,768]{1,0:T(8,128)(2,1)}, f32[96,2304]{1,0:T(8,128)}, f32[96,768]{1,0:T(8,128)}, f32[96,3072]{1,0:T(8,1...) custom-call(bf16[12,96,768]{2,1,0:T(8,128)(2,1)} %get-tuple-element.43.sums, bf16[96,2304]{1,0:T(8,128)(2,1)} %wq.1, ...), custom_call_target="tpu_custom_call" | custom-call | flops 1048576 | bytes 20971520 | tf_op jit(solution)/shard_map/finish/pallas_call | solution.py:903

commit v6 on v5

--- a/solution.py
+++ b/solution.py
@@ -190,6 +190,7 @@
 MESH = pl.DeviceIdType.MESH
 D_MODEL = 768
 P_B = 3
+BACK = 256
 EARLY = 6
 MESSAGES = {
     "x0s": (0, 2, 0, "mine", None), "y0s": (0, 4, 0, "mine", None), "x0c": (0, 2, 0, "middle", None), "y0c": (0, 4, 0, "middle", None),
@@ -202,22 +203,24 @@
 }
 ARRIVALS = [None, "x0s", "y0s", "x0c", "y0c", "xf", "yf", "xz", "yz", "dz"]
 RELAYS = {
-    0: [0, 10, 1, 2, 20, 3, 4, 11, 12, 7, 13, 14, 8, 21, 5, 17, 30, 23, 22, 18, 6, 24, 27, 16, 15, 9, 40, 31, 25, 28, 33, 32],
-    1: [19, 26, 34, 37, 41, 42, 29, 50, 60, 43, 44, 38, 35, 70],
-    2: [36, 45, 47, 51, 52, 48, 80],
-    3: [53, 54, 39, 61, 62, 63, 64, 49, 90],
-    4: [46, 72, 57, 71, 74, 58],
-    5: [73, 55, 67, 81, 82],
-    6: [68, 83, 84, 78, 100, 56, 65],
-    7: [77, 66, 92, 59, 110],
-    8: [91, 94, 87, 93, 75, 88],
-    9: [76, 85, 69, 86, 102],
-    10: [98, 101, 104, 97, 103],
-    11: [112, 79, 111, 114, 89],
-    12: [113, 95, 108, 96, 105, 107, 106],
-    13: [115, 118, 116, 117],
-    14: [99, 109],
-    15: [119],
+    0: [0, 10, 1, 2, 20, 3, 4, 11, 12, 13, 14, 7, 21, 5, 8, 30, 23, 22, 17, 6, 24, 18, 16, 15, 40, 27, 31, 25, 9, 33, 32, 50, 28, 26, 34, 19],
+    1: [41, 42, 37, 43, 44, 29, 60, 70],
+    2: [51, 35, 38, 53, 52, 36, 54, 80],
+    3: [47, 45, 46, 48, 62, 61, 64, 63, 90],
+    4: [57, 72, 71, 100, 39, 74],
+    5: [73, 58, 55, 56],
+    6: [49, 82, 81, 68, 110, 84, 83],
+    7: [67, 65, 66],
+    8: [78, 92, 91, 77, 94],
+    9: [93, 59, 75, 101],
+    10: [88, 102, 103, 87],
+    11: [104, 76, 69, 85, 111],
+    12: [98, 112, 113, 97, 114, 86],
+    13: [79, 95, 96, 107, 105, 106],
+    14: [108, 115, 89, 116],
+    15: [117, 118],
+    16: [99, 109],
+    17: [119],
 }
 
 
@@ -321,7 +324,7 @@
     tiles = T // TILE
     p_h = P_B + tiles
     p_in, p_back = p_h + 2, p_h + 10
-    steps = p_back + tiles
+    steps = p_back + T // BACK
     me, rep = lax.axis_index("fsdp"), lax.axis_index("rep")
     part = lambda j: pl.ds(j * D, D)
     rows_of_part = lambda j: pl.ds(j * 96, 96)
@@ -363,7 +366,7 @@
         return pltpu.make_async_copy(qa.at[place], za_out.at[(1, *place)], a_sem.at[e])
 
     def store_dz(t):
-        return pltpu.make_async_copy(zs.at[rows_at(t, TILE)], za_out.at[0, rows_at(t, TILE)], dz_sem.at[t])
+        return pltpu.make_async_copy(zs.at[rows_at(t, BACK)], za_out.at[0, rows_at(t, BACK)], dz_sem.at[t])
 
     def relay(code):
         blocks[code // 10].relay(ARRIVALS[code % 10])
@@ -465,7 +468,7 @@
         j, half = lax.div(e, 2), lax.rem(e, 2)
         cols = pl.ds(pl.multiple_of(j * FC, FC), FC)
         w = flat(wi[j])
-        block = 2 * TILE
+        block = TILE
         for s in range(T // 2 // block):
             rows = rows_at(half * (T // 2 // block) + s, block)
             z = nn(wn[rows, :], w)
@@ -478,7 +481,7 @@
     @pl.when(step >= p_back)
     def _():
         t = step - p_back
-        rows = rows_at(t, TILE)
+        rows = rows_at(t, BACK)
         h = high[rows, :].astype(f32) + low[rows, :].astype(f32)
         n, r = moments(h)
         dm = dy[...]
@@ -504,8 +507,9 @@
         export.wait()
         export_wt.wait()
         store_wn.wait()
-        for t in range(tiles):
+        for t in range(8):
             store_a(t).wait()
+        for t in range(T // BACK):
             store_dz(t).wait()
         if remote:
             for d in range(1, 8):
@@ -525,17 +529,18 @@
         return pl.BlockSpec(shape, lambda i: (jnp.clip(i - start, 0, tiles - 1),) + (0,) * (len(shape) - 1))
 
     p_back = P_B + tiles + 10
+    back_rows = pl.BlockSpec((BACK, D), lambda i: (jnp.clip(i - p_back, 0, T // BACK - 1), 0))
     whole = pl.BlockSpec(ga.shape, lambda i: (0, 0))
     hbm = pl.BlockSpec(memory_space=pl.ANY)
 
     return pl.pallas_call(
         functools.partial(kernel_one, remote),
         name="forward_and_mlp",
-        grid=(p_back + tiles,),
-        in_specs=[pl.BlockSpec(memory_space=pltpu.SMEM), hbm, tile_from(p_back, TILE, D), whole, whole, hbm, hbm, hbm, hbm],
+        grid=(p_back + T // BACK,),
+        in_specs=[pl.BlockSpec(memory_space=pltpu.SMEM), hbm, back_rows, whole, whole, hbm, hbm, hbm, hbm],
         out_specs=[
             hbm, tile_from(P_B, TILE, 2 * D), hbm, hbm, hbm, hbm,
-            tile_from(p_back, TILE, D), tile_from(p_back, TILE, D), pl.BlockSpec((8, D), lambda i: (0, 0)), hbm, hbm, hbm,
+            back_rows, back_rows, pl.BlockSpec((8, D), lambda i: (0, 0)), hbm, hbm, hbm,
         ],
         out_shape=[
             sds(T, 3 * D), sds(T, 2 * D), sds(T, D),
@@ -566,9 +571,10 @@
 BLOCK = 512
 REUSE = {P_ATT + 5: [0], P_ATT + 8: [1], P_DX + 2: [2, 3, 4, 5]}
 START = [
-    [1, 2, 5, 7, 10, 13, 15], [1, 3, 7, 9, 12, 14, 19], [2, 4, 7, 9, 12, 15, 25], [3, 5, 8, 10, 13, 16, 20],
-    [6, 8, 10, 12, 14, 16, 26], [8, 9, 12, 14, 16, 18, 27], [8, 11, 13, 15, 17, 19, 29], [11, 12, 15, 17, 19, 21, 24],
-    [8, 10, 13, 16, 18, 20, 25], [12, 14, 16, 18, 20, 22, 28], [15, 16, 19, 20, 22, 23, 32], [17, 18, 20, 21, 22, 24, 28],
+    [1, 2, 5, 7, 9, 13, 15], [1, 3, 6, 11, 13, 15, 25], [2, 4, 6, 8, 10, 13, 16], [3, 6, 9, 10, 12, 14, 28],
+    [5, 8, 10, 12, 14, 16, 23], [8, 9, 11, 13, 15, 16, 23], [8, 10, 13, 15, 16, 18, 22], [8, 13, 15, 16, 18, 20, 30],
+    [11, 12, 15, 17, 19, 21, 25], [12, 13, 16, 18, 20, 22, 32], [12, 14, 16, 18, 20, 22, 24], [14, 15, 18, 19, 21, 23, 26],
+    [14, 16, 19, 20, 22, 23, 27], [17, 18, 20, 21, 23, 24, 29], [17, 19, 21, 22, 23, 24, 27],
 ]
 RECEIVE = {"s1": 0, "s2x": 1, "s2y": 1, "s3y": 2, "s3x": 2, "z1": 3, "z2": 4, "z3": 3}
 
@@ -578,13 +584,17 @@
 
 
 class Reduce:
-    def __init__(self, k, grads, bufs, send, recv, place):
-        self.n = k
+    def __init__(self, n, grads, bufs, send, recv, place):
+        self.n = n
+        k = n if n < 9 else 9 + (n - 9) // 2
+        cols = pl.ds(0, WIDE) if n < 9 else pl.ds((n - 9) % 2 * (WIDE // 2), WIDE // 2)
         first, x2, y2, y3, x3, outer, inner, out = bufs
         r = k % RING
-        self.g = grads.at[slot_of(k)]
-        self.first, self.x2, self.y2 = first.at[r], x2.at[r], y2.at[r]
-        self.x3, self.y3, self.outer, self.inner, self.out = x3.at[k], y3.at[k], outer.at[k], inner.at[k], out.at[k]
+        self.g = grads.at[slot_of(k), :, :, :, :, cols]
+        self.first = first.at[r, :, :, :, cols]
+        self.x2, self.y2 = x2.at[r, :, :, cols], y2.at[r, :, :, cols]
+        self.x3, self.y3 = x3.at[k, :, cols], y3.at[k, :, cols]
+        self.outer, self.inner, self.out = outer.at[k, :, cols], inner.at[k, :, cols], out.at[k, :, cols]
         self.send, self.recv = send, recv
         self.y, self.x, self.c, self.me, self.rep = place
         self.is_inner = (self.rep == 1) | (self.rep == 2)
@@ -865,33 +875,51 @@
     )(gwo.reshape(2, 2, 2, CHUNK, WIDE), wn, dy, u, wq, wt.reshape(4, 2, 2, 2, CHUNK, WIDE), gains, za, qkv, probs, do, x, dh, h)
 
 
-def kernel_finish(sums, wq, wi, ga, gm, y, dx, y_out, dx_out, gq, gwo, gwi, gwt, gg1, gg2, hold, sem):
+def kernel_finish(
+    sums_in, wq_in, wi_in, ga, gm, y, dx, y_out, dx_out, gq_out, gwo_out, gwi_out, gwt_out, gg1, gg2,
+    hold, sums, wq, wi, gq, gwo, gwi, gwt, sem, load_sem, store_sem,
+):
     parts = sem.shape[2]
     n = y.shape[0] // parts
+    loads = [pltpu.make_async_copy(src, dst, load_sem.at[k]) for k, (src, dst) in enumerate(((sums_in, sums), (wq_in, wq), (wi_in, wi)))]
     moves = []
     for p in range(parts):
         for k, (src, dst) in enumerate(((y, y_out), (dx, dx_out))):
             rows = pl.ds(p * n, n)
             there = pltpu.make_async_copy(src.at[rows], hold.at[k, rows], sem.at[0, k, p])
             moves.append((there, pltpu.make_async_copy(hold.at[k, rows], dst.at[rows], sem.at[1, k, p])))
-            there.start()
+    for load in loads:
+        load.start()
+    for there, _ in moves:
+        there.start()
+    stores = [pltpu.make_async_copy(src, dst, store_sem.at[k]) for k, (src, dst) in enumerate(((gwt, gwt_out), (gwi, gwi_out), (gq, gq_out), (gwo, gwo_out)))]
     D = gwo.shape[1]
-    gwo[...] = sums[0].astype(f32)
+    loads[0].wait()
+    for j in range(4):
+        gwt[j * CHUNK : (j + 1) * CHUNK, :] = sums[5 + j].astype(f32)
+    stores[0].start()
     for j in range(4):
         gwi[:, j * D : (j + 1) * D] = sums[1 + j].astype(f32)
-        gwt[j * CHUNK : (j + 1) * CHUNK, :] = sums[5 + j].astype(f32)
+    stores[1].start()
     for pair in range(D // 128):
         for j in range(3):
             cols = (pair % 2) * (WIDE // 2) + j * 128
             gq[:, j * D + pair * 128 : j * D + pair * 128 + 128] = sums[9 + pair // 2, :, cols : cols + 128].astype(f32)
+    stores[2].start()
+    gwo[...] = sums[0].astype(f32)
+    stores[3].start()
     for there, out in moves:
         there.wait()
         out.start()
+    loads[1].wait()
+    loads[2].wait()
     for grad, w, gain, out in ((gq, wq, ga, gg1), (gwi, wi, gm, gg2)):
         acc = jnp.zeros((CHUNK, 128), f32)
         for c in range(0, w.shape[1], 128):
             acc = acc + w[:, c : c + 128].astype(f32) * grad[:, c : c + 128]
         out[...] = jnp.sum(acc.T, axis=0, keepdims=True) / gain[...].astype(f32)
+    for store in stores:
+        store.wait()
     for _, out in moves:
         out.wait()
 
@@ -899,14 +927,19 @@
 def finish(sums, w_qkv, w_mlp_in, gain_attn, gain_mlp, y, dx):
     rows, D = w_qkv.shape[0], w_qkv.shape[1] // 3
     vmem, hbm = pl.BlockSpec(memory_space=pltpu.VMEM), pl.BlockSpec(memory_space=pl.ANY)
+    shapes = [(rows, 3 * D), (rows, D), (rows, 4 * D), (4 * rows, D)]
     fs = functools.partial(sds, dtype=f32)
     y, dx, gq, gwo, gwi, gwt, gg1, gg2 = pl.pallas_call(
         kernel_finish,
         name="finish",
-        in_specs=[vmem] * 5 + [hbm] * 2,
-        out_specs=[hbm] * 2 + [vmem] * 6,
-        out_shape=[sds(*y.shape), sds(*dx.shape), fs(rows, 3 * D), fs(rows, D), fs(rows, 4 * D), fs(4 * rows, D), fs(1, rows), fs(1, rows)],
-        scratch_shapes=[pltpu.VMEM((2, *y.shape), bf), pltpu.SemaphoreType.DMA((2, 2, 4))],
+        in_specs=[hbm] * 3 + [vmem] * 2 + [hbm] * 2,
+        out_specs=[hbm] * 6 + [vmem] * 2,
+        out_shape=[sds(*y.shape), sds(*dx.shape), *(fs(*shape) for shape in shapes), fs(1, rows), fs(1, rows)],
+        scratch_shapes=[
+            pltpu.VMEM((2, *y.shape), bf), pltpu.VMEM(sums.shape, bf), pltpu.VMEM(w_qkv.shape, bf), pltpu.VMEM(w_mlp_in.shape, bf),
+            *(pltpu.VMEM(shape, f32) for shape in shapes),
+            pltpu.SemaphoreType.DMA((2, 2, 4)), pltpu.SemaphoreType.DMA((3,)), pltpu.SemaphoreType.DMA((4,)),
+        ],
         cost_estimate=pl.CostEstimate(flops=1 << 20, bytes_accessed=20 << 20, transcendentals=0),
         compiler_params=pltpu.CompilerParams(vmem_limit_bytes=VMEM),
     )(sums, w_qkv, w_mlp_in, gain_attn.reshape(1, rows), gain_mlp.reshape(1, rows), y, dx)

time: 204 us -> 198 us (0.971)
  Pallas kernels: 203 us -> 197 us
    pallas_call x1, Pallas kernels: 106 us -> 101 us  [forward_and_mlp(): pl.pallas_call(functools.partial(kernel_one, remote), name='forward_and_m...]
where the time goes in v6:
time: 198 us
  Pallas kernels  197 us (99%)
    pallas_call x1, Pallas kernels, forward_and_mlp(): pl.pallas_call(functools.partial(kernel_one, remote), name='forward_and_m...  101 us
    pallas_call x1, Pallas kernels, gradients(): pl.pallas_call(kernel_two, name='gradients', grid=(STEPS,), in_specs=[hbm...  88 us
    pallas_call x1, Pallas kernels, finish(): pl.pallas_call(kernel_finish, name='finish', in_specs=[hbm] * 3 + [vmem]...  7.86 us

profile of v6, /device:TPU:0, one launch (start us, length us, event | category | flops | bytes accessed | tf_op | source)
XLA Modules:
  0.0 198.0 jit_solution(11858210376393830946)
XLA Ops:
  0.6 101.3 %forward_and_mlp.1 = (bf16[2048,2304]{1,0:T(8,128)(2,1)}, bf16[2048,1536]{1,0:T(8,128)(2,1)}, bf16[2048,768]{1,0:T(8,128)(2,1)}, bf16[2,2048,768]{2,1,0:T(8,128)...) custom-call(s32[4,16]{1,0:T(4,128)} %bitcast.11, ...), custom_call_target="tpu_custom_call" | custom-call | flops 60397977600 | bytes 94371840 | tf_op jit(solution)/shard_map/forward_and_mlp/pallas_call | solution.py:536
  101.9 88.0 %gradients.1 = (bf16[2048,768]{1,0:T(8,128)(2,1)}, bf16[2048,768]{1,0:T(8,128)(2,1)}, bf16[12,96,768]{2,1,0:T(8,128)(2,1)}) custom-call(bf16[2,2,2,96,768]{4,3,2,1,0:T(8,128)(2,1)} %bitcast.15, bf16[2048,768]{1,0:T(8,128)(2,1)} %get-tuple-element.32.wn, bf16[2048,768]{1,0:T(8,128)(2,1)} %dm.1, bf16[2048,768]{1,0:T(8,128)(2,1)} %get-tuple-element.33.u, ...), custom_call_target="tpu_custom_call" | custom-call | flops 53150220288 | bytes 94371840 | tf_op jit(solution)/shard_map/gradients/pallas_call | solution.py:858
  190.0 7.9 %finish.1 = (bf16[2048,768]{1,0:T(8,128)(2,1)}, bf16[2048,768]{1,0:T(8,128)(2,1)}, f32[96,2304]{1,0:T(8,128)}, f32[96,768]{1,0:T(8,128)}, f32[96,3072]{1,0:T(8,1...) custom-call(bf16[12,96,768]{2,1,0:T(8,128)(2,1)} %get-tuple-element.43.sums_in, ...), custom_call_target="tpu_custom_call" | custom-call | flops 1048576 | bytes 20971520 | tf_op jit(solution)/shard_map/finish/pallas_call | solution.py:932

commit v7 on v6

--- a/solution.py
+++ b/solution.py
@@ -317,7 +317,7 @@
 def kernel_one(
     remote, lengths, x, dy, ga, gm, q_in, o_in, i_in, t_in,
     qkv_out, probs_out, u_out, h_out, wn_out, za_out, dh_out, do_out, gains_out, gwo_out, wq_out, wt_out,
-    wq, wo, wi, wt, gain_piece, gain_parts, gains, high, low, qa, zs, mixed_all, wn, send, recv, gain_send, gain_recv, local, out_sem, a_sem, dz_sem,
+    wq, wo, wi, wt, gain_piece, gain_parts, gains, high, low, qa, zs, mixed_all, wn, send, recv, gain_send, gain_recv, local, out_sem, a_sem, dz_sem, back_sem,
 ):
     step = pl.program_id(0)
     T, D = high.shape
@@ -367,6 +367,10 @@
 
     def store_dz(t):
         return pltpu.make_async_copy(zs.at[rows_at(t, BACK)], za_out.at[0, rows_at(t, BACK)], dz_sem.at[t])
+
+    def store_back(t):
+        rows = rows_at(t, BACK)
+        return [pltpu.make_async_copy(v.at[rows], to.at[rows], back_sem.at[k, t]) for k, (v, to) in enumerate(((high, dh_out), (low, do_out)))]
 
     def relay(code):
         blocks[code // 10].relay(ARRIVALS[code % 10])
@@ -495,9 +499,10 @@
             dw = add if dw is None else dw + add
         store_dz(t).start()
         dt = (dm.astype(f32) + norm_back(dw, n, r, gains[1:2])).astype(bf)
-        dh_out[...] = dt
         high[rows, :] = dt
-        do_out[...] = nt(dt, flat(wo[...])).astype(bf)
+        low[rows, :] = nt(dt, flat(wo[...])).astype(bf)
+        for store in store_back(t):
+            store.start()
 
     @pl.when(step == steps - 1)
     def _():
@@ -511,6 +516,8 @@
             store_a(t).wait()
         for t in range(T // BACK):
             store_dz(t).wait()
+            for store in store_back(t):
+                store.wait()
         if remote:
             for d in range(1, 8):
                 gain_copy(d).wait_send()
@@ -540,7 +547,7 @@
         in_specs=[pl.BlockSpec(memory_space=pltpu.SMEM), hbm, back_rows, whole, whole, hbm, hbm, hbm, hbm],
         out_specs=[
             hbm, tile_from(P_B, TILE, 2 * D), hbm, hbm, hbm, hbm,
-            back_rows, back_rows, pl.BlockSpec((8, D), lambda i: (0, 0)), hbm, hbm, hbm,
+            hbm, hbm, pl.BlockSpec((8, D), lambda i: (0, 0)), hbm, hbm, hbm,
         ],
         out_shape=[
             sds(T, 3 * D), sds(T, 2 * D), sds(T, D),
@@ -551,7 +558,7 @@
             pltpu.VMEM((8, F // 8, D), bf), pltpu.VMEM((16, 128), bf), pltpu.VMEM((8, 16, 128), bf), pltpu.VMEM((8, D), f32), pltpu.VMEM((T, D), bf),
             pltpu.VMEM((T, D), bf), pltpu.VMEM((T, F), bf), pltpu.VMEM((T, F), bf), pltpu.VMEM((T, D), bf), pltpu.VMEM((T, D), bf),
             pltpu.SemaphoreType.DMA((12,)), pltpu.SemaphoreType.DMA((12, len(ARRIVALS))), pltpu.SemaphoreType.DMA((8,)), pltpu.SemaphoreType.DMA((8,)),
-            pltpu.SemaphoreType.DMA((14,)), pltpu.SemaphoreType.DMA((10,)), pltpu.SemaphoreType.DMA((tiles,)), pltpu.SemaphoreType.DMA((tiles,)),
+            pltpu.SemaphoreType.DMA((14,)), pltpu.SemaphoreType.DMA((10,)), pltpu.SemaphoreType.DMA((tiles,)), pltpu.SemaphoreType.DMA((T // BACK,)), pltpu.SemaphoreType.DMA((2, T // BACK)),
         ],
         cost_estimate=pl.CostEstimate(flops=12 * T * D * D + 8 * T * D * F + 6 * T * D * D, bytes_accessed=90 << 20, transcendentals=0),
         compiler_params=pltpu.CompilerParams(

time: 198 us -> 198 us (level)
  no operation moved by 1% of the time
where the time goes in v7:
time: 198 us
  Pallas kernels  197 us (99%)
    pallas_call x1, Pallas kernels, forward_and_mlp(): pl.pallas_call(functools.partial(kernel_one, remote), name='forward_and_m...  101 us
    pallas_call x1, Pallas kernels, gradients(): pl.pallas_call(kernel_two, name='gradients', grid=(STEPS,), in_specs=[hbm...  88.1 us
    pallas_call x1, Pallas kernels, finish(): pl.pallas_call(kernel_finish, name='finish', in_specs=[hbm] * 3 + [vmem]...  7.86 us

profile of v7, /device:TPU:0, one launch (start us, length us, event | category | flops | bytes accessed | tf_op | source)
XLA Modules:
  0.0 197.6 jit_solution(12460567483123704299)
XLA Ops:
  0.6 100.8 %forward_and_mlp.1 = (bf16[2048,2304]{1,0:T(8,128)(2,1)}, bf16[2048,1536]{1,0:T(8,128)(2,1)}, bf16[2048,768]{1,0:T(8,128)(2,1)}, bf16[2,2048,768]{2,1,0:T(8,128)...) custom-call(s32[4,16]{1,0:T(4,128)} %bitcast.11, ...), custom_call_target="tpu_custom_call" | custom-call | flops 60397977600 | bytes 94371840 | tf_op jit(solution)/shard_map/forward_and_mlp/pallas_call | solution.py:543
  101.5 88.1 %gradients.1 = (bf16[2048,768]{1,0:T(8,128)(2,1)}, bf16[2048,768]{1,0:T(8,128)(2,1)}, bf16[12,96,768]{2,1,0:T(8,128)(2,1)}) custom-call(bf16[2,2,2,96,768]{4,3,2,1,0:T(8,128)(2,1)} %bitcast.15, bf16[2048,768]{1,0:T(8,128)(2,1)} %get-tuple-element.32.wn, bf16[2048,768]{1,0:T(8,128)(2,1)} %dm.1, bf16[2048,768]{1,0:T(8,128)(2,1)} %get-tuple-element.33.u, ...), custom_call_target="tpu_custom_call" | custom-call | flops 53150220288 | bytes 94371840 | tf_op jit(solution)/shard_map/gradients/pallas_call | solution.py:865
  189.5 7.9 %finish.1 = (bf16[2048,768]{1,0:T(8,128)(2,1)}, bf16[2048,768]{1,0:T(8,128)(2,1)}, f32[96,2304]{1,0:T(8,128)}, f32[96,768]{1,0:T(8,128)}, f32[96,3072]{1,0:T(8,1...) custom-call(bf16[12,96,768]{2,1,0:T(8,128)(2,1)} %get-tuple-element.43.sums_in, ...), custom_call_target="tpu_custom_call" | custom-call | flops 1048576 | bytes 20971520 | tf_op jit(solution)/shard_map/finish/pallas_call | solution.py:939
